TPU v7x, 32 devices: a whole 2x2x4 slice. The times are simulated.
32 devices in a mesh: grp: 4 (over x, core), wide: 8 (over z, y).
Axes of the slice: x: 2, y: 2, z: 4, core: 2. Of those that a mesh axis runs over, the one named last changes fastest.
Arguments:
- velocity: float32 [3, 64, 128, 512], P(None, 'grp', 'wide'), may hold values from -6 to 6
- level_set: float32 [64, 128, 512], P('grp', 'wide'), may hold values from -8 to 8
Outputs:
- force: float32 [3, 64, 128, 512], P(None, 'grp', 'wide')
All inputs are finite; a program needn't handle non-finite values.
Results may differ from a plain program's by a relative error of at most 0.000054.
Values sent between devices are 32-bit elements; how exact they have to be, the bound alone decides.
No kernel may reach another device: no remote copies, remote signals or barrier semaphores. Data moves between devices by JAX's collectives and lax.ppermute only.
A program may use at most 64 MiB of HBM per device.

v0:
```python
import jax
import jax.numpy as jnp
import numpy as np
from jax import lax
from jax.sharding import PartitionSpec as P

interface_width = 1.0


def derivative_table(count):
    offsets = np.arange(count)
    offset_mod = (offsets[:, None] - offsets[None, :]) % count
    angle_arg = np.pi * offset_mod / count
    safe_angle = np.where(offset_mod == 0, 0.5, angle_arg)
    parity = np.where(offset_mod % 2 == 0, 1.0, -1.0)
    entries = np.pi / count * parity * np.cos(safe_angle) / np.sin(safe_angle)
    return np.where(offset_mod == 0, 0.0, entries).astype(np.float32)


def along_last(source, table_t):
    return jnp.dot(source, table_t, precision=lax.Precision.HIGHEST)


def properties(level_set):
    heavy = 0.5 * (1.0 + jnp.tanh(level_set / interface_width))
    return (0.2 + 0.8 * heavy, 0.25 + 0.75 * heavy)


def shards(velocity, level_set):
    cells_x = velocity.shape[3]
    slab_z = velocity.shape[1]
    slab_y = velocity.shape[2]
    wide_count = lax.axis_size("wide")
    group_count = lax.axis_size("grp")
    cells_y = slab_y * wide_count
    cells_z = slab_z * group_count
    dx_t = jnp.asarray(derivative_table(cells_x).T)
    dy_full = jnp.asarray(derivative_table(cells_y))
    dz_full = jnp.asarray(derivative_table(cells_z))
    viscosity, density = properties(level_set)
    z_columns = slab_y * cells_x // group_count
    y_columns = slab_z * cells_x // wide_count
    visc_panels = viscosity.reshape(slab_z, group_count, z_columns)
    result = jnp.einsum(
        "ij,jgk->igk",
        dz_full,
        lax.all_to_all(visc_panels, "grp", split_axis=1, concat_axis=0, tiled=True),
        precision=lax.Precision.HIGHEST,
    )
    dz_visc = lax.all_to_all(result, "grp", split_axis=0, concat_axis=1, tiled=True).reshape(
        slab_z, slab_y, cells_x
    )

    def to_lines(field):
        count = field.shape[0]
        return jnp.transpose(field, (0, 2, 1, 3)).reshape(count, slab_y, wide_count, y_columns)

    def from_lines(field):
        count = field.shape[0]
        return jnp.transpose(field.reshape(count, slab_y, slab_z, cells_x), (0, 2, 1, 3))

    def yline(block):
        return jnp.einsum("ij,cjgk->cigk", dy_full, block, precision=lax.Precision.HIGHEST)

    grad_x = along_last(velocity, dx_t)
    grad_y = from_lines(
        lax.all_to_all(
            yline(
                lax.all_to_all(to_lines(velocity), "wide", split_axis=2, concat_axis=1, tiled=True)
            ),
            "wide",
            split_axis=1,
            concat_axis=2,
            tiled=True,
        )
    )
    s_xy = viscosity * (grad_y[0] + grad_x[1])
    s_yy = 2.0 * viscosity * grad_y[1]
    s_yz = viscosity * grad_y[2]
    stresses = to_lines(jnp.stack([s_xy, s_yy, s_yz]))
    dy_stress = from_lines(
        lax.all_to_all(
            yline(lax.all_to_all(stresses, "wide", split_axis=2, concat_axis=1, tiled=True)),
            "wide",
            split_axis=1,
            concat_axis=2,
            tiled=True,
        )
    )
    grad_yw = grad_y[2]
    s_xx = 2.0 * viscosity * grad_x[0]
    s_xz = viscosity * grad_x[2]
    dx_stress = along_last(jnp.stack([s_xx, s_xy, s_xz]), dx_t)
    first = (dx_stress[0] + dy_stress[0] + dz_visc * grad_x[2]) / density
    second = (dx_stress[1] + dy_stress[1] + dz_visc * grad_yw) / density
    third = (dx_stress[2] + dy_stress[2]) / density
    return jnp.stack([first, second, third])


def solution(mesh):
    return jax.shard_map(
        shards,
        mesh=mesh,
        in_specs=(P(None, "grp", "wide", None), P("grp", "wide", None)),
        out_specs=P(None, "grp", "wide", None),
        check_vma=False,
    )
```

profile of v0, /device:TPU:0, one launch (start us, length us, event | category | flops | bytes accessed | tf_op | source)
XLA Modules:
  0.0 216.3 jit_solution(13507969912813457006)
XLA Ops:
  0.0 2.3 %copy.69 = f32[3,16,16,512]{3,2,1,0:T(8,128)S(1)} copy(f32[3,16,16,512]{3,1,2,0:T(8,128)} %bitcast.142) | data formatting | bytes 3145728 | tf_op jit(solution)/shard_map/transpose | solution.py:56
  2.3 0.5 reshape.40
  2.8 0.9 copy.70
  3.8 0.0 copy-start.8
  3.8 44.2 %all_to_all.90 = f32[3,16,8,1024]{3,1,0,2:T(8,128)S(1)} all-to-all(f32[3,16,8,1024]{3,1,0,2:T(8,128)S(1)} %copy.70), channel_id=1, replica_groups=mesh['grp'=4,'wide'=8] {'wide'}, dimensions={2} | all-to-all | bytes 3145728 | tf_op jit(solution)/shard_map/all_to_all | solution.py:69
  48.0 2.3 %fusion.12 = f32[3,128,1,1024]{3,1,0,2:T(8,128)S(1)} fusion(f32[128,128,1]{1,0,2:T(8,128)S(1)} %copy-done.8, f32[3,16,8,1024]{3,1,0,2:T(8,128)S(1)} %all_to_all.90), kind=kOutput, calls=%fused_computation.17 | convolution fusion | flops 603979776 | bytes 3211264 | tf_op jit(solution)/shard_map/ij,cjgk->cigk/dot_general | solution.py:63
  50.3 2.8 %copy.72 = f32[3,128,1,1024]{3,2,0,1:T(1,128)} copy(f32[3,128,1,1024]{3,1,0,2:T(8,128)S(1)} %fusion.12) | data formatting | bytes 3145728 | tf_op jit(solution)/shard_map/ij,cjgk->cigk/transpose | solution.py:63
  53.0 3.9 %all-to-all-start.1 = ((f32[3,128,1,1024]{3,2,0,1:T(1,128)}), f32[3,128,1,1024]{3,2,0,1:T(1,128)S(1)}, u32[]{:S(2)}, u32[]{:S(2)}) async-start(f32[3,128,1,1024]{3,2,0,1:T(1,128)} %copy.72), calls=%async_computation.1 | async-start | bytes 3145728 | tf_op jit(solution)/shard_map/all_to_all | solution.py:67
  57.0 5.0 %convolution_bitcast_fusion.1 = f32[3,16,16,512]{3,2,1,0:T(8,128)} fusion(f32[512,512,1,1]{1,0,3,2:T(8,128)} %constant.30, f32[3,16,16,512]{3,2,1,0:T(8,128)S(1)} %copy-done.7), kind=kOutput, calls=%fused_computation.19 | convolution fusion | flops 2415919104 | bytes 4194304 | tf_op jit(solution)/shard_map/dot_general | solution.py:21
  62.0 31.5 %all-to-all-done.1 = f32[3,128,1,1024]{3,2,0,1:T(1,128)S(1)} async-done(((f32[3,128,1,1024]{3,2,0,1:T(1,128)}), f32[3,128,1,1024]{3,2,0,1:T(1,128)S(1)}, u32[]{:S(2)}, u32[]{:S(2)}) %all-to-all-start.1) | async-done | bytes 1572896 | tf_op jit(solution)/shard_map/all_to_all | solution.py:67
  93.5 0.3 copy.73
  93.8 0.9 copy.74
  94.7 0.2 reshape.42
  95.0 0.0 copy-start.2
  95.0 0.0 copy-start.5
  95.0 0.9 copy.106
  95.9 0.5 copy-done.2
  96.4 0.1 copy-done.5
  96.5 1.7 fusion.35
  98.2 0.3 reshape.46
  98.5 1.1 copy.84
  99.6 4.1 %all-to-all-start.4 = ((f32[16,4,2048]{2,0,1:T(8,128)}), f32[16,4,2048]{2,0,1:T(8,128)}, u32[]{:S(2)}, u32[]{:S(2)}) async-start(f32[16,4,2048]{2,0,1:T(8,128)} %copy.84), calls=%async_computation.4 | async-start | bytes 1048576 | tf_op jit(solution)/shard_map/all_to_all | solution.py:47
  103.8 1.2 maximum_bitcast_fusion
  105.0 0.9 copy.76
  105.9 1.6 reshape.43
  107.6 3.5 %copy.77 = f32[3,16,8,1024]{3,1,0,2:T(8,128)} copy(f32[3,16,8,1024]{3,2,1,0:T(8,128)} %reshape.43) | data formatting | bytes 3145728 | tf_op jit(solution)/shard_map/reshape | solution.py:56
  111.1 1.6 all-to-all-done.4
  112.7 3.6 %all-to-all-start.2 = ((f32[3,16,8,1024]{3,1,0,2:T(8,128)}), f32[3,16,8,1024]{3,1,0,2:T(8,128)S(1)}, u32[]{:S(2)}, u32[]{:S(2)}) async-start(f32[3,16,8,1024]{3,1,0,2:T(8,128)} %copy.77), calls=%async_computation.2 | async-start | bytes 3145728 | tf_op jit(solution)/shard_map/all_to_all | solution.py:83
  116.3 0.0 copy-start.9
  116.3 2.2 %copy.85 = f32[16,4,2048]{2,1,0:T(4,128)} copy(f32[16,4,2048]{2,0,1:T(8,128)} %all-to-all-done.4) | data formatting | bytes 1048576 | tf_op jit(solution)/shard_map/all_to_all | solution.py:47
  118.5 2.0 reshape.55
  120.5 1.6 convolution_bitcast_fusion
  122.1 1.4 copy.86
  123.5 29.8 %all-to-all-done.2 = f32[3,16,8,1024]{3,1,0,2:T(8,128)S(1)} async-done(((f32[3,16,8,1024]{3,1,0,2:T(8,128)}), f32[3,16,8,1024]{3,1,0,2:T(8,128)S(1)}, u32[]{:S(2)}, u32[]{:S(2)}) %all-to-all-start.2) | async-done | bytes 1572896 | tf_op jit(solution)/shard_map/all_to_all | solution.py:83
  153.3 4.4 %all-to-all-start.5 = ((f32[64,1,2048]{2,1,0:T(1,128)}), f32[64,1,2048]{2,1,0:T(1,128)}, u32[]{:S(2)}, u32[]{:S(2)}) async-start(f32[64,1,2048]{2,1,0:T(1,128)} %copy.86), calls=%async_computation.5 | async-start | bytes 1048576 | tf_op jit(solution)/shard_map/all_to_all | solution.py:50
  157.6 4.4 %fusion.15 = f32[3,128,1,1024]{1,3,0,2:T(8,128)} fusion(f32[128,128,1]{1,0,2:T(8,128)S(1)} %copy-done.8, f32[3,16,8,1024]{3,1,0,2:T(8,128)S(1)} %all-to-all-done.2), kind=kOutput, calls=%fused_computation.18 | convolution fusion | flops 603979776 | bytes 3211264 | tf_op jit(solution)/shard_map/ij,cjgk->cigk/dot_general | solution.py:63
  162.0 4.9 %copy.80 = f32[3,128,1,1024]{3,2,0,1:T(1,128)} copy(f32[3,128,1,1024]{1,3,0,2:T(8,128)} %fusion.15) | data formatting | bytes 3145728 | tf_op jit(solution)/shard_map/ij,cjgk->cigk/transpose | solution.py:63
  166.9 3.6 %all-to-all-start.3 = ((f32[3,128,1,1024]{3,2,0,1:T(1,128)}), f32[3,128,1,1024]{3,2,0,1:T(1,128)S(1)}, u32[]{:S(2)}, u32[]{:S(2)}) async-start(f32[3,128,1,1024]{3,2,0,1:T(1,128)} %copy.80), calls=%async_computation.3 | async-start | bytes 3145728 | tf_op jit(solution)/shard_map/all_to_all | solution.py:82
  170.5 5.5 %fusion = f32[3,16,16,512]{3,2,1,0:T(8,128)} fusion(f32[512,512,1,1]{1,0,3,2:T(8,128)} %constant.30, f32[1,16,16,512]{3,2,1,0:T(8,128)} %get-tuple-element.9, f32[1,16,16,512]{3,2,1,0:T(8,128)} %copy-done.1, f32[1,16,16,512]{3,2,1,0:T(8,128)} %get-tuple-element.8), kind=kOutput, calls=%fused_computation.1 | convolution fusion | flops 2416705536 | bytes 4194304 | tf_op jit(solution)/shard_map/dot_general | solution.py:21
  176.0 2.2 %copy.107 = f32[4,16,1,2048]{3,0,1,2:T(4,128)} copy(f32[4,16,1,2048]{3,2,1,0:T(1,128)} %bitcast.31) | data formatting | bytes 1048576 | tf_op jit(solution)/shard_map/all_to_all | solution.py:50
  178.2 2.1 reshape.48
  180.3 27.8 %all-to-all-done.3 = f32[3,128,1,1024]{3,2,0,1:T(1,128)S(1)} async-done(((f32[3,128,1,1024]{3,2,0,1:T(1,128)}), f32[3,128,1,1024]{3,2,0,1:T(1,128)S(1)}, u32[]{:S(2)}, u32[]{:S(2)}) %all-to-all-start.3) | async-done | bytes 1572896 | tf_op jit(solution)/shard_map/all_to_all | solution.py:82
  208.1 0.3 copy.81
  208.4 0.9 copy.82
  209.4 1.4 reshape.45
  210.8 2.5 %copy.105 = f32[3,16,16,512]{3,1,2,0:T(8,128)S(1)} copy(f32[3,16,16,512]{3,2,1,0:T(8,128)} %reshape.45) | data formatting | bytes 3145728 | tf_op jit(solution)/shard_map/reshape | solution.py:60
  213.3 1.7 fusion.28
  215.0 1.3 pad_maximum_fusion
  (15 shorter events, 0.0 us)
Async XLA Ops:
  3.8 44.2 %copy-start.8 = (f32[128,128,1]{1,0,2:T(8,128)S(1)}, f32[128,128,1]{1,0,2:T(8,128)}, u32[]{:S(2)}) copy-start(f32[128,128,1]{1,0,2:T(8,128)} %constant.31) | copy-start | bytes 196612
  53.0 3.9 %copy-start.7 = (f32[3,16,16,512]{3,2,1,0:T(8,128)S(1)}, f32[3,16,16,512]{3,2,1,0:T(8,128)}, u32[]{:S(2)}) copy-start(f32[3,16,16,512]{3,2,1,0:T(8,128)} %param.5) | copy-start | bytes 4718596
  53.0 40.4 %all-to-all-start.1 = ((f32[3,128,1,1024]{3,2,0,1:T(1,128)}), f32[3,128,1,1024]{3,2,0,1:T(1,128)S(1)}, u32[]{:S(2)}, u32[]{:S(2)}) async-start(f32[3,128,1,1024]{3,2,0,1:T(1,128)} %copy.72), calls=%async_computation.1 | async-start | bytes 3145728 | tf_op jit(solution)/shard_map/all_to_all | solution.py:67
  95.0 1.4 copy-start.2
  95.0 1.5 copy-start.5
  98.2 5.6 %copy-start.1 = (f32[1,16,16,512]{3,2,1,0:T(8,128)}, f32[1,16,16,512]{3,2,1,0:T(8,128)S(1)}, u32[]{:S(2)}) copy-start(f32[1,16,16,512]{3,2,1,0:T(8,128)S(1)} %get-tuple-element.10) | copy-start | bytes 1572868
  98.5 5.3 %copy-start.4 = (f32[1,16,16,512]{3,2,1,0:T(8,128)S(1)}, f32[1,16,16,512]{3,2,1,0:T(8,128)}, u32[]{:S(2)}) copy-start(f32[1,16,16,512]{3,2,1,0:T(8,128)} %get-tuple-element.11) | copy-start | bytes 1572868
  99.6 13.0 %all-to-all-start.4 = ((f32[16,4,2048]{2,0,1:T(8,128)}), f32[16,4,2048]{2,0,1:T(8,128)}, u32[]{:S(2)}, u32[]{:S(2)}) async-start(f32[16,4,2048]{2,0,1:T(8,128)} %copy.84), calls=%async_computation.4 | async-start | bytes 1048576 | tf_op jit(solution)/shard_map/all_to_all | solution.py:47
  112.7 40.6 %all-to-all-start.2 = ((f32[3,16,8,1024]{3,1,0,2:T(8,128)}), f32[3,16,8,1024]{3,1,0,2:T(8,128)S(1)}, u32[]{:S(2)}, u32[]{:S(2)}) async-start(f32[3,16,8,1024]{3,1,0,2:T(8,128)} %copy.77), calls=%async_computation.2 | async-start | bytes 3145728 | tf_op jit(solution)/shard_map/all_to_all | solution.py:83
  116.3 4.2 %copy-start.9 = (f32[64,64]{1,0:T(8,128)S(1)}, f32[64,64]{1,0:T(8,128)}, u32[]{:S(2)}) copy-start(f32[64,64]{1,0:T(8,128)} %constant.29) | copy-start | bytes 49156
  153.3 13.6 %all-to-all-start.5 = ((f32[64,1,2048]{2,1,0:T(1,128)}), f32[64,1,2048]{2,1,0:T(1,128)}, u32[]{:S(2)}, u32[]{:S(2)}) async-start(f32[64,1,2048]{2,1,0:T(1,128)} %copy.86), calls=%async_computation.5 | async-start | bytes 1048576 | tf_op jit(solution)/shard_map/all_to_all | solution.py:50
  166.9 41.2 %all-to-all-start.3 = ((f32[3,128,1,1024]{3,2,0,1:T(1,128)}), f32[3,128,1,1024]{3,2,0,1:T(1,128)S(1)}, u32[]{:S(2)}, u32[]{:S(2)}) async-start(f32[3,128,1,1024]{3,2,0,1:T(1,128)} %copy.80), calls=%async_computation.3 | async-start | bytes 3145728 | tf_op jit(solution)/shard_map/all_to_all | solution.py:82
  210.8 2.5 %copy-start = (f32[3,16,16,512]{3,2,1,0:T(8,128)S(1)}, f32[3,16,16,512]{3,2,1,0:T(8,128)}, u32[]{:S(2)}) copy-start(f32[3,16,16,512]{3,2,1,0:T(8,128)} %fusion) | copy-start | bytes 4718596
  210.8 2.5 %copy-start.3 = (f32[16,16,512]{2,1,0:T(8,128)S(1)}, f32[16,16,512]{2,1,0:T(8,128)}, u32[]{:S(2)}) copy-start(f32[16,16,512]{2,1,0:T(8,128)} %reshape.48) | copy-start | bytes 1572868
  210.8 2.5 %copy-start.6 = (f32[16,16,512]{2,1,0:T(8,128)S(1)}, f32[16,16,512]{2,1,0:T(8,128)}, u32[]{:S(2)}) copy-start(f32[16,16,512]{2,1,0:T(8,128)} %param.6) | copy-start | bytes 1572868
where the time goes:
time: 217 us; the launch traced here: 216 us
  waiting for transfers between devices  90.7 us (42%)
  blocking collectives  44.2 us (20%)
  local copies, waits for them, and re-layouts  36.9 us (17%)
  starting transfers between devices  19.6 us (9%)
  matrix products  18.7 us (9%)
  other arithmetic  5.94 us (3%)
    all_to_all x1, blocking collectives, shards(): lax.all_to_all(to_lines(velocity), 'wide', split_axis=2, concat_axis=1, t...  44.2 us
    all_to_all x1, waiting for transfers between devices, shards(): lax.all_to_all(yline(lax.all_to_all(to_lines(velocity), 'wide', split_axi...  31.5 us
    all_to_all x1, waiting for transfers between devices, shards(): lax.all_to_all(stresses, 'wide', split_axis=2, concat_axis=1, tiled=True)  29.8 us
    all_to_all x1, waiting for transfers between devices, shards(): lax.all_to_all(yline(lax.all_to_all(stresses, 'wide', split_axis=2, conca...  27.8 us
    dot_general x2, matrix products, along_last(): return jnp.dot(source, table_t, precision=lax.Precision.HIGHEST)  10.5 us
    transpose x2, local copies, waits for them, and re-layouts, yline(): jnp.einsum('ij,cjgk->cigk', dy_full, block, precision=lax.Precision.HIGHEST)  7.7 us
    dot_general x2, matrix products, yline(): jnp.einsum('ij,cjgk->cigk', dy_full, block, precision=lax.Precision.HIGHEST)  6.6 us
    reshape x4, local copies, waits for them, and re-layouts, to_lines(): jnp.transpose(field, (0, 2, 1, 3))  6.55 us
  transfers between devices with their start and end apart: 5, of which 4 were waited for; matrix products, arithmetic and copies ran while one was open for 18% of the time, Pallas kernels for 0%

commit v1 on v0

--- a/solution.py
+++ b/solution.py
@@ -1,10 +1,15 @@
+import functools
+
 import jax
 import jax.numpy as jnp
 import numpy as np
 from jax import lax
+from jax.experimental import pallas as pl
+from jax.experimental.pallas import tpu as pltpu
 from jax.sharding import PartitionSpec as P
 
 interface_width = 1.0
+vmem_bytes = 40 * 1024 * 1024
 
 
 def derivative_table(count):
@@ -17,6 +22,12 @@
     return np.where(offset_mod == 0, 0.0, entries).astype(np.float32)
 
 
+def halves(table):
+    high = table.astype(jnp.bfloat16)
+    low = (table - high.astype(np.float32)).astype(jnp.bfloat16)
+    return high, low
+
+
 def along_last(source, table_t):
     return jnp.dot(source, table_t, precision=lax.Precision.HIGHEST)
 
@@ -26,7 +37,183 @@
     return (0.2 + 0.8 * heavy, 0.25 + 0.75 * heavy)
 
 
-def shards(velocity, level_set):
+def pack_kernel(count, planes, chunk, velocity, level_set, *refs):
+    outs, sems = refs[:count], refs[count]
+    me = lax.axis_index("wide")
+    copies = []
+    for step in range(count):
+        plane = (me ^ step) * planes + chunk
+        copies.append(
+            pltpu.make_async_copy(velocity.at[:, plane], outs[step].at[0:3], sems.at[step, 0])
+        )
+        copies.append(
+            pltpu.make_async_copy(level_set.at[plane], outs[step].at[3], sems.at[step, 1])
+        )
+    for copy in copies:
+        copy.start()
+    for copy in copies:
+        copy.wait()
+
+
+def pack(velocity, level_set, count, planes, chunk):
+    rows, cells = level_set.shape[1:]
+    piece = jax.ShapeDtypeStruct((4, rows, cells), jnp.float32)
+    return pl.pallas_call(
+        functools.partial(pack_kernel, count, planes, chunk),
+        out_shape=(piece,) * count,
+        in_specs=[pl.BlockSpec(memory_space=pl.ANY)] * 2,
+        out_specs=(pl.BlockSpec(memory_space=pl.ANY),) * count,
+        scratch_shapes=[pltpu.SemaphoreType.DMA((count, 2))],
+        cost_estimate=pl.CostEstimate(
+            flops=0, transcendentals=0, bytes_accessed=2 * count * 16 * rows * cells
+        ),
+        name="pack",
+    )(velocity, level_set)
+
+
+def split(value):
+    high = value.astype(jnp.bfloat16)
+    low = (value - high.astype(jnp.float32)).astype(jnp.bfloat16)
+    return high, low
+
+
+def times_x(fields, table):
+    high, low = split(fields)
+    return jnp.dot(
+        jnp.concatenate([high, low, high], axis=1), table, preferred_element_type=jnp.float32
+    )
+
+
+def times_y(table, fields):
+    high, low = split(fields)
+    return jnp.dot(
+        table, jnp.concatenate([high, high, low], axis=0), preferred_element_type=jnp.float32
+    )
+
+
+def plane_kernel(count, dx, dy, *refs):
+    pieces, outs = refs[:count], refs[count : 2 * count]
+    held, result = refs[2 * count :]
+    me = lax.axis_index("wide")
+    rows, cells = pieces[0].shape[1:]
+    lines = rows * count
+    for step in range(count):
+        held[:, pl.ds(pl.multiple_of((me ^ step) * rows, 8), rows), :] = pieces[step][...]
+    heavy = 0.5 * (1.0 + jnp.tanh(held[3] / interface_width))
+    viscosity = 0.2 + 0.8 * heavy
+    grad_x = times_x(held[0:3].reshape(3 * lines, cells), dx[...]).reshape(3, lines, cells)
+    grad_y = times_y(dy[...], jnp.concatenate([held[0], held[1], held[2]], axis=1))
+    grad_yu, grad_yv, grad_yw = (grad_y[:, i * cells : (i + 1) * cells] for i in range(3))
+    s_xx = 2.0 * viscosity * grad_x[0]
+    s_xy = viscosity * (grad_yu + grad_x[1])
+    s_xz = viscosity * grad_x[2]
+    s_yy = 2.0 * viscosity * grad_yv
+    s_yz = viscosity * grad_yw
+    along_x = times_x(jnp.concatenate([s_xx, s_xy, s_xz], axis=0), dx[...])
+    along_y = times_y(dy[...], jnp.concatenate([s_xy, s_yy, s_yz], axis=1))
+    for i in range(3):
+        result[i] = (
+            along_x[i * lines : (i + 1) * lines] + along_y[:, i * cells : (i + 1) * cells]
+        )
+    result[3] = grad_yw
+    for step in range(count):
+        outs[step][...] = result[:, pl.ds(pl.multiple_of((me ^ step) * rows, 8), rows), :]
+
+
+def on_plane(pieces, dx, dy):
+    count = len(pieces)
+    rows, cells = pieces[0].shape[1:]
+    lines = rows * count
+    piece = jax.ShapeDtypeStruct((4, rows, cells), jnp.float32)
+    vmem = pl.BlockSpec(memory_space=pltpu.VMEM)
+    return pl.pallas_call(
+        functools.partial(plane_kernel, count),
+        out_shape=(piece,) * count,
+        in_specs=[vmem] * (2 + count),
+        out_specs=(vmem,) * count,
+        scratch_shapes=[pltpu.VMEM((4, lines, cells), jnp.float32)] * 2,
+        compiler_params=pltpu.CompilerParams(vmem_limit_bytes=vmem_bytes),
+        cost_estimate=pl.CostEstimate(
+            flops=36 * lines * cells * (cells + lines),
+            transcendentals=lines * cells,
+            bytes_accessed=32 * lines * cells,
+        ),
+        name="plane",
+    )(dx, dy, *pieces)
+
+
+def join_kernel(count, planes, *refs):
+    pieces = refs[: count * planes]
+    inverse, first_add, cross, out = refs[count * planes :]
+    me = lax.axis_index("wide")
+    for step in range(count):
+        for chunk in range(planes):
+            plane = (me ^ step) * planes + chunk
+            piece = pieces[chunk * count + step]
+            scale = inverse[plane]
+            out[0, plane] = piece[0] * scale + first_add[plane]
+            out[1, plane] = piece[1] * scale + piece[3] * cross[plane]
+            out[2, plane] = piece[2] * scale
+
+
+def join(pieces, inverse, first_add, cross, count, planes):
+    vmem = pl.BlockSpec(memory_space=pltpu.VMEM)
+    return pl.pallas_call(
+        functools.partial(join_kernel, count, planes),
+        out_shape=jax.ShapeDtypeStruct((3,) + inverse.shape, jnp.float32),
+        in_specs=[vmem] * (count * planes + 3),
+        out_specs=vmem,
+        compiler_params=pltpu.CompilerParams(vmem_limit_bytes=vmem_bytes),
+        name="join",
+    )(*pieces, inverse, first_add, cross)
+
+
+def exchange(pieces, order):
+    count = len(pieces)
+    got = [pieces[0]] + [None] * (count - 1)
+    for step in order:
+        got[step] = lax.ppermute(pieces[step], "wide", [(i, i ^ step) for i in range(count)])
+    return got
+
+
+def by_planes(velocity, level_set):
+    cells_x = velocity.shape[3]
+    slab_z, slab_y = velocity.shape[1:3]
+    count = lax.axis_size("wide")
+    group_count = lax.axis_size("grp")
+    planes = slab_z // count
+    table_x = derivative_table(cells_x).T
+    high, low = halves(table_x)
+    dx = jnp.asarray(np.concatenate([high, high, low], axis=0))
+    high, low = halves(derivative_table(slab_y * count))
+    dy = jnp.asarray(np.concatenate([high, low, high], axis=1))
+    far = list(range(count // 2, count))
+    near = list(range(1, count // 2))
+    order = [step for pair in zip(far, near + [None]) for step in pair if step is not None]
+
+    arrived = [
+        exchange(pack(velocity, level_set, count, planes, chunk), order) for chunk in range(planes)
+    ]
+    returned = []
+    for chunk in range(planes):
+        returned += exchange(on_plane(arrived[chunk], dx, dy), order)
+
+    viscosity, density = properties(level_set)
+    whole = lax.all_gather(viscosity, "grp", axis=0, tiled=True)
+    dz_rows = lax.dynamic_slice_in_dim(
+        jnp.asarray(derivative_table(slab_z * group_count)),
+        lax.axis_index("grp") * slab_z,
+        slab_z,
+        0,
+    )
+    dz_visc = jnp.einsum("ij,jyx->iyx", dz_rows, whole, precision=lax.Precision.HIGHEST)
+    inverse = 1.0 / density
+    cross = dz_visc * inverse
+    first_add = cross * along_last(velocity[2], jnp.asarray(table_x))
+    return join(returned, inverse, first_add, cross, count, planes)
+
+
+def by_lines(velocity, level_set):
     cells_x = velocity.shape[3]
     slab_z = velocity.shape[1]
     slab_y = velocity.shape[2]
@@ -62,39 +249,32 @@
     def yline(block):
         return jnp.einsum("ij,cjgk->cigk", dy_full, block, precision=lax.Precision.HIGHEST)
 
+    def y_derivative(field):
+        lines = lax.all_to_all(to_lines(field), "wide", split_axis=2, concat_axis=1, tiled=True)
+        return from_lines(
+            lax.all_to_all(yline(lines), "wide", split_axis=1, concat_axis=2, tiled=True)
+        )
+
     grad_x = along_last(velocity, dx_t)
-    grad_y = from_lines(
-        lax.all_to_all(
-            yline(
-                lax.all_to_all(to_lines(velocity), "wide", split_axis=2, concat_axis=1, tiled=True)
-            ),
-            "wide",
-            split_axis=1,
-            concat_axis=2,
-            tiled=True,
-        )
-    )
+    grad_y = y_derivative(velocity)
+    s_xx = 2.0 * viscosity * grad_x[0]
     s_xy = viscosity * (grad_y[0] + grad_x[1])
     s_yy = 2.0 * viscosity * grad_y[1]
+    s_xz = viscosity * grad_x[2]
     s_yz = viscosity * grad_y[2]
-    stresses = to_lines(jnp.stack([s_xy, s_yy, s_yz]))
-    dy_stress = from_lines(
-        lax.all_to_all(
-            yline(lax.all_to_all(stresses, "wide", split_axis=2, concat_axis=1, tiled=True)),
-            "wide",
-            split_axis=1,
-            concat_axis=2,
-            tiled=True,
-        )
-    )
-    grad_yw = grad_y[2]
-    s_xx = 2.0 * viscosity * grad_x[0]
-    s_xz = viscosity * grad_x[2]
+    dy_stress = y_derivative(jnp.stack([s_xy, s_yy, s_yz]))
     dx_stress = along_last(jnp.stack([s_xx, s_xy, s_xz]), dx_t)
     first = (dx_stress[0] + dy_stress[0] + dz_visc * grad_x[2]) / density
-    second = (dx_stress[1] + dy_stress[1] + dz_visc * grad_yw) / density
+    second = (dx_stress[1] + dy_stress[1] + dz_visc * grad_y[2]) / density
     third = (dx_stress[2] + dy_stress[2]) / density
     return jnp.stack([first, second, third])
+
+
+def shards(velocity, level_set):
+    count = lax.axis_size("wide")
+    if count & (count - 1) == 0 and velocity.shape[1] % count == 0:
+        return by_planes(velocity, level_set)
+    return by_lines(velocity, level_set)
 
 
 def solution(mesh):

time: 217 us -> 171 us (0.79)
  the two profiles are of different devices: /device:TPU:0 before, /device:TPU:8 now
where the time goes in v1:
time: 171 us; the launch traced here: 170 us
  Pallas kernels  71.4 us (42%)
  starting transfers between devices  43.5 us (25%)
  waiting for transfers between devices  31.9 us (19%)
  between operations  13.6 us (8%)
  matrix products  6.02 us (4%)
  other arithmetic  2.3 us (1%)
    pallas_call x2, Pallas kernels, pack(): pl.pallas_call(functools.partial(pack_kernel, count, planes, chunk), out_...  66 us
    ppermute x28, starting transfers between devices, exchange(): lax.ppermute(pieces[step], 'wide', [(i, i ^ step) for i in range(count)])  43.5 us
    ppermute x28, waiting for transfers between devices, exchange(): lax.ppermute(pieces[step], 'wide', [(i, i ^ step) for i in range(count)])  31.9 us
    pallas_call x2, Pallas kernels, on_plane(): pl.pallas_call(functools.partial(plane_kernel, count), out_shape=(piece,)...  3.92 us
    dot_general x1, matrix products, by_planes(): jnp.einsum('ij,jyx->iyx', dz_rows, whole, precision=lax.Precision.HIGHEST)  3.89 us
  transfers between devices with their start and end apart: 29, of which 10 were waited for; matrix products, arithmetic and copies ran while one was open for 4% of the time, Pallas kernels for 41%

profile of v1, /device:TPU:8, one launch (start us, length us, event | category | flops | bytes accessed | tf_op | source)
XLA Modules:
  0.0 170.2 jit_solution(7855006467874039469)
XLA Ops:
  6.5 1.9 %multiply_add_fusion = f32[16,16,512]{2,1,0:T(8,128)} fusion(f32[16,16,512]{2,1,0:T(8,128)} %level_set.3), kind=kLoop, calls=%fused_computation.7 | loop fusion | flops 393216 | bytes 1048576 | tf_op jit(solution)/shard_map/add | solution.py:37
  8.5 0.0 all-gather.2.cloned.1.call-update
  8.5 0.0 copy-start.3
  8.5 33.0 %pack.2 = (f32[4,16,512]{2,1,0:T(8,128)}, f32[4,16,512]{2,1,0:T(8,128)}, f32[4,16,512]{2,1,0:T(8,128)}, f32[4,16,512]{2,1,0:T(8,128)}, f32[4,16,512]{2,1,0:T(8,1...) custom-call(f32[3,16,16,512]{3,2,1,0:T(8,128)} %velocity.3, f32[16,16,512]{2,1,0:T(8,128)} %level_set.3), custom_call_target="tpu_custom_call" | custom-call | bytes 2097152 | tf_op jit(solution)/shard_map/pack/pallas_call | solution.py:61
  41.6 1.6 collective-permute-start
  43.1 0.4 collective-permute-start.1
  43.6 1.5 collective-permute-start.2
  45.1 2.6 %collective-permute-start.3 = (f32[4,16,512]{2,1,0:T(8,128)}, f32[4,16,512]{2,1,0:T(8,128)S(1)}, u32[]{:S(2)}, u32[]{:S(2)}) collective-permute-start(f32[4,16,512]{2,1,0:T(8,128)} %get-tuple-element.41), channel_id=1, source_target_pairs={{0,4},{1,5},{2,6},{3,7},{4,0},{5,1},{6,2},{7,3},{8,12},{9,13},{10,... | collective-permute-start | bytes 393224 | tf_op jit(solution)/shard_map/ppermute | solution.py:175
  47.7 1.3 collective-permute-start.4
  49.0 33.0 %pack.3 = (f32[4,16,512]{2,1,0:T(8,128)}, f32[4,16,512]{2,1,0:T(8,128)}, f32[4,16,512]{2,1,0:T(8,128)}, f32[4,16,512]{2,1,0:T(8,128)}, f32[4,16,512]{2,1,0:T(8,1...) custom-call(f32[3,16,16,512]{3,2,1,0:T(8,128)} %velocity.3, f32[16,16,512]{2,1,0:T(8,128)} %level_set.3), custom_call_target="tpu_custom_call" | custom-call | bytes 2097152 | tf_op jit(solution)/shard_map/pack/pallas_call | solution.py:61
  82.0 1.6 collective-permute-start.5
  83.7 0.4 collective-permute-start.6
  84.1 1.5 collective-permute-start.14
  85.6 2.2 %collective-permute-start.15 = (f32[4,16,512]{2,1,0:T(8,128)}, f32[4,16,512]{2,1,0:T(8,128)S(1)}, u32[]{:S(2)}, u32[]{:S(2)}) collective-permute-start(f32[4,16,512]{2,1,0:T(8,128)} %get-tuple-element.55), channel_id=1, source_target_pairs={{0,2},{1,3},{2,0},{3,1},{4,6},{5,7},{6,4},{7,5},{8,10},{9,11},{10,... | collective-permute-start | bytes 393224 | tf_op jit(solution)/shard_map/ppermute | solution.py:175
  87.8 4.8 %collective-permute-done.5.refs_6_ = f32[4,16,512]{2,1,0:T(8,128)S(1)} collective-permute-done((f32[4,16,512]{2,1,0:T(8,128)S(1)}, f32[4,16,512]{2,1,0:T(8,128)S(1)}, u32[]{:S(2)}, u32[]{:S(2)}) %collective-permute-start.5) | collective-permute-done | bytes 131104 | tf_op jit(solution)/shard_map/ppermute | solution.py:175
  92.6 0.3 collective-permute-start.17
  92.9 4.8 %collective-permute-done.6.refs_7_ = f32[4,16,512]{2,1,0:T(8,128)S(1)} collective-permute-done((f32[4,16,512]{2,1,0:T(8,128)S(1)}, f32[4,16,512]{2,1,0:T(8,128)S(1)}, u32[]{:S(2)}, u32[]{:S(2)}) %collective-permute-start.6) | collective-permute-done | bytes 131104 | tf_op jit(solution)/shard_map/ppermute | solution.py:175
  97.7 7.3 %collective-permute-start.19 = (f32[4,16,512]{2,1,0:T(8,128)}, f32[4,16,512]{2,1,0:T(8,128)S(1)}, u32[]{:S(2)}, u32[]{:S(2)}) collective-permute-start(f32[4,16,512]{2,1,0:T(8,128)} %get-tuple-element.59), channel_id=1, source_target_pairs={{0,6},{1,7},{2,4},{3,5},{4,2},{5,3},{6,0},{7,1},{8,14},{9,15},{10,... | collective-permute-start | bytes 393224 | tf_op jit(solution)/shard_map/ppermute | solution.py:175
  105.0 1.0 collective-permute-start.20
  106.0 1.4 copy-done.2
  107.4 2.0 %plane.2 = (f32[4,16,512]{2,1,0:T(8,128)S(1)}, f32[4,16,512]{2,1,0:T(8,128)S(1)}, f32[4,16,512]{2,1,0:T(8,128)S(1)}, f32[4,16,512]{2,1,0:T(8,128)S(1)}, f32[4,16...) custom-call(bf16[1536,512]{1,0:T(8,128)(2,1)S(1)} %copy-done.2, ...), custom_call_target="tpu_custom_call" | custom-call | flops 1509949440 | bytes 2097152 | tf_op jit(solution)/shard_map/plane/pallas_call | solution.py:129
  109.4 0.6 collective-permute-start.7
  110.0 6.2 %collective-permute-start.8 = (f32[4,16,512]{2,1,0:T(8,128)S(1)}, f32[4,16,512]{2,1,0:T(8,128)S(1)}, u32[]{:S(2)}, u32[]{:S(2)}) collective-permute-start(f32[4,16,512]{2,1,0:T(8,128)S(1)} %get-tuple-element.47), channel_id=1, source_target_pairs={{0,2},{1,3},{2,0},{3,1},{4,6},{5,7},{6,4},{7,5},{8,10},{9,11},{10,... | collective-permute-start | bytes 393224 | tf_op jit(solution)/shard_map/ppermute | solution.py:175
  116.2 0.0 collective-permute-start.9
  116.2 1.0 collective-permute-done.19.refs_6_
  117.2 2.8 %collective-permute-done.20.refs_7_ = f32[4,16,512]{2,1,0:T(8,128)S(1)} collective-permute-done((f32[4,16,512]{2,1,0:T(8,128)}, f32[4,16,512]{2,1,0:T(8,128)S(1)}, u32[]{:S(2)}, u32[]{:S(2)}) %collective-permute-start.20) | collective-permute-done | bytes 131104 | tf_op jit(solution)/shard_map/ppermute | solution.py:175
  120.0 0.5 collective-permute-start.11
  120.5 2.0 %plane.3 = (f32[4,16,512]{2,1,0:T(8,128)S(1)}, f32[4,16,512]{2,1,0:T(8,128)S(1)}, f32[4,16,512]{2,1,0:T(8,128)S(1)}, f32[4,16,512]{2,1,0:T(8,128)S(1)}, f32[4,16...) custom-call(bf16[1536,512]{1,0:T(8,128)(2,1)S(1)} %copy-done.2, ...), custom_call_target="tpu_custom_call" | custom-call | flops 1509949440 | bytes 2097152 | tf_op jit(solution)/shard_map/plane/pallas_call | solution.py:129
  122.5 0.0 copy-start.4
  122.5 0.0 all-gather.2.cloned.1.call-done
  122.5 0.0 copy-start.7
  122.5 3.9 %fusion = f32[16,16,512]{2,0,1:T(8,128)S(1)} fusion(f32[64,16,512]{2,1,0:T(8,128)} %all-gather.2.cloned.1.call-done, f32[64,64]{1,0:T(8,128)} %constant.34.clone, s32[]{:T(128)S(6)} %select_n.3), kind=kOutput, calls=%fused_computation | convolution fusion | flops 100663296 | bytes 2629636 | tf_op jit(solution)/shard_map/ij,jyx->iyx/dot_general | solution.py:209
  126.4 2.0 %collective-permute-start.12 = (f32[4,16,512]{2,1,0:T(8,128)S(1)}, f32[4,16,512]{2,1,0:T(8,128)S(1)}, u32[]{:S(2)}, u32[]{:S(2)}) collective-permute-start(f32[4,16,512]{2,1,0:T(8,128)S(1)} %get-tuple-element.51), channel_id=1, source_target_pairs={{0,6},{1,7},{2,4},{3,5},{4,2},{5,3},{6,0},{7,1},{8,14},{9,15},{10,... | collective-permute-start | bytes 393224 | tf_op jit(solution)/shard_map/ppermute | solution.py:175
  128.4 1.0 collective-permute-start.13
  129.5 0.5 collective-permute-start.21
  130.0 6.0 %collective-permute-start.22 = (f32[4,16,512]{2,1,0:T(8,128)S(1)}, f32[4,16,512]{2,1,0:T(8,128)S(1)}, u32[]{:S(2)}, u32[]{:S(2)}) collective-permute-start(f32[4,16,512]{2,1,0:T(8,128)S(1)} %get-tuple-element.63), channel_id=1, source_target_pairs={{0,2},{1,3},{2,0},{3,1},{4,6},{5,7},{6,4},{7,5},{8,10},{9,11},{10,... | collective-permute-start | bytes 393224 | tf_op jit(solution)/shard_map/ppermute | solution.py:175
  136.0 0.4 copy_multiply_fusion
  136.4 0.2 collective-permute-start.23
  136.6 3.5 %collective-permute-done.12.refs_6_ = f32[4,16,512]{2,1,0:T(8,128)S(1)} collective-permute-done((f32[4,16,512]{2,1,0:T(8,128)S(1)}, f32[4,16,512]{2,1,0:T(8,128)S(1)}, u32[]{:S(2)}, u32[]{:S(2)}) %collective-permute-start.12) | collective-permute-done | bytes 131104 | tf_op jit(solution)/shard_map/ppermute | solution.py:175
  140.1 2.7 %collective-permute-done.13.refs_7_ = f32[4,16,512]{2,1,0:T(8,128)S(1)} collective-permute-done((f32[4,16,512]{2,1,0:T(8,128)S(1)}, f32[4,16,512]{2,1,0:T(8,128)S(1)}, u32[]{:S(2)}, u32[]{:S(2)}) %collective-permute-start.13) | collective-permute-done | bytes 131104 | tf_op jit(solution)/shard_map/ppermute | solution.py:175
  142.8 1.7 collective-permute-start.26
  144.4 3.0 %collective-permute-start.27 = (f32[4,16,512]{2,1,0:T(8,128)S(1)}, f32[4,16,512]{2,1,0:T(8,128)S(1)}, u32[]{:S(2)}, u32[]{:S(2)}) collective-permute-start(f32[4,16,512]{2,1,0:T(8,128)S(1)} %get-tuple-element.68), channel_id=1, source_target_pairs={{0,7},{1,6},{2,5},{3,4},{4,3},{5,2},{6,1},{7,0},{8,15},{9,14},{10,... | collective-permute-start | bytes 393224 | tf_op jit(solution)/shard_map/ppermute | solution.py:175
  147.4 2.1 %fusion.2.refs_17_ = f32[16,16,512]{2,1,0:T(8,128)S(1)} fusion(f32[16,16,512]{2,1,0:T(8,128)S(1)} %get-tuple-element.69.refs_18_, f32[512,512,1]{1,0,2:T(8,128)S(1)} %copy-done.7, f32[3,16,16,512]{3,2,1,0:T(8,128)} %velocity.3), kind=kOutput, calls=%fused_computation.3 | convolution fusion | flops 805437440 | bytes 2621440 | tf_op jit(solution)/shard_map/dot_general | solution.py:32
  149.6 5.4 %collective-permute-done.24.refs_12_ = f32[4,16,512]{2,1,0:T(8,128)S(1)} collective-permute-done((f32[4,16,512]{2,1,0:T(8,128)S(1)}, f32[4,16,512]{2,1,0:T(8,128)S(1)}, u32[]{:S(2)}, u32[]{:S(2)}) %collective-permute-start.24) | collective-permute-done | bytes 131104 | tf_op jit(solution)/shard_map/ppermute | solution.py:175
  155.0 2.8 %collective-permute-done.25.refs_13_ = f32[4,16,512]{2,1,0:T(8,128)S(1)} collective-permute-done((f32[4,16,512]{2,1,0:T(8,128)S(1)}, f32[4,16,512]{2,1,0:T(8,128)S(1)}, u32[]{:S(2)}, u32[]{:S(2)}) %collective-permute-start.25) | collective-permute-done | bytes 131104 | tf_op jit(solution)/shard_map/ppermute | solution.py:175
  157.8 3.1 %collective-permute-done.26.refs_14_ = f32[4,16,512]{2,1,0:T(8,128)S(1)} collective-permute-done((f32[4,16,512]{2,1,0:T(8,128)S(1)}, f32[4,16,512]{2,1,0:T(8,128)S(1)}, u32[]{:S(2)}, u32[]{:S(2)}) %collective-permute-start.26) | collective-permute-done | bytes 131104 | tf_op jit(solution)/shard_map/ppermute | solution.py:175
  160.9 1.0 collective-permute-done.27.refs_15_
  161.9 1.4 join.1
  (36 shorter events, 0.1 us)
Async XLA Ops:
  6.5 116.0 %all-gather.2.cloned.1.call-start = ((), (), s32[]{:S(2)}) async-start(), calls=%async_computation | async-start | bytes 2621440 | tf_op jit(solution)/shard_map/all_gather | solution.py:202
  8.5 97.5 %copy-start.3 = (bf16[128,384]{1,0:T(8,128)(2,1)S(1)}, bf16[128,384]{1,0:T(8,128)(2,1)}, u32[]{:S(2)}) copy-start(bf16[128,384]{1,0:T(8,128)(2,1)} %constant.33.clone.dy) | copy-start | bytes 294916
  41.5 40.5 %copy-start.6 = (f32[4,16,512]{2,1,0:T(8,128)S(1)}, f32[4,16,512]{2,1,0:T(8,128)}, u32[]{:S(2)}) copy-start(f32[4,16,512]{2,1,0:T(8,128)} %get-tuple-element.43) | copy-start | bytes 393220
  41.5 42.1 %copy-start.5 = (f32[4,16,512]{2,1,0:T(8,128)S(1)}, f32[4,16,512]{2,1,0:T(8,128)}, u32[]{:S(2)}) copy-start(f32[4,16,512]{2,1,0:T(8,128)} %get-tuple-element.44) | copy-start | bytes 393220
  41.5 64.5 %copy-start.1 = (f32[4,16,512]{2,1,0:T(8,128)S(1)}, f32[4,16,512]{2,1,0:T(8,128)}, u32[]{:S(2)}) copy-start(f32[4,16,512]{2,1,0:T(8,128)} %get-tuple-element.37.refs_0_) | copy-start | bytes 393220
  41.6 40.5 %collective-permute-start = (f32[4,16,512]{2,1,0:T(8,128)}, f32[4,16,512]{2,1,0:T(8,128)S(1)}, u32[]{:S(2)}, u32[]{:S(2)}) collective-permute-start(f32[4,16,512]{2,1,0:T(8,128)} %get-tuple-element.38), channel_id=1, source_target_pairs={{0,1},{1,0},{2,3},{3,2},{4,5},{5,4},{6,7},{7,6},{8,9},{9,8},{10,11... | collective-permute-start | bytes 393224 | tf_op jit(solution)/shard_map/ppermute | solution.py:175
  43.1 40.5 %collective-permute-start.1 = (f32[4,16,512]{2,1,0:T(8,128)}, f32[4,16,512]{2,1,0:T(8,128)S(1)}, u32[]{:S(2)}, u32[]{:S(2)}) collective-permute-start(f32[4,16,512]{2,1,0:T(8,128)} %get-tuple-element.39), channel_id=1, source_target_pairs={{0,2},{1,3},{2,0},{3,1},{4,6},{5,7},{6,4},{7,5},{8,10},{9,11},{10,... | collective-permute-start | bytes 393224 | tf_op jit(solution)/shard_map/ppermute | solution.py:175
  43.6 40.5 %collective-permute-start.2 = (f32[4,16,512]{2,1,0:T(8,128)}, f32[4,16,512]{2,1,0:T(8,128)S(1)}, u32[]{:S(2)}, u32[]{:S(2)}) collective-permute-start(f32[4,16,512]{2,1,0:T(8,128)} %get-tuple-element.40), channel_id=1, source_target_pairs={{0,3},{1,2},{2,1},{3,0},{4,7},{5,6},{6,5},{7,4},{8,11},{9,10},{10,... | collective-permute-start | bytes 393224 | tf_op jit(solution)/shard_map/ppermute | solution.py:175
  45.1 40.5 %collective-permute-start.3 = (f32[4,16,512]{2,1,0:T(8,128)}, f32[4,16,512]{2,1,0:T(8,128)S(1)}, u32[]{:S(2)}, u32[]{:S(2)}) collective-permute-start(f32[4,16,512]{2,1,0:T(8,128)} %get-tuple-element.41), channel_id=1, source_target_pairs={{0,4},{1,5},{2,6},{3,7},{4,0},{5,1},{6,2},{7,3},{8,12},{9,13},{10,... | collective-permute-start | bytes 393224 | tf_op jit(solution)/shard_map/ppermute | solution.py:175
  47.7 40.1 %collective-permute-start.4 = (f32[4,16,512]{2,1,0:T(8,128)}, f32[4,16,512]{2,1,0:T(8,128)S(1)}, u32[]{:S(2)}, u32[]{:S(2)}) collective-permute-start(f32[4,16,512]{2,1,0:T(8,128)} %get-tuple-element.42), channel_id=1, source_target_pairs={{0,5},{1,4},{2,7},{3,6},{4,1},{5,0},{6,3},{7,2},{8,13},{9,12},{10,... | collective-permute-start | bytes 393224 | tf_op jit(solution)/shard_map/ppermute | solution.py:175
  82.0 10.6 %collective-permute-start.5 = (f32[4,16,512]{2,1,0:T(8,128)S(1)}, f32[4,16,512]{2,1,0:T(8,128)S(1)}, u32[]{:S(2)}, u32[]{:S(2)}) collective-permute-start(f32[4,16,512]{2,1,0:T(8,128)S(1)} %copy-done.6), channel_id=1, source_target_pairs={{0,6},{1,7},{2,4},{3,5},{4,2},{5,3},{6,0},{7,1},{8,14},{9,15},{10,... | collective-permute-start | bytes 393224 | tf_op jit(solution)/shard_map/ppermute | solution.py:175
  83.7 14.0 %collective-permute-start.6 = (f32[4,16,512]{2,1,0:T(8,128)S(1)}, f32[4,16,512]{2,1,0:T(8,128)S(1)}, u32[]{:S(2)}, u32[]{:S(2)}) collective-permute-start(f32[4,16,512]{2,1,0:T(8,128)S(1)} %copy-done.5), channel_id=1, source_target_pairs={{0,7},{1,6},{2,5},{3,4},{4,3},{5,2},{6,1},{7,0},{8,15},{9,14},{10,... | collective-permute-start | bytes 393224 | tf_op jit(solution)/shard_map/ppermute | solution.py:175
  84.1 13.6 %collective-permute-start.14 = (f32[4,16,512]{2,1,0:T(8,128)}, f32[4,16,512]{2,1,0:T(8,128)S(1)}, u32[]{:S(2)}, u32[]{:S(2)}) collective-permute-start(f32[4,16,512]{2,1,0:T(8,128)} %get-tuple-element.54), channel_id=1, source_target_pairs={{0,1},{1,0},{2,3},{3,2},{4,5},{5,4},{6,7},{7,6},{8,9},{9,8},{10,11... | collective-permute-start | bytes 393224 | tf_op jit(solution)/shard_map/ppermute | solution.py:175
  85.6 19.4 %collective-permute-start.15 = (f32[4,16,512]{2,1,0:T(8,128)}, f32[4,16,512]{2,1,0:T(8,128)S(1)}, u32[]{:S(2)}, u32[]{:S(2)}) collective-permute-start(f32[4,16,512]{2,1,0:T(8,128)} %get-tuple-element.55), channel_id=1, source_target_pairs={{0,2},{1,3},{2,0},{3,1},{4,6},{5,7},{6,4},{7,5},{8,10},{9,11},{10,... | collective-permute-start | bytes 393224 | tf_op jit(solution)/shard_map/ppermute | solution.py:175
  87.8 21.6 %collective-permute-start.16 = (f32[4,16,512]{2,1,0:T(8,128)}, f32[4,16,512]{2,1,0:T(8,128)S(1)}, u32[]{:S(2)}, u32[]{:S(2)}) collective-permute-start(f32[4,16,512]{2,1,0:T(8,128)} %get-tuple-element.56), channel_id=1, source_target_pairs={{0,3},{1,2},{2,1},{3,0},{4,7},{5,6},{6,5},{7,4},{8,11},{9,10},{10,... | collective-permute-start | bytes 393224 | tf_op jit(solution)/shard_map/ppermute | solution.py:175
  92.6 17.4 %collective-permute-start.17 = (f32[4,16,512]{2,1,0:T(8,128)}, f32[4,16,512]{2,1,0:T(8,128)S(1)}, u32[]{:S(2)}, u32[]{:S(2)}) collective-permute-start(f32[4,16,512]{2,1,0:T(8,128)} %get-tuple-element.57), channel_id=1, source_target_pairs={{0,4},{1,5},{2,6},{3,7},{4,0},{5,1},{6,2},{7,3},{8,12},{9,13},{10,... | collective-permute-start | bytes 393224 | tf_op jit(solution)/shard_map/ppermute | solution.py:175
  97.7 18.5 %collective-permute-start.18 = (f32[4,16,512]{2,1,0:T(8,128)}, f32[4,16,512]{2,1,0:T(8,128)S(1)}, u32[]{:S(2)}, u32[]{:S(2)}) collective-permute-start(f32[4,16,512]{2,1,0:T(8,128)} %get-tuple-element.58), channel_id=1, source_target_pairs={{0,5},{1,4},{2,7},{3,6},{4,1},{5,0},{6,3},{7,2},{8,13},{9,12},{10,... | collective-permute-start | bytes 393224 | tf_op jit(solution)/shard_map/ppermute | solution.py:175
  97.7 19.5 %collective-permute-start.19 = (f32[4,16,512]{2,1,0:T(8,128)}, f32[4,16,512]{2,1,0:T(8,128)S(1)}, u32[]{:S(2)}, u32[]{:S(2)}) collective-permute-start(f32[4,16,512]{2,1,0:T(8,128)} %get-tuple-element.59), channel_id=1, source_target_pairs={{0,6},{1,7},{2,4},{3,5},{4,2},{5,3},{6,0},{7,1},{8,14},{9,15},{10,... | collective-permute-start | bytes 393224 | tf_op jit(solution)/shard_map/ppermute | solution.py:175
  105.0 15.0 %collective-permute-start.20 = (f32[4,16,512]{2,1,0:T(8,128)}, f32[4,16,512]{2,1,0:T(8,128)S(1)}, u32[]{:S(2)}, u32[]{:S(2)}) collective-permute-start(f32[4,16,512]{2,1,0:T(8,128)} %get-tuple-element.60), channel_id=1, source_target_pairs={{0,7},{1,6},{2,5},{3,4},{4,3},{5,2},{6,1},{7,0},{8,15},{9,14},{10,... | collective-permute-start | bytes 393224 | tf_op jit(solution)/shard_map/ppermute | solution.py:175
  106.0 1.4 copy-start.2
  107.4 13.1 %copy-start = (f32[4,16,512]{2,1,0:T(8,128)S(1)}, f32[4,16,512]{2,1,0:T(8,128)}, u32[]{:S(2)}) copy-start(f32[4,16,512]{2,1,0:T(8,128)} %get-tuple-element.53.refs_0_) | copy-start | bytes 393220
  109.4 17.0 %collective-permute-start.7 = (f32[4,16,512]{2,1,0:T(8,128)S(1)}, f32[4,16,512]{2,1,0:T(8,128)S(1)}, u32[]{:S(2)}, u32[]{:S(2)}) collective-permute-start(f32[4,16,512]{2,1,0:T(8,128)S(1)} %get-tuple-element.46), channel_id=1, source_target_pairs={{0,1},{1,0},{2,3},{3,2},{4,5},{5,4},{6,7},{7,6},{8,9},{9,8},{10,11... | collective-permute-start | bytes 393224 | tf_op jit(solution)/shard_map/ppermute | solution.py:175
  110.0 18.5 %collective-permute-start.8 = (f32[4,16,512]{2,1,0:T(8,128)S(1)}, f32[4,16,512]{2,1,0:T(8,128)S(1)}, u32[]{:S(2)}, u32[]{:S(2)}) collective-permute-start(f32[4,16,512]{2,1,0:T(8,128)S(1)} %get-tuple-element.47), channel_id=1, source_target_pairs={{0,2},{1,3},{2,0},{3,1},{4,6},{5,7},{6,4},{7,5},{8,10},{9,11},{10,... | collective-permute-start | bytes 393224 | tf_op jit(solution)/shard_map/ppermute | solution.py:175
  116.2 13.3 %collective-permute-start.9 = (f32[4,16,512]{2,1,0:T(8,128)S(1)}, f32[4,16,512]{2,1,0:T(8,128)S(1)}, u32[]{:S(2)}, u32[]{:S(2)}) collective-permute-start(f32[4,16,512]{2,1,0:T(8,128)S(1)} %get-tuple-element.48), channel_id=1, source_target_pairs={{0,3},{1,2},{2,1},{3,0},{4,7},{5,6},{6,5},{7,4},{8,11},{9,10},{10,... | collective-permute-start | bytes 393224 | tf_op jit(solution)/shard_map/ppermute | solution.py:175
  117.2 12.8 %collective-permute-start.10 = (f32[4,16,512]{2,1,0:T(8,128)S(1)}, f32[4,16,512]{2,1,0:T(8,128)S(1)}, u32[]{:S(2)}, u32[]{:S(2)}) collective-permute-start(f32[4,16,512]{2,1,0:T(8,128)S(1)} %get-tuple-element.49), channel_id=1, source_target_pairs={{0,4},{1,5},{2,6},{3,7},{4,0},{5,1},{6,2},{7,3},{8,12},{9,13},{10,... | collective-permute-start | bytes 393224 | tf_op jit(solution)/shard_map/ppermute | solution.py:175
  120.0 16.4 %collective-permute-start.11 = (f32[4,16,512]{2,1,0:T(8,128)S(1)}, f32[4,16,512]{2,1,0:T(8,128)S(1)}, u32[]{:S(2)}, u32[]{:S(2)}) collective-permute-start(f32[4,16,512]{2,1,0:T(8,128)S(1)} %get-tuple-element.50), channel_id=1, source_target_pairs={{0,5},{1,4},{2,7},{3,6},{4,1},{5,0},{6,3},{7,2},{8,13},{9,12},{10,... | collective-permute-start | bytes 393224 | tf_op jit(solution)/shard_map/ppermute | solution.py:175
  122.5 13.5 %copy-start.4 = (f32[16,16,512]{2,1,0:T(8,128)S(1)}, f32[16,16,512]{2,1,0:T(8,128)}, u32[]{:S(2)}) copy-start(f32[16,16,512]{2,1,0:T(8,128)} %level_set.3) | copy-start | bytes 1572868
  122.5 24.9 %copy-start.7 = (f32[512,512,1]{1,0,2:T(8,128)S(1)}, f32[512,512,1]{1,0,2:T(8,128)}, u32[]{:S(2)}) copy-start(f32[512,512,1]{1,0,2:T(8,128)} %constant.36) | copy-start | bytes 3145732
  126.4 13.6 %collective-permute-start.12 = (f32[4,16,512]{2,1,0:T(8,128)S(1)}, f32[4,16,512]{2,1,0:T(8,128)S(1)}, u32[]{:S(2)}, u32[]{:S(2)}) collective-permute-start(f32[4,16,512]{2,1,0:T(8,128)S(1)} %get-tuple-element.51), channel_id=1, source_target_pairs={{0,6},{1,7},{2,4},{3,5},{4,2},{5,3},{6,0},{7,1},{8,14},{9,15},{10,... | collective-permute-start | bytes 393224 | tf_op jit(solution)/shard_map/ppermute | solution.py:175
  128.4 14.3 %collective-permute-start.13 = (f32[4,16,512]{2,1,0:T(8,128)S(1)}, f32[4,16,512]{2,1,0:T(8,128)S(1)}, u32[]{:S(2)}, u32[]{:S(2)}) collective-permute-start(f32[4,16,512]{2,1,0:T(8,128)S(1)} %get-tuple-element.52), channel_id=1, source_target_pairs={{0,7},{1,6},{2,5},{3,4},{4,3},{5,2},{6,1},{7,0},{8,15},{9,14},{10,... | collective-permute-start | bytes 393224 | tf_op jit(solution)/shard_map/ppermute | solution.py:175
  129.5 13.3 %collective-permute-start.21 = (f32[4,16,512]{2,1,0:T(8,128)S(1)}, f32[4,16,512]{2,1,0:T(8,128)S(1)}, u32[]{:S(2)}, u32[]{:S(2)}) collective-permute-start(f32[4,16,512]{2,1,0:T(8,128)S(1)} %get-tuple-element.62), channel_id=1, source_target_pairs={{0,1},{1,0},{2,3},{3,2},{4,5},{5,4},{6,7},{7,6},{8,9},{9,8},{10,11... | collective-permute-start | bytes 393224 | tf_op jit(solution)/shard_map/ppermute | solution.py:175
  130.0 14.4 %collective-permute-start.22 = (f32[4,16,512]{2,1,0:T(8,128)S(1)}, f32[4,16,512]{2,1,0:T(8,128)S(1)}, u32[]{:S(2)}, u32[]{:S(2)}) collective-permute-start(f32[4,16,512]{2,1,0:T(8,128)S(1)} %get-tuple-element.63), channel_id=1, source_target_pairs={{0,2},{1,3},{2,0},{3,1},{4,6},{5,7},{6,4},{7,5},{8,10},{9,11},{10,... | collective-permute-start | bytes 393224 | tf_op jit(solution)/shard_map/ppermute | solution.py:175
  136.4 13.2 %collective-permute-start.23 = (f32[4,16,512]{2,1,0:T(8,128)S(1)}, f32[4,16,512]{2,1,0:T(8,128)S(1)}, u32[]{:S(2)}, u32[]{:S(2)}) collective-permute-start(f32[4,16,512]{2,1,0:T(8,128)S(1)} %get-tuple-element.64), channel_id=1, source_target_pairs={{0,3},{1,2},{2,1},{3,0},{4,7},{5,6},{6,5},{7,4},{8,11},{9,10},{10,... | collective-permute-start | bytes 393224 | tf_op jit(solution)/shard_map/ppermute | solution.py:175
  140.1 14.9 %collective-permute-start.24 = (f32[4,16,512]{2,1,0:T(8,128)S(1)}, f32[4,16,512]{2,1,0:T(8,128)S(1)}, u32[]{:S(2)}, u32[]{:S(2)}) collective-permute-start(f32[4,16,512]{2,1,0:T(8,128)S(1)} %get-tuple-element.65), channel_id=1, source_target_pairs={{0,4},{1,5},{2,6},{3,7},{4,0},{5,1},{6,2},{7,3},{8,12},{9,13},{10,... | collective-permute-start | bytes 393224 | tf_op jit(solution)/shard_map/ppermute | solution.py:175
  142.8 15.0 %collective-permute-start.25 = (f32[4,16,512]{2,1,0:T(8,128)S(1)}, f32[4,16,512]{2,1,0:T(8,128)S(1)}, u32[]{:S(2)}, u32[]{:S(2)}) collective-permute-start(f32[4,16,512]{2,1,0:T(8,128)S(1)} %get-tuple-element.66), channel_id=1, source_target_pairs={{0,5},{1,4},{2,7},{3,6},{4,1},{5,0},{6,3},{7,2},{8,13},{9,12},{10,... | collective-permute-start | bytes 393224 | tf_op jit(solution)/shard_map/ppermute | solution.py:175
  142.8 18.1 %collective-permute-start.26 = (f32[4,16,512]{2,1,0:T(8,128)S(1)}, f32[4,16,512]{2,1,0:T(8,128)S(1)}, u32[]{:S(2)}, u32[]{:S(2)}) collective-permute-start(f32[4,16,512]{2,1,0:T(8,128)S(1)} %get-tuple-element.67), channel_id=1, source_target_pairs={{0,6},{1,7},{2,4},{3,5},{4,2},{5,3},{6,0},{7,1},{8,14},{9,15},{10,... | collective-permute-start | bytes 393224 | tf_op jit(solution)/shard_map/ppermute | solution.py:175
  144.4 17.5 %collective-permute-start.27 = (f32[4,16,512]{2,1,0:T(8,128)S(1)}, f32[4,16,512]{2,1,0:T(8,128)S(1)}, u32[]{:S(2)}, u32[]{:S(2)}) collective-permute-start(f32[4,16,512]{2,1,0:T(8,128)S(1)} %get-tuple-element.68), channel_id=1, source_target_pairs={{0,7},{1,6},{2,5},{3,4},{4,3},{5,2},{6,1},{7,0},{8,15},{9,14},{10,... | collective-permute-start | bytes 393224 | tf_op jit(solution)/shard_map/ppermute | solution.py:175
Sparse Core Ops, SparseCore 0:
  8.9 23.7 all-gather.1

commit v2 on v1

--- a/solution.py
+++ b/solution.py
@@ -37,35 +37,27 @@
     return (0.2 + 0.8 * heavy, 0.25 + 0.75 * heavy)
 
 
-def pack_kernel(count, planes, chunk, velocity, level_set, *refs):
-    outs, sems = refs[:count], refs[count]
+def pack_kernel(count, planes, velocity, level_set, *outs):
     me = lax.axis_index("wide")
-    copies = []
-    for step in range(count):
-        plane = (me ^ step) * planes + chunk
-        copies.append(
-            pltpu.make_async_copy(velocity.at[:, plane], outs[step].at[0:3], sems.at[step, 0])
-        )
-        copies.append(
-            pltpu.make_async_copy(level_set.at[plane], outs[step].at[3], sems.at[step, 1])
-        )
-    for copy in copies:
-        copy.start()
-    for copy in copies:
-        copy.wait()
-
-
-def pack(velocity, level_set, count, planes, chunk):
+    for chunk in range(planes):
+        for step in range(count):
+            plane = (me ^ step) * planes + chunk
+            outs[chunk * count + step][0:3] = velocity[:, plane]
+            outs[chunk * count + step][3] = level_set[plane]
+
+
+def pack(velocity, level_set, count, planes):
     rows, cells = level_set.shape[1:]
     piece = jax.ShapeDtypeStruct((4, rows, cells), jnp.float32)
+    vmem = pl.BlockSpec(memory_space=pltpu.VMEM)
     return pl.pallas_call(
-        functools.partial(pack_kernel, count, planes, chunk),
-        out_shape=(piece,) * count,
-        in_specs=[pl.BlockSpec(memory_space=pl.ANY)] * 2,
-        out_specs=(pl.BlockSpec(memory_space=pl.ANY),) * count,
-        scratch_shapes=[pltpu.SemaphoreType.DMA((count, 2))],
+        functools.partial(pack_kernel, count, planes),
+        out_shape=(piece,) * (count * planes),
+        in_specs=[vmem] * 2,
+        out_specs=(vmem,) * (count * planes),
+        compiler_params=pltpu.CompilerParams(vmem_limit_bytes=vmem_bytes),
         cost_estimate=pl.CostEstimate(
-            flops=0, transcendentals=0, bytes_accessed=2 * count * 16 * rows * cells
+            flops=0, transcendentals=0, bytes_accessed=2 * count * planes * 16 * rows * cells
         ),
         name="pack",
     )(velocity, level_set)
@@ -191,22 +183,27 @@
     near = list(range(1, count // 2))
     order = [step for pair in zip(far, near + [None]) for step in pair if step is not None]
 
-    arrived = [
-        exchange(pack(velocity, level_set, count, planes, chunk), order) for chunk in range(planes)
-    ]
+    pieces = pack(velocity, level_set, count, planes)
+    arrived = [exchange(pieces[i * count : (i + 1) * count], order) for i in range(planes)]
     returned = []
     for chunk in range(planes):
         returned += exchange(on_plane(arrived[chunk], dx, dy), order)
 
     viscosity, density = properties(level_set)
-    whole = lax.all_gather(viscosity, "grp", axis=0, tiled=True)
-    dz_rows = lax.dynamic_slice_in_dim(
-        jnp.asarray(derivative_table(slab_z * group_count)),
-        lax.axis_index("grp") * slab_z,
-        slab_z,
-        0,
-    )
-    dz_visc = jnp.einsum("ij,jyx->iyx", dz_rows, whole, precision=lax.Precision.HIGHEST)
+    dz_full = derivative_table(slab_z * group_count)
+    dz_blocks = jnp.asarray(dz_full.reshape(group_count, slab_z, group_count, slab_z))
+    place = lax.axis_index("grp")
+    dz_visc = 0.0
+    for turn in range(group_count):
+        slab = viscosity
+        if turn:
+            slab = lax.ppermute(
+                viscosity, "grp", [(i, (i + turn) % group_count) for i in range(group_count)]
+            )
+        owner = lax.rem(place - turn + group_count, group_count)
+        dz_visc += jnp.einsum(
+            "ij,jyx->iyx", dz_blocks[place, :, owner], slab, precision=lax.Precision.HIGHEST
+        )
     inverse = 1.0 / density
     cross = dz_visc * inverse
     first_add = cross * along_last(velocity[2], jnp.asarray(table_x))

time: 171 us -> 111 us (0.65)
  Pallas kernels: 71.4 us -> 5.48 us
  waiting for transfers between devices: 31.9 us -> 57.5 us
  between operations: 13.6 us -> 0.16 us
  starting transfers between devices: 43.5 us -> 35.9 us
  matrix products: 6.02 us -> 8.17 us
    pallas_call x2 -> x1, Pallas kernels: 66 us -> 0.14 us  [pack(): pl.pallas_call(functools.partial(pack_kernel, count, planes), out_shape=(...]
    ppermute x28, waiting for transfers between devices: 31.9 us -> 57.5 us  [exchange(): lax.ppermute(pieces[step], 'wide', [(i, i ^ step) for i in range(count)])]
    ppermute x28, starting transfers between devices: 43.5 us -> 34.3 us  [exchange(): lax.ppermute(pieces[step], 'wide', [(i, i ^ step) for i in range(count)])]
    dot_general x1 -> x4, matrix products: 3.89 us -> 6.05 us  [by_planes(): jnp.einsum('ij,jyx->iyx', dz_blocks[place, :, owner], slab, precision=lax...]
    add x1, other arithmetic: 1.92 us -> 0.09 us  [properties(): return (0.2 + 0.8 * heavy, 0.25 + 0.75 * heavy)]
  transfers between devices with their start and end apart: 29 -> 31, of which waited for: 10 -> 17; matrix products, arithmetic and copies ran while one was open for 4% -> 9% of each run, Pallas kernels for 41% -> 4%
where the time goes in v2:
time: 111 us
  waiting for transfers between devices  57.5 us (52%)
  starting transfers between devices  35.9 us (32%)
  matrix products  8.17 us (7%)
  Pallas kernels  5.48 us (5%)
  local copies, waits for them, and re-layouts  2.47 us (2%)
  other arithmetic  1.38 us (1%)
    ppermute x28, waiting for transfers between devices, exchange(): lax.ppermute(pieces[step], 'wide', [(i, i ^ step) for i in range(count)])  57.5 us
    ppermute x28, starting transfers between devices, exchange(): lax.ppermute(pieces[step], 'wide', [(i, i ^ step) for i in range(count)])  34.3 us
    dot_general x4, matrix products, by_planes(): jnp.einsum('ij,jyx->iyx', dz_blocks[place, :, owner], slab, precision=lax...  6.05 us
    pallas_call x2, Pallas kernels, on_plane(): pl.pallas_call(functools.partial(plane_kernel, count), out_shape=(piece,)...  3.93 us
    unnamed x12, local copies, waits for them, and re-layouts  2.47 us
  transfers between devices with their start and end apart: 31, of which 17 were waited for; matrix products, arithmetic and copies ran while one was open for 9% of the time, Pallas kernels for 4%

profile of v2, /device:TPU:8, one launch (start us, length us, event | category | flops | bytes accessed | tf_op | source)
XLA Modules:
  0.0 111.1 jit_solution(10572191853861985732)
XLA Ops:
  0.0 1.0 copy-done
  1.0 1.4 %copy-done.2 = f32[3,16,16,512]{3,2,1,0:T(8,128)S(1)} copy-done((f32[3,16,16,512]{3,2,1,0:T(8,128)S(1)}, f32[3,16,16,512]{3,2,1,0:T(8,128)}, u32[]{:S(2)}) %copy-start.2) | copy-done | bytes 1572888
  2.6 1.6 %collective-permute-start = (f32[4,16,512]{2,1,0:T(8,128)S(1)}, f32[4,16,512]{2,1,0:T(8,128)S(1)}, u32[]{:S(2)}, u32[]{:S(2)}) collective-permute-start(f32[4,16,512]{2,1,0:T(8,128)S(1)} %get-tuple-element.38), channel_id=1, source_target_pairs={{0,1},{1,0},{2,3},{3,2},{4,5},{5,4},{6,7},{7,6},{8,9},{9,8},{10,11... | collective-permute-start | bytes 393224 | tf_op jit(solution)/shard_map/ppermute | solution.py:167
  4.6 1.5 %collective-permute-start.2 = (f32[4,16,512]{2,1,0:T(8,128)S(1)}, f32[4,16,512]{2,1,0:T(8,128)S(1)}, u32[]{:S(2)}, u32[]{:S(2)}) collective-permute-start(f32[4,16,512]{2,1,0:T(8,128)S(1)} %get-tuple-element.40), channel_id=1, source_target_pairs={{0,3},{1,2},{2,1},{3,0},{4,7},{5,6},{6,5},{7,4},{8,11},{9,10},{10,... | collective-permute-start | bytes 393224 | tf_op jit(solution)/shard_map/ppermute | solution.py:167
  6.2 2.6 %collective-permute-start.3 = (f32[4,16,512]{2,1,0:T(8,128)S(1)}, f32[4,16,512]{2,1,0:T(8,128)S(1)}, u32[]{:S(2)}, u32[]{:S(2)}) collective-permute-start(f32[4,16,512]{2,1,0:T(8,128)S(1)} %get-tuple-element.41), channel_id=1, source_target_pairs={{0,4},{1,5},{2,6},{3,7},{4,0},{5,1},{6,2},{7,3},{8,12},{9,13},{10,... | collective-permute-start | bytes 393224 | tf_op jit(solution)/shard_map/ppermute | solution.py:167
  8.7 1.3 %collective-permute-start.4 = (f32[4,16,512]{2,1,0:T(8,128)S(1)}, f32[4,16,512]{2,1,0:T(8,128)S(1)}, u32[]{:S(2)}, u32[]{:S(2)}) collective-permute-start(f32[4,16,512]{2,1,0:T(8,128)S(1)} %get-tuple-element.42), channel_id=1, source_target_pairs={{0,5},{1,4},{2,7},{3,6},{4,1},{5,0},{6,3},{7,2},{8,13},{9,12},{10,... | collective-permute-start | bytes 393224 | tf_op jit(solution)/shard_map/ppermute | solution.py:167
  10.0 1.6 %collective-permute-start.5 = (f32[4,16,512]{2,1,0:T(8,128)S(1)}, f32[4,16,512]{2,1,0:T(8,128)S(1)}, u32[]{:S(2)}, u32[]{:S(2)}) collective-permute-start(f32[4,16,512]{2,1,0:T(8,128)S(1)} %get-tuple-element.43), channel_id=1, source_target_pairs={{0,6},{1,7},{2,4},{3,5},{4,2},{5,3},{6,0},{7,1},{8,14},{9,15},{10,... | collective-permute-start | bytes 393224 | tf_op jit(solution)/shard_map/ppermute | solution.py:167
  11.6 1.2 %collective-permute-done.1.refs_2_ = f32[4,16,512]{2,1,0:T(8,128)S(1)} collective-permute-done((f32[4,16,512]{2,1,0:T(8,128)S(1)}, f32[4,16,512]{2,1,0:T(8,128)S(1)}, u32[]{:S(2)}, u32[]{:S(2)}) %collective-permute-start.1) | collective-permute-done | bytes 131104 | tf_op jit(solution)/shard_map/ppermute | solution.py:167
  13.0 1.5 %collective-permute-done.2.refs_3_ = f32[4,16,512]{2,1,0:T(8,128)S(1)} collective-permute-done((f32[4,16,512]{2,1,0:T(8,128)S(1)}, f32[4,16,512]{2,1,0:T(8,128)S(1)}, u32[]{:S(2)}, u32[]{:S(2)}) %collective-permute-start.2) | collective-permute-done | bytes 131104 | tf_op jit(solution)/shard_map/ppermute | solution.py:167
  14.5 9.3 %collective-permute-done.3.refs_4_ = f32[4,16,512]{2,1,0:T(8,128)S(1)} collective-permute-done((f32[4,16,512]{2,1,0:T(8,128)S(1)}, f32[4,16,512]{2,1,0:T(8,128)S(1)}, u32[]{:S(2)}, u32[]{:S(2)}) %collective-permute-start.3) | collective-permute-done | bytes 131104 | tf_op jit(solution)/shard_map/ppermute | solution.py:167
  23.8 1.0 collective-permute-start.14
  24.8 1.8 %collective-permute-done.4.refs_5_ = f32[4,16,512]{2,1,0:T(8,128)S(1)} collective-permute-done((f32[4,16,512]{2,1,0:T(8,128)S(1)}, f32[4,16,512]{2,1,0:T(8,128)S(1)}, u32[]{:S(2)}, u32[]{:S(2)}) %collective-permute-start.4) | collective-permute-done | bytes 131104 | tf_op jit(solution)/shard_map/ppermute | solution.py:167
  26.6 2.1 %collective-permute-start.15 = (f32[4,16,512]{2,1,0:T(8,128)S(1)}, f32[4,16,512]{2,1,0:T(8,128)S(1)}, u32[]{:S(2)}, u32[]{:S(2)}) collective-permute-start(f32[4,16,512]{2,1,0:T(8,128)S(1)} %get-tuple-element.55), channel_id=1, source_target_pairs={{0,2},{1,3},{2,0},{3,1},{4,6},{5,7},{6,4},{7,5},{8,10},{9,11},{10,... | collective-permute-start | bytes 393224 | tf_op jit(solution)/shard_map/ppermute | solution.py:167
  28.6 0.5 collective-permute-done.5.refs_6_
  29.2 3.8 %collective-permute-done.6.refs_7_ = f32[4,16,512]{2,1,0:T(8,128)S(1)} collective-permute-done((f32[4,16,512]{2,1,0:T(8,128)S(1)}, f32[4,16,512]{2,1,0:T(8,128)S(1)}, u32[]{:S(2)}, u32[]{:S(2)}) %collective-permute-start.6) | collective-permute-done | bytes 131104 | tf_op jit(solution)/shard_map/ppermute | solution.py:167
  32.9 0.8 collective-permute-start.17
  33.8 1.5 %fusion.9 = f32[16,16,512]{2,0,1:T(8,128)S(1)} fusion(f32[16,16,512]{2,1,0:T(8,128)S(1)} %multiply_add_fusion, f32[4,16,4,16]{3,1,2,0:T(8,128)} %constant.52.clone, s32[]{:T(128)S(6)} %select_n.18, s32[]{:T(128)S(6)} %select_n.19), kind=kOutput, calls=%fused_computation.13 | convolution fusion | flops 25165824 | bytes 1056776 | tf_op jit(solution)/shard_map/ij,jyx->iyx/dot_general | solution.py:204
  35.3 1.6 %collective-permute-start.29 = (f32[16,16,512]{2,1,0:T(8,128)S(1)}, f32[16,16,512]{2,1,0:T(8,128)S(1)}, u32[]{:S(2)}, u32[]{:S(2)}) collective-permute-start(f32[16,16,512]{2,1,0:T(8,128)S(1)} %multiply_add_fusion), channel_id=1, source_target_pairs={{0,16},{8,24},{16,0},{24,8},{1,17},{9,25},{17,1},{25,9},{2,18},{10... | collective-permute-start | bytes 1572872 | tf_op jit(solution)/shard_map/ppermute | solution.py:200
  36.9 1.2 %collective-permute-start.18 = (f32[4,16,512]{2,1,0:T(8,128)S(1)}, f32[4,16,512]{2,1,0:T(8,128)S(1)}, u32[]{:S(2)}, u32[]{:S(2)}) collective-permute-start(f32[4,16,512]{2,1,0:T(8,128)S(1)} %get-tuple-element.58), channel_id=1, source_target_pairs={{0,5},{1,4},{2,7},{3,6},{4,1},{5,0},{6,3},{7,2},{8,13},{9,12},{10,... | collective-permute-start | bytes 393224 | tf_op jit(solution)/shard_map/ppermute | solution.py:167
  38.1 2.0 %collective-permute-start.19 = (f32[4,16,512]{2,1,0:T(8,128)S(1)}, f32[4,16,512]{2,1,0:T(8,128)S(1)}, u32[]{:S(2)}, u32[]{:S(2)}) collective-permute-start(f32[4,16,512]{2,1,0:T(8,128)S(1)} %get-tuple-element.59), channel_id=1, source_target_pairs={{0,6},{1,7},{2,4},{3,5},{4,2},{5,3},{6,0},{7,1},{8,14},{9,15},{10,... | collective-permute-start | bytes 393224 | tf_op jit(solution)/shard_map/ppermute | solution.py:167
  40.1 5.8 %collective-permute-done.17.refs_4_ = f32[4,16,512]{2,1,0:T(8,128)S(1)} collective-permute-done((f32[4,16,512]{2,1,0:T(8,128)S(1)}, f32[4,16,512]{2,1,0:T(8,128)S(1)}, u32[]{:S(2)}, u32[]{:S(2)}) %collective-permute-start.17) | collective-permute-done | bytes 131104 | tf_op jit(solution)/shard_map/ppermute | solution.py:167
  46.0 2.0 %plane.2 = (f32[4,16,512]{2,1,0:T(8,128)S(1)}, f32[4,16,512]{2,1,0:T(8,128)S(1)}, f32[4,16,512]{2,1,0:T(8,128)S(1)}, f32[4,16,512]{2,1,0:T(8,128)S(1)}, f32[4,16...) custom-call(bf16[1536,512]{1,0:T(8,128)(2,1)S(1)} %copy-done.3, ...), custom_call_target="tpu_custom_call" | custom-call | flops 1509949440 | bytes 2097152 | tf_op jit(solution)/shard_map/plane/pallas_call | solution.py:121
  47.9 0.8 collective-permute-done.18.refs_5_
  48.8 5.0 %collective-permute-done.19.refs_6_ = f32[4,16,512]{2,1,0:T(8,128)S(1)} collective-permute-done((f32[4,16,512]{2,1,0:T(8,128)S(1)}, f32[4,16,512]{2,1,0:T(8,128)S(1)}, u32[]{:S(2)}, u32[]{:S(2)}) %collective-permute-start.19) | collective-permute-done | bytes 131104 | tf_op jit(solution)/shard_map/ppermute | solution.py:167
  53.7 1.6 %collective-permute-done.20.refs_7_ = f32[4,16,512]{2,1,0:T(8,128)S(1)} collective-permute-done((f32[4,16,512]{2,1,0:T(8,128)S(1)}, f32[4,16,512]{2,1,0:T(8,128)S(1)}, u32[]{:S(2)}, u32[]{:S(2)}) %collective-permute-start.20) | collective-permute-done | bytes 131104 | tf_op jit(solution)/shard_map/ppermute | solution.py:167
  55.3 0.6 collective-permute-start.8
  55.9 2.0 %plane.3 = (f32[4,16,512]{2,1,0:T(8,128)S(1)}, f32[4,16,512]{2,1,0:T(8,128)S(1)}, f32[4,16,512]{2,1,0:T(8,128)S(1)}, f32[4,16,512]{2,1,0:T(8,128)S(1)}, f32[4,16...) custom-call(bf16[1536,512]{1,0:T(8,128)(2,1)S(1)} %copy-done.3, ...), custom_call_target="tpu_custom_call" | custom-call | flops 1509949440 | bytes 2097152 | tf_op jit(solution)/shard_map/plane/pallas_call | solution.py:121
  57.9 3.3 %collective-permute-start.9 = (f32[4,16,512]{2,1,0:T(8,128)S(1)}, f32[4,16,512]{2,1,0:T(8,128)S(1)}, u32[]{:S(2)}, u32[]{:S(2)}) collective-permute-start(f32[4,16,512]{2,1,0:T(8,128)S(1)} %get-tuple-element.48), channel_id=1, source_target_pairs={{0,3},{1,2},{2,1},{3,0},{4,7},{5,6},{6,5},{7,4},{8,11},{9,10},{10,... | collective-permute-start | bytes 393224 | tf_op jit(solution)/shard_map/ppermute | solution.py:167
  61.2 1.5 %fusion.3 = f32[16,16,512]{2,0,1:T(8,128)S(1)} fusion(f32[16,16,512]{2,1,0:T(8,128)S(1)} %collective-permute-done.30, f32[4,16,4,16]{3,1,2,0:T(8,128)} %constant.52.clone, s32[]{:T(128)S(6)} %select_n.18, s32[]{:T(128)S(6)} %select_n.22), kind=kOutput, calls=%fused_computation.5 | convolution fusion | flops 25165824 | bytes 1056776 | tf_op jit(solution)/shard_map/ij,jyx->iyx/dot_general | solution.py:204
  62.8 0.8 collective-permute-start.10
  63.6 1.5 %fusion.5 = f32[16,16,512]{2,0,1:T(8,128)S(1)} fusion(f32[16,16,512]{2,1,0:T(8,128)S(1)} %collective-permute-done.29, f32[4,16,4,16]{3,1,2,0:T(8,128)} %constant.52.clone, s32[]{:T(128)S(6)} %select_n.18, s32[]{:T(128)S(6)} %select_n.21), kind=kOutput, calls=%fused_computation.8 | convolution fusion | flops 25165824 | bytes 1056776 | tf_op jit(solution)/shard_map/ij,jyx->iyx/dot_general | solution.py:204
  65.1 1.3 %collective-permute-start.11 = (f32[4,16,512]{2,1,0:T(8,128)S(1)}, f32[4,16,512]{2,1,0:T(8,128)S(1)}, u32[]{:S(2)}, u32[]{:S(2)}) collective-permute-start(f32[4,16,512]{2,1,0:T(8,128)S(1)} %get-tuple-element.50), channel_id=1, source_target_pairs={{0,5},{1,4},{2,7},{3,6},{4,1},{5,0},{6,3},{7,2},{8,13},{9,12},{10,... | collective-permute-start | bytes 393224 | tf_op jit(solution)/shard_map/ppermute | solution.py:167
  66.4 1.5 %fusion.7 = f32[16,16,512]{2,0,1:T(8,128)S(1)} fusion(f32[16,16,512]{2,1,0:T(8,128)S(1)} %collective-permute-done.28, f32[4,16,4,16]{3,1,2,0:T(8,128)} %constant.52.clone, s32[]{:T(128)S(6)} %select_n.18, s32[]{:T(128)S(6)} %select_n.20), kind=kOutput, calls=%fused_computation.11 | convolution fusion | flops 25165824 | bytes 1056776 | tf_op jit(solution)/shard_map/ij,jyx->iyx/dot_general | solution.py:204
  67.9 2.2 %collective-permute-start.12 = (f32[4,16,512]{2,1,0:T(8,128)S(1)}, f32[4,16,512]{2,1,0:T(8,128)S(1)}, u32[]{:S(2)}, u32[]{:S(2)}) collective-permute-start(f32[4,16,512]{2,1,0:T(8,128)S(1)} %get-tuple-element.51), channel_id=1, source_target_pairs={{0,6},{1,7},{2,4},{3,5},{4,2},{5,3},{6,0},{7,1},{8,14},{9,15},{10,... | collective-permute-start | bytes 393224 | tf_op jit(solution)/shard_map/ppermute | solution.py:167
  70.2 1.7 %collective-permute-start.13 = (f32[4,16,512]{2,1,0:T(8,128)S(1)}, f32[4,16,512]{2,1,0:T(8,128)S(1)}, u32[]{:S(2)}, u32[]{:S(2)}) collective-permute-start(f32[4,16,512]{2,1,0:T(8,128)S(1)} %get-tuple-element.52), channel_id=1, source_target_pairs={{0,7},{1,6},{2,5},{3,4},{4,3},{5,2},{6,1},{7,0},{8,15},{9,14},{10,... | collective-permute-start | bytes 393224 | tf_op jit(solution)/shard_map/ppermute | solution.py:167
  71.9 6.1 %collective-permute-done.10.refs_4_ = f32[4,16,512]{2,1,0:T(8,128)S(1)} collective-permute-done((f32[4,16,512]{2,1,0:T(8,128)S(1)}, f32[4,16,512]{2,1,0:T(8,128)S(1)}, u32[]{:S(2)}, u32[]{:S(2)}) %collective-permute-start.10) | collective-permute-done | bytes 131104 | tf_op jit(solution)/shard_map/ppermute | solution.py:167
  78.0 3.0 %collective-permute-start.22 = (f32[4,16,512]{2,1,0:T(8,128)S(1)}, f32[4,16,512]{2,1,0:T(8,128)S(1)}, u32[]{:S(2)}, u32[]{:S(2)}) collective-permute-start(f32[4,16,512]{2,1,0:T(8,128)S(1)} %get-tuple-element.63), channel_id=1, source_target_pairs={{0,2},{1,3},{2,0},{3,1},{4,6},{5,7},{6,4},{7,5},{8,10},{9,11},{10,... | collective-permute-start | bytes 393224 | tf_op jit(solution)/shard_map/ppermute | solution.py:167
  81.0 1.3 %fusion.2 = (f32[16,16,512]{2,1,0:T(8,128)S(1)}, f32[16,16,512]{2,1,0:T(8,128)S(1)}) fusion(f32[16,16,512]{2,0,1:T(8,128)S(1)} %fusion.3, f32[16,16,512]{2,0,1:T(8,128)S(1)} %fusion.5, f32[16,16,512]{2,0,1:T(8,128)S(1)} %fusion.7, f32[16,16,512]{2,0,1:T(8,128)S(1)} %fusion.9, f32[16,16,512]{2,1,0:T(8,128)S(1)} %copy-done.1), kind=kLoop, calls=%fused_computation.4 | loop fusion | flops 1048576 | bytes 3670016 | tf_op jit(solution)/shard_map/mul | solution.py:208
  82.3 2.3 %collective-permute-start.23 = (f32[4,16,512]{2,1,0:T(8,128)S(1)}, f32[4,16,512]{2,1,0:T(8,128)S(1)}, u32[]{:S(2)}, u32[]{:S(2)}) collective-permute-start(f32[4,16,512]{2,1,0:T(8,128)S(1)} %get-tuple-element.64), channel_id=1, source_target_pairs={{0,3},{1,2},{2,1},{3,0},{4,7},{5,6},{6,5},{7,4},{8,11},{9,10},{10,... | collective-permute-start | bytes 393224 | tf_op jit(solution)/shard_map/ppermute | solution.py:167
  85.1 4.4 %collective-permute-done.13.refs_7_ = f32[4,16,512]{2,1,0:T(8,128)S(1)} collective-permute-done((f32[4,16,512]{2,1,0:T(8,128)S(1)}, f32[4,16,512]{2,1,0:T(8,128)S(1)}, u32[]{:S(2)}, u32[]{:S(2)}) %collective-permute-start.13) | collective-permute-done | bytes 131104 | tf_op jit(solution)/shard_map/ppermute | solution.py:167
  89.5 1.1 %collective-permute-start.26 = (f32[4,16,512]{2,1,0:T(8,128)S(1)}, f32[4,16,512]{2,1,0:T(8,128)S(1)}, u32[]{:S(2)}, u32[]{:S(2)}) collective-permute-start(f32[4,16,512]{2,1,0:T(8,128)S(1)} %get-tuple-element.67), channel_id=1, source_target_pairs={{0,6},{1,7},{2,4},{3,5},{4,2},{5,3},{6,0},{7,1},{8,14},{9,15},{10,... | collective-permute-start | bytes 393224 | tf_op jit(solution)/shard_map/ppermute | solution.py:167
  90.7 1.6 %collective-permute-start.27 = (f32[4,16,512]{2,1,0:T(8,128)S(1)}, f32[4,16,512]{2,1,0:T(8,128)S(1)}, u32[]{:S(2)}, u32[]{:S(2)}) collective-permute-start(f32[4,16,512]{2,1,0:T(8,128)S(1)} %get-tuple-element.68), channel_id=1, source_target_pairs={{0,7},{1,6},{2,5},{3,4},{4,3},{5,2},{6,1},{7,0},{8,15},{9,14},{10,... | collective-permute-start | bytes 393224 | tf_op jit(solution)/shard_map/ppermute | solution.py:167
  92.3 2.1 %fusion.refs_17_ = f32[16,16,512]{2,1,0:T(8,128)S(1)} fusion(f32[16,16,512]{2,1,0:T(8,128)S(1)} %get-tuple-element.69.refs_18_, f32[512,512,1]{1,0,2:T(8,128)S(1)} %copy-done.5, f32[3,16,16,512]{3,2,1,0:T(8,128)} %velocity.1), kind=kOutput, calls=%fused_computation.1 | convolution fusion | flops 805437440 | bytes 2621440 | tf_op jit(solution)/shard_map/dot_general | solution.py:32
  94.4 6.2 %collective-permute-done.24.refs_12_ = f32[4,16,512]{2,1,0:T(8,128)S(1)} collective-permute-done((f32[4,16,512]{2,1,0:T(8,128)S(1)}, f32[4,16,512]{2,1,0:T(8,128)S(1)}, u32[]{:S(2)}, u32[]{:S(2)}) %collective-permute-start.24) | collective-permute-done | bytes 131104 | tf_op jit(solution)/shard_map/ppermute | solution.py:167
  100.6 2.8 %collective-permute-done.25.refs_13_ = f32[4,16,512]{2,1,0:T(8,128)S(1)} collective-permute-done((f32[4,16,512]{2,1,0:T(8,128)S(1)}, f32[4,16,512]{2,1,0:T(8,128)S(1)}, u32[]{:S(2)}, u32[]{:S(2)}) %collective-permute-start.25) | collective-permute-done | bytes 131104 | tf_op jit(solution)/shard_map/ppermute | solution.py:167
  103.4 4.2 %collective-permute-done.26.refs_14_ = f32[4,16,512]{2,1,0:T(8,128)S(1)} collective-permute-done((f32[4,16,512]{2,1,0:T(8,128)S(1)}, f32[4,16,512]{2,1,0:T(8,128)S(1)}, u32[]{:S(2)}, u32[]{:S(2)}) %collective-permute-start.26) | collective-permute-done | bytes 131104 | tf_op jit(solution)/shard_map/ppermute | solution.py:167
  107.6 2.1 %collective-permute-done.27.refs_15_ = f32[4,16,512]{2,1,0:T(8,128)S(1)} collective-permute-done((f32[4,16,512]{2,1,0:T(8,128)S(1)}, f32[4,16,512]{2,1,0:T(8,128)S(1)}, u32[]{:S(2)}, u32[]{:S(2)}) %collective-permute-start.27) | collective-permute-done | bytes 131104 | tf_op jit(solution)/shard_map/ppermute | solution.py:167
  109.7 1.4 %join.1 = f32[3,16,16,512]{3,2,1,0:T(8,128)} custom-call(f32[4,16,512]{2,1,0:T(8,128)S(1)} %get-tuple-element.45.refs_0_, f32[4,16,512]{2,1,0:T(8,128)S(1)} %collective-permute-done.7.refs_1_, f32[4,16,512]{2,1,0:T(8,128)S(1)} %collective-permute-done.8.refs_2_, f32[4,16,512]{2,1,0:T(8,128)S(1)} %collective-permute-done.9.refs_3_, ...), custom_call_target="tpu_custom_call" | custom-call | tf_op jit(solution)/shard_map/join/pallas_call | solution.py:153
  (37 shorter events, 1.2 us)
Async XLA Ops:
  0.0 1.0 copy-start
  1.0 1.4 %copy-start.2 = (f32[3,16,16,512]{3,2,1,0:T(8,128)S(1)}, f32[3,16,16,512]{3,2,1,0:T(8,128)}, u32[]{:S(2)}) copy-start(f32[3,16,16,512]{3,2,1,0:T(8,128)} %velocity.1) | copy-start | bytes 4718596
  2.5 10.4 %copy-start.1 = (f32[16,16,512]{2,1,0:T(8,128)S(1)}, f32[16,16,512]{2,1,0:T(8,128)}, u32[]{:S(2)}) copy-start(f32[16,16,512]{2,1,0:T(8,128)} %level_set.1) | copy-start | bytes 1572868
  2.6 43.4 %copy-start.4 = (bf16[128,384]{1,0:T(8,128)(2,1)S(1)}, bf16[128,384]{1,0:T(8,128)(2,1)}, u32[]{:S(2)}) copy-start(bf16[128,384]{1,0:T(8,128)(2,1)} %constant.51.clone.dy) | copy-start | bytes 294916
  2.6 7.4 %collective-permute-start = (f32[4,16,512]{2,1,0:T(8,128)S(1)}, f32[4,16,512]{2,1,0:T(8,128)S(1)}, u32[]{:S(2)}, u32[]{:S(2)}) collective-permute-start(f32[4,16,512]{2,1,0:T(8,128)S(1)} %get-tuple-element.38), channel_id=1, source_target_pairs={{0,1},{1,0},{2,3},{3,2},{4,5},{5,4},{6,7},{7,6},{8,9},{9,8},{10,11... | collective-permute-start | bytes 393224 | tf_op jit(solution)/shard_map/ppermute | solution.py:167
  4.2 8.7 %collective-permute-start.1 = (f32[4,16,512]{2,1,0:T(8,128)S(1)}, f32[4,16,512]{2,1,0:T(8,128)S(1)}, u32[]{:S(2)}, u32[]{:S(2)}) collective-permute-start(f32[4,16,512]{2,1,0:T(8,128)S(1)} %get-tuple-element.39), channel_id=1, source_target_pairs={{0,2},{1,3},{2,0},{3,1},{4,6},{5,7},{6,4},{7,5},{8,10},{9,11},{10,... | collective-permute-start | bytes 393224 | tf_op jit(solution)/shard_map/ppermute | solution.py:167
  4.6 9.8 %collective-permute-start.2 = (f32[4,16,512]{2,1,0:T(8,128)S(1)}, f32[4,16,512]{2,1,0:T(8,128)S(1)}, u32[]{:S(2)}, u32[]{:S(2)}) collective-permute-start(f32[4,16,512]{2,1,0:T(8,128)S(1)} %get-tuple-element.40), channel_id=1, source_target_pairs={{0,3},{1,2},{2,1},{3,0},{4,7},{5,6},{6,5},{7,4},{8,11},{9,10},{10,... | collective-permute-start | bytes 393224 | tf_op jit(solution)/shard_map/ppermute | solution.py:167
  6.2 17.6 %collective-permute-start.3 = (f32[4,16,512]{2,1,0:T(8,128)S(1)}, f32[4,16,512]{2,1,0:T(8,128)S(1)}, u32[]{:S(2)}, u32[]{:S(2)}) collective-permute-start(f32[4,16,512]{2,1,0:T(8,128)S(1)} %get-tuple-element.41), channel_id=1, source_target_pairs={{0,4},{1,5},{2,6},{3,7},{4,0},{5,1},{6,2},{7,3},{8,12},{9,13},{10,... | collective-permute-start | bytes 393224 | tf_op jit(solution)/shard_map/ppermute | solution.py:167
  8.7 17.8 %collective-permute-start.4 = (f32[4,16,512]{2,1,0:T(8,128)S(1)}, f32[4,16,512]{2,1,0:T(8,128)S(1)}, u32[]{:S(2)}, u32[]{:S(2)}) collective-permute-start(f32[4,16,512]{2,1,0:T(8,128)S(1)} %get-tuple-element.42), channel_id=1, source_target_pairs={{0,5},{1,4},{2,7},{3,6},{4,1},{5,0},{6,3},{7,2},{8,13},{9,12},{10,... | collective-permute-start | bytes 393224 | tf_op jit(solution)/shard_map/ppermute | solution.py:167
  10.0 35.9 %copy-start.3 = (bf16[1536,512]{1,0:T(8,128)(2,1)S(1)}, bf16[1536,512]{1,0:T(8,128)(2,1)}, u32[]{:S(2)}) copy-start(bf16[1536,512]{1,0:T(8,128)(2,1)} %constant.50.clone.dx) | copy-start | bytes 4718596
  10.0 19.1 %collective-permute-start.5 = (f32[4,16,512]{2,1,0:T(8,128)S(1)}, f32[4,16,512]{2,1,0:T(8,128)S(1)}, u32[]{:S(2)}, u32[]{:S(2)}) collective-permute-start(f32[4,16,512]{2,1,0:T(8,128)S(1)} %get-tuple-element.43), channel_id=1, source_target_pairs={{0,6},{1,7},{2,4},{3,5},{4,2},{5,3},{6,0},{7,1},{8,14},{9,15},{10,... | collective-permute-start | bytes 393224 | tf_op jit(solution)/shard_map/ppermute | solution.py:167
  12.9 20.1 %collective-permute-start.6 = (f32[4,16,512]{2,1,0:T(8,128)S(1)}, f32[4,16,512]{2,1,0:T(8,128)S(1)}, u32[]{:S(2)}, u32[]{:S(2)}) collective-permute-start(f32[4,16,512]{2,1,0:T(8,128)S(1)} %get-tuple-element.44), channel_id=1, source_target_pairs={{0,7},{1,6},{2,5},{3,4},{4,3},{5,2},{6,1},{7,0},{8,15},{9,14},{10,... | collective-permute-start | bytes 393224 | tf_op jit(solution)/shard_map/ppermute | solution.py:167
  14.5 43.4 %collective-permute-start.30 = (f32[16,16,512]{2,1,0:T(8,128)S(1)}, f32[16,16,512]{2,1,0:T(8,128)S(1)}, u32[]{:S(2)}, u32[]{:S(2)}) collective-permute-start(f32[16,16,512]{2,1,0:T(8,128)S(1)} %multiply_add_fusion), channel_id=1, source_target_pairs={{0,24},{8,0},{16,8},{24,16},{1,25},{9,1},{17,9},{25,17},{2,26},{10... | collective-permute-start | bytes 1572872 | tf_op jit(solution)/shard_map/ppermute | solution.py:200
  23.8 11.5 %collective-permute-start.14 = (f32[4,16,512]{2,1,0:T(8,128)S(1)}, f32[4,16,512]{2,1,0:T(8,128)S(1)}, u32[]{:S(2)}, u32[]{:S(2)}) collective-permute-start(f32[4,16,512]{2,1,0:T(8,128)S(1)} %get-tuple-element.54), channel_id=1, source_target_pairs={{0,1},{1,0},{2,3},{3,2},{4,5},{5,4},{6,7},{7,6},{8,9},{9,8},{10,11... | collective-permute-start | bytes 393224 | tf_op jit(solution)/shard_map/ppermute | solution.py:167
  26.6 10.3 %collective-permute-start.15 = (f32[4,16,512]{2,1,0:T(8,128)S(1)}, f32[4,16,512]{2,1,0:T(8,128)S(1)}, u32[]{:S(2)}, u32[]{:S(2)}) collective-permute-start(f32[4,16,512]{2,1,0:T(8,128)S(1)} %get-tuple-element.55), channel_id=1, source_target_pairs={{0,2},{1,3},{2,0},{3,1},{4,6},{5,7},{6,4},{7,5},{8,10},{9,11},{10,... | collective-permute-start | bytes 393224 | tf_op jit(solution)/shard_map/ppermute | solution.py:167
  29.2 8.9 %collective-permute-start.16 = (f32[4,16,512]{2,1,0:T(8,128)S(1)}, f32[4,16,512]{2,1,0:T(8,128)S(1)}, u32[]{:S(2)}, u32[]{:S(2)}) collective-permute-start(f32[4,16,512]{2,1,0:T(8,128)S(1)} %get-tuple-element.56), channel_id=1, source_target_pairs={{0,3},{1,2},{2,1},{3,0},{4,7},{5,6},{6,5},{7,4},{8,11},{9,10},{10,... | collective-permute-start | bytes 393224 | tf_op jit(solution)/shard_map/ppermute | solution.py:167
  32.9 13.0 %collective-permute-start.17 = (f32[4,16,512]{2,1,0:T(8,128)S(1)}, f32[4,16,512]{2,1,0:T(8,128)S(1)}, u32[]{:S(2)}, u32[]{:S(2)}) collective-permute-start(f32[4,16,512]{2,1,0:T(8,128)S(1)} %get-tuple-element.57), channel_id=1, source_target_pairs={{0,4},{1,5},{2,6},{3,7},{4,0},{5,1},{6,2},{7,3},{8,12},{9,13},{10,... | collective-permute-start | bytes 393224 | tf_op jit(solution)/shard_map/ppermute | solution.py:167
  35.3 27.5 %collective-permute-start.29 = (f32[16,16,512]{2,1,0:T(8,128)S(1)}, f32[16,16,512]{2,1,0:T(8,128)S(1)}, u32[]{:S(2)}, u32[]{:S(2)}) collective-permute-start(f32[16,16,512]{2,1,0:T(8,128)S(1)} %multiply_add_fusion), channel_id=1, source_target_pairs={{0,16},{8,24},{16,0},{24,8},{1,17},{9,25},{17,1},{25,9},{2,18},{10... | collective-permute-start | bytes 1572872 | tf_op jit(solution)/shard_map/ppermute | solution.py:200
  36.9 11.9 %collective-permute-start.18 = (f32[4,16,512]{2,1,0:T(8,128)S(1)}, f32[4,16,512]{2,1,0:T(8,128)S(1)}, u32[]{:S(2)}, u32[]{:S(2)}) collective-permute-start(f32[4,16,512]{2,1,0:T(8,128)S(1)} %get-tuple-element.58), channel_id=1, source_target_pairs={{0,5},{1,4},{2,7},{3,6},{4,1},{5,0},{6,3},{7,2},{8,13},{9,12},{10,... | collective-permute-start | bytes 393224 | tf_op jit(solution)/shard_map/ppermute | solution.py:167
  38.1 15.6 %collective-permute-start.19 = (f32[4,16,512]{2,1,0:T(8,128)S(1)}, f32[4,16,512]{2,1,0:T(8,128)S(1)}, u32[]{:S(2)}, u32[]{:S(2)}) collective-permute-start(f32[4,16,512]{2,1,0:T(8,128)S(1)} %get-tuple-element.59), channel_id=1, source_target_pairs={{0,6},{1,7},{2,4},{3,5},{4,2},{5,3},{6,0},{7,1},{8,14},{9,15},{10,... | collective-permute-start | bytes 393224 | tf_op jit(solution)/shard_map/ppermute | solution.py:167
  46.0 9.4 %collective-permute-start.20 = (f32[4,16,512]{2,1,0:T(8,128)S(1)}, f32[4,16,512]{2,1,0:T(8,128)S(1)}, u32[]{:S(2)}, u32[]{:S(2)}) collective-permute-start(f32[4,16,512]{2,1,0:T(8,128)S(1)} %get-tuple-element.60), channel_id=1, source_target_pairs={{0,7},{1,6},{2,5},{3,4},{4,3},{5,2},{6,1},{7,0},{8,15},{9,14},{10,... | collective-permute-start | bytes 393224 | tf_op jit(solution)/shard_map/ppermute | solution.py:167
  48.8 16.4 %collective-permute-start.28 = (f32[16,16,512]{2,1,0:T(8,128)S(1)}, f32[16,16,512]{2,1,0:T(8,128)S(1)}, u32[]{:S(2)}, u32[]{:S(2)}) collective-permute-start(f32[16,16,512]{2,1,0:T(8,128)S(1)} %multiply_add_fusion), channel_id=1, source_target_pairs={{0,8},{8,16},{16,24},{24,0},{1,9},{9,17},{17,25},{25,1},{2,10},{10... | collective-permute-start | bytes 1572872 | tf_op jit(solution)/shard_map/ppermute | solution.py:200
  53.7 14.2 %collective-permute-start.7 = (f32[4,16,512]{2,1,0:T(8,128)S(1)}, f32[4,16,512]{2,1,0:T(8,128)S(1)}, u32[]{:S(2)}, u32[]{:S(2)}) collective-permute-start(f32[4,16,512]{2,1,0:T(8,128)S(1)} %get-tuple-element.46), channel_id=1, source_target_pairs={{0,1},{1,0},{2,3},{3,2},{4,5},{5,4},{6,7},{7,6},{8,9},{9,8},{10,11... | collective-permute-start | bytes 393224 | tf_op jit(solution)/shard_map/ppermute | solution.py:167
  55.3 14.8 %collective-permute-start.8 = (f32[4,16,512]{2,1,0:T(8,128)S(1)}, f32[4,16,512]{2,1,0:T(8,128)S(1)}, u32[]{:S(2)}, u32[]{:S(2)}) collective-permute-start(f32[4,16,512]{2,1,0:T(8,128)S(1)} %get-tuple-element.47), channel_id=1, source_target_pairs={{0,2},{1,3},{2,0},{3,1},{4,6},{5,7},{6,4},{7,5},{8,10},{9,11},{10,... | collective-permute-start | bytes 393224 | tf_op jit(solution)/shard_map/ppermute | solution.py:167
  57.9 14.0 %collective-permute-start.9 = (f32[4,16,512]{2,1,0:T(8,128)S(1)}, f32[4,16,512]{2,1,0:T(8,128)S(1)}, u32[]{:S(2)}, u32[]{:S(2)}) collective-permute-start(f32[4,16,512]{2,1,0:T(8,128)S(1)} %get-tuple-element.48), channel_id=1, source_target_pairs={{0,3},{1,2},{2,1},{3,0},{4,7},{5,6},{6,5},{7,4},{8,11},{9,10},{10,... | collective-permute-start | bytes 393224 | tf_op jit(solution)/shard_map/ppermute | solution.py:167
  62.8 15.2 %collective-permute-start.10 = (f32[4,16,512]{2,1,0:T(8,128)S(1)}, f32[4,16,512]{2,1,0:T(8,128)S(1)}, u32[]{:S(2)}, u32[]{:S(2)}) collective-permute-start(f32[4,16,512]{2,1,0:T(8,128)S(1)} %get-tuple-element.49), channel_id=1, source_target_pairs={{0,4},{1,5},{2,6},{3,7},{4,0},{5,1},{6,2},{7,3},{8,12},{9,13},{10,... | collective-permute-start | bytes 393224 | tf_op jit(solution)/shard_map/ppermute | solution.py:167
  65.1 17.2 %collective-permute-start.11 = (f32[4,16,512]{2,1,0:T(8,128)S(1)}, f32[4,16,512]{2,1,0:T(8,128)S(1)}, u32[]{:S(2)}, u32[]{:S(2)}) collective-permute-start(f32[4,16,512]{2,1,0:T(8,128)S(1)} %get-tuple-element.50), channel_id=1, source_target_pairs={{0,5},{1,4},{2,7},{3,6},{4,1},{5,0},{6,3},{7,2},{8,13},{9,12},{10,... | collective-permute-start | bytes 393224 | tf_op jit(solution)/shard_map/ppermute | solution.py:167
  67.9 17.2 %collective-permute-start.12 = (f32[4,16,512]{2,1,0:T(8,128)S(1)}, f32[4,16,512]{2,1,0:T(8,128)S(1)}, u32[]{:S(2)}, u32[]{:S(2)}) collective-permute-start(f32[4,16,512]{2,1,0:T(8,128)S(1)} %get-tuple-element.51), channel_id=1, source_target_pairs={{0,6},{1,7},{2,4},{3,5},{4,2},{5,3},{6,0},{7,1},{8,14},{9,15},{10,... | collective-permute-start | bytes 393224 | tf_op jit(solution)/shard_map/ppermute | solution.py:167
  70.2 19.3 %collective-permute-start.13 = (f32[4,16,512]{2,1,0:T(8,128)S(1)}, f32[4,16,512]{2,1,0:T(8,128)S(1)}, u32[]{:S(2)}, u32[]{:S(2)}) collective-permute-start(f32[4,16,512]{2,1,0:T(8,128)S(1)} %get-tuple-element.52), channel_id=1, source_target_pairs={{0,7},{1,6},{2,5},{3,4},{4,3},{5,2},{6,1},{7,0},{8,15},{9,14},{10,... | collective-permute-start | bytes 393224 | tf_op jit(solution)/shard_map/ppermute | solution.py:167
  71.9 17.6 %collective-permute-start.21 = (f32[4,16,512]{2,1,0:T(8,128)S(1)}, f32[4,16,512]{2,1,0:T(8,128)S(1)}, u32[]{:S(2)}, u32[]{:S(2)}) collective-permute-start(f32[4,16,512]{2,1,0:T(8,128)S(1)} %get-tuple-element.62), channel_id=1, source_target_pairs={{0,1},{1,0},{2,3},{3,2},{4,5},{5,4},{6,7},{7,6},{8,9},{9,8},{10,11... | collective-permute-start | bytes 393224 | tf_op jit(solution)/shard_map/ppermute | solution.py:167
  78.0 14.3 %copy-start.5 = (f32[512,512,1]{1,0,2:T(8,128)S(1)}, f32[512,512,1]{1,0,2:T(8,128)}, u32[]{:S(2)}) copy-start(f32[512,512,1]{1,0,2:T(8,128)} %constant.54) | copy-start | bytes 3145732
  78.0 12.7 %collective-permute-start.22 = (f32[4,16,512]{2,1,0:T(8,128)S(1)}, f32[4,16,512]{2,1,0:T(8,128)S(1)}, u32[]{:S(2)}, u32[]{:S(2)}) collective-permute-start(f32[4,16,512]{2,1,0:T(8,128)S(1)} %get-tuple-element.63), channel_id=1, source_target_pairs={{0,2},{1,3},{2,0},{3,1},{4,6},{5,7},{6,4},{7,5},{8,10},{9,11},{10,... | collective-permute-start | bytes 393224 | tf_op jit(solution)/shard_map/ppermute | solution.py:167
  82.3 12.1 %collective-permute-start.23 = (f32[4,16,512]{2,1,0:T(8,128)S(1)}, f32[4,16,512]{2,1,0:T(8,128)S(1)}, u32[]{:S(2)}, u32[]{:S(2)}) collective-permute-start(f32[4,16,512]{2,1,0:T(8,128)S(1)} %get-tuple-element.64), channel_id=1, source_target_pairs={{0,3},{1,2},{2,1},{3,0},{4,7},{5,6},{6,5},{7,4},{8,11},{9,10},{10,... | collective-permute-start | bytes 393224 | tf_op jit(solution)/shard_map/ppermute | solution.py:167
  85.1 15.5 %collective-permute-start.24 = (f32[4,16,512]{2,1,0:T(8,128)S(1)}, f32[4,16,512]{2,1,0:T(8,128)S(1)}, u32[]{:S(2)}, u32[]{:S(2)}) collective-permute-start(f32[4,16,512]{2,1,0:T(8,128)S(1)} %get-tuple-element.65), channel_id=1, source_target_pairs={{0,4},{1,5},{2,6},{3,7},{4,0},{5,1},{6,2},{7,3},{8,12},{9,13},{10,... | collective-permute-start | bytes 393224 | tf_op jit(solution)/shard_map/ppermute | solution.py:167
  89.5 13.9 %collective-permute-start.25 = (f32[4,16,512]{2,1,0:T(8,128)S(1)}, f32[4,16,512]{2,1,0:T(8,128)S(1)}, u32[]{:S(2)}, u32[]{:S(2)}) collective-permute-start(f32[4,16,512]{2,1,0:T(8,128)S(1)} %get-tuple-element.66), channel_id=1, source_target_pairs={{0,5},{1,4},{2,7},{3,6},{4,1},{5,0},{6,3},{7,2},{8,13},{9,12},{10,... | collective-permute-start | bytes 393224 | tf_op jit(solution)/shard_map/ppermute | solution.py:167
  89.5 18.1 %collective-permute-start.26 = (f32[4,16,512]{2,1,0:T(8,128)S(1)}, f32[4,16,512]{2,1,0:T(8,128)S(1)}, u32[]{:S(2)}, u32[]{:S(2)}) collective-permute-start(f32[4,16,512]{2,1,0:T(8,128)S(1)} %get-tuple-element.67), channel_id=1, source_target_pairs={{0,6},{1,7},{2,4},{3,5},{4,2},{5,3},{6,0},{7,1},{8,14},{9,15},{10,... | collective-permute-start | bytes 393224 | tf_op jit(solution)/shard_map/ppermute | solution.py:167
  90.7 19.0 %collective-permute-start.27 = (f32[4,16,512]{2,1,0:T(8,128)S(1)}, f32[4,16,512]{2,1,0:T(8,128)S(1)}, u32[]{:S(2)}, u32[]{:S(2)}) collective-permute-start(f32[4,16,512]{2,1,0:T(8,128)S(1)} %get-tuple-element.68), channel_id=1, source_target_pairs={{0,7},{1,6},{2,5},{3,4},{4,3},{5,2},{6,1},{7,0},{8,15},{9,14},{10,... | collective-permute-start | bytes 393224 | tf_op jit(solution)/shard_map/ppermute | solution.py:167

commit v3 on v1

--- a/solution.py
+++ b/solution.py
@@ -9,7 +9,10 @@
 from jax.sharding import PartitionSpec as P
 
 interface_width = 1.0
-vmem_bytes = 40 * 1024 * 1024
+flight = 5
+mebibyte = 1024 * 1024
+no_cost = pl.CostEstimate(flops=0, transcendentals=0, bytes_accessed=0)
+small_cost = pl.CostEstimate(flops=10_000_000, transcendentals=0, bytes_accessed=0)
 
 
 def derivative_table(count):
@@ -37,38 +40,36 @@
     return (0.2 + 0.8 * heavy, 0.25 + 0.75 * heavy)
 
 
-def pack_kernel(count, planes, chunk, velocity, level_set, *refs):
-    outs, sems = refs[:count], refs[count]
+def pack_kernel(steps, planes, velocity, level_set, *refs):
+    outs, sems = refs[-1 - len(steps) : -1], refs[-1]
     me = lax.axis_index("wide")
     copies = []
-    for step in range(count):
+    for i, (out, (chunk, step)) in enumerate(zip(outs, steps)):
         plane = (me ^ step) * planes + chunk
-        copies.append(
-            pltpu.make_async_copy(velocity.at[:, plane], outs[step].at[0:3], sems.at[step, 0])
-        )
-        copies.append(
-            pltpu.make_async_copy(level_set.at[plane], outs[step].at[3], sems.at[step, 1])
-        )
+        copies += [
+            pltpu.make_async_copy(velocity.at[:, plane], out.at[0:3], sems.at[i, 0]),
+            pltpu.make_async_copy(level_set.at[plane], out.at[3], sems.at[i, 1]),
+        ]
     for copy in copies:
         copy.start()
     for copy in copies:
         copy.wait()
 
 
-def pack(velocity, level_set, count, planes, chunk):
+def pack(velocity, level_set, steps, planes, after=()):
     rows, cells = level_set.shape[1:]
-    piece = jax.ShapeDtypeStruct((4, rows, cells), jnp.float32)
-    return pl.pallas_call(
-        functools.partial(pack_kernel, count, planes, chunk),
-        out_shape=(piece,) * count,
-        in_specs=[pl.BlockSpec(memory_space=pl.ANY)] * 2,
-        out_specs=(pl.BlockSpec(memory_space=pl.ANY),) * count,
-        scratch_shapes=[pltpu.SemaphoreType.DMA((count, 2))],
-        cost_estimate=pl.CostEstimate(
-            flops=0, transcendentals=0, bytes_accessed=2 * count * 16 * rows * cells
-        ),
+    whole = pl.BlockSpec(memory_space=pl.ANY)
+    hbm = pl.BlockSpec(memory_space=pltpu.HBM)
+    return pl.pallas_call(
+        functools.partial(pack_kernel, steps, planes),
+        out_shape=(jax.ShapeDtypeStruct((4, rows, cells), jnp.float32),) * len(steps),
+        in_specs=[hbm] * 2 + [whole] * len(after),
+        out_specs=(pl.BlockSpec(memory_space=pltpu.VMEM),) * len(steps),
+        scratch_shapes=[pltpu.SemaphoreType.DMA((len(steps), 2))],
+        compiler_params=pltpu.CompilerParams(vmem_limit_bytes=(4 if after else 61) * mebibyte),
+        cost_estimate=no_cost,
         name="pack",
-    )(velocity, level_set)
+    )(velocity, level_set, *after)
 
 
 def split(value):
@@ -123,57 +124,217 @@
 def on_plane(pieces, dx, dy):
     count = len(pieces)
     rows, cells = pieces[0].shape[1:]
-    lines = rows * count
-    piece = jax.ShapeDtypeStruct((4, rows, cells), jnp.float32)
     vmem = pl.BlockSpec(memory_space=pltpu.VMEM)
     return pl.pallas_call(
         functools.partial(plane_kernel, count),
-        out_shape=(piece,) * count,
+        out_shape=(jax.ShapeDtypeStruct((4, rows, cells), jnp.float32),) * count,
         in_specs=[vmem] * (2 + count),
         out_specs=(vmem,) * count,
-        scratch_shapes=[pltpu.VMEM((4, lines, cells), jnp.float32)] * 2,
-        compiler_params=pltpu.CompilerParams(vmem_limit_bytes=vmem_bytes),
-        cost_estimate=pl.CostEstimate(
-            flops=36 * lines * cells * (cells + lines),
-            transcendentals=lines * cells,
-            bytes_accessed=32 * lines * cells,
-        ),
+        scratch_shapes=[pltpu.VMEM((4, rows * count, cells), jnp.float32)] * 2,
+        compiler_params=pltpu.CompilerParams(vmem_limit_bytes=16 * mebibyte),
+        cost_estimate=no_cost,
         name="plane",
     )(dx, dy, *pieces)
 
 
-def join_kernel(count, planes, *refs):
-    pieces = refs[: count * planes]
-    inverse, first_add, cross, out = refs[count * planes :]
+def join_kernel(steps, planes, *refs):
+    pieces = refs[: len(steps)]
+    inverse, first_add, cross = refs[len(steps) : len(steps) + 3]
+    out, held, sems = refs[-3:]
     me = lax.axis_index("wide")
+    copies = []
+    for i, (chunk, step) in enumerate(steps):
+        plane = (me ^ step) * planes + chunk
+        piece = pieces[i]
+        scale = inverse[plane]
+        held[i, 0] = piece[0] * scale + first_add[plane]
+        held[i, 1] = piece[1] * scale + piece[3] * cross[plane]
+        held[i, 2] = piece[2] * scale
+        copies.append(pltpu.make_async_copy(held.at[i], out.at[:, plane], sems.at[i]))
+        copies[-1].start()
+    for copy in copies:
+        copy.wait()
+
+
+def join(steps, pieces, fields, planes, total=None):
+    shape = fields[0].shape
+    vmem = pl.BlockSpec(memory_space=pltpu.VMEM)
+    whole = pl.BlockSpec(memory_space=pl.ANY)
+    extra = [] if total is None else [total]
+    return pl.pallas_call(
+        functools.partial(join_kernel, steps, planes),
+        out_shape=jax.ShapeDtypeStruct((3,) + shape, jnp.float32),
+        in_specs=[vmem] * (len(steps) + 3) + [whole] * len(extra),
+        out_specs=whole,
+        input_output_aliases={len(steps) + 3: 0} if extra else {},
+        scratch_shapes=[
+            pltpu.VMEM((len(steps), 3) + shape[1:], jnp.float32),
+            pltpu.SemaphoreType.DMA((len(steps),)),
+        ],
+        compiler_params=pltpu.CompilerParams(vmem_limit_bytes=8 * mebibyte),
+        cost_estimate=small_cost,
+        name="join",
+    )(*pieces, *fields, *extra)
+
+
+def panel_kernel(count, level_set, after, *refs):
+    outs, (held, sem) = refs[:count], refs[count:]
+    copy = pltpu.make_async_copy(level_set, held, sem)
+    copy.start()
+    copy.wait()
+    heavy = 0.5 * (1.0 + jnp.tanh(held[...] / interface_width))
+    held[...] = 0.2 + 0.8 * heavy
+    me = lax.axis_index("grp")
+    width = outs[0].shape[2]
     for step in range(count):
-        for chunk in range(planes):
-            plane = (me ^ step) * planes + chunk
-            piece = pieces[chunk * count + step]
-            scale = inverse[plane]
-            out[0, plane] = piece[0] * scale + first_add[plane]
-            out[1, plane] = piece[1] * scale + piece[3] * cross[plane]
-            out[2, plane] = piece[2] * scale
-
-
-def join(pieces, inverse, first_add, cross, count, planes):
+        outs[step][...] = held[:, :, pl.ds(pl.multiple_of((me ^ step) * width, 128), width)]
+
+
+def panels(level_set, after, count):
+    slab, rows, cells = level_set.shape
     vmem = pl.BlockSpec(memory_space=pltpu.VMEM)
     return pl.pallas_call(
-        functools.partial(join_kernel, count, planes),
-        out_shape=jax.ShapeDtypeStruct((3,) + inverse.shape, jnp.float32),
-        in_specs=[vmem] * (count * planes + 3),
-        out_specs=vmem,
-        compiler_params=pltpu.CompilerParams(vmem_limit_bytes=vmem_bytes),
-        name="join",
-    )(*pieces, inverse, first_add, cross)
-
-
-def exchange(pieces, order):
-    count = len(pieces)
-    got = [pieces[0]] + [None] * (count - 1)
-    for step in order:
-        got[step] = lax.ppermute(pieces[step], "wide", [(i, i ^ step) for i in range(count)])
-    return got
+        functools.partial(panel_kernel, count),
+        out_shape=(jax.ShapeDtypeStruct((slab, rows, cells // count), jnp.float32),) * count,
+        in_specs=[pl.BlockSpec(memory_space=pltpu.HBM), pl.BlockSpec(memory_space=pl.ANY)],
+        out_specs=(vmem,) * count,
+        scratch_shapes=[pltpu.VMEM((slab, rows, cells), jnp.float32), pltpu.SemaphoreType.DMA],
+        compiler_params=pltpu.CompilerParams(vmem_limit_bytes=6 * mebibyte),
+        cost_estimate=no_cost,
+        name="panels",
+    )(level_set, after)
+
+
+def z_lines_kernel(count, tables, *refs):
+    parts, outs, held = refs[:count], refs[count : 2 * count], refs[-1]
+    slab, rows, _ = parts[0].shape
+    for step in range(count):
+        held[step * slab : (step + 1) * slab] = parts[step][...]
+    table = tables[lax.axis_index("grp")]
+    for row in range(rows):
+        line = jnp.dot(
+            table,
+            held[:, row, :],
+            precision=lax.Precision.HIGHEST,
+            preferred_element_type=jnp.float32,
+        )
+        for step in range(count):
+            outs[step][:, row, :] = line[step * slab : (step + 1) * slab]
+
+
+def z_lines(tables, parts):
+    count = len(parts)
+    slab, rows, width = parts[0].shape
+    vmem = pl.BlockSpec(memory_space=pltpu.VMEM)
+    return pl.pallas_call(
+        functools.partial(z_lines_kernel, count),
+        out_shape=(jax.ShapeDtypeStruct(parts[0].shape, jnp.float32),) * count,
+        in_specs=[vmem] * (1 + count),
+        out_specs=(vmem,) * count,
+        scratch_shapes=[pltpu.VMEM((slab * count, rows, width), jnp.float32)],
+        compiler_params=pltpu.CompilerParams(vmem_limit_bytes=6 * mebibyte),
+        cost_estimate=no_cost,
+        name="z_lines",
+    )(tables, *parts)
+
+
+def prepare_kernel(count, dx, level_set, velocity, *refs):
+    parts, (inverse, first_add, cross) = refs[:count], refs[count : count + 3]
+    held, sems = refs[count + 3 :]
+    copies = [
+        pltpu.make_async_copy(level_set, held.at[0], sems.at[0]),
+        pltpu.make_async_copy(velocity.at[2], held.at[1], sems.at[1]),
+    ]
+    for copy in copies:
+        copy.start()
+    for copy in copies:
+        copy.wait()
+    me = lax.axis_index("grp")
+    width = parts[0].shape[2]
+    slab, rows, cells = level_set.shape
+    heavy = 0.5 * (1.0 + jnp.tanh(held[0] / interface_width))
+    inverse[...] = 1.0 / (0.25 + 0.75 * heavy)
+    for step in range(count):
+        here = pl.ds(pl.multiple_of((me ^ step) * width, 128), width)
+        cross[:, :, here] = parts[step][...] * inverse[:, :, here]
+    grad = times_x(held[1].reshape(slab * rows, cells), dx[...]).reshape(slab, rows, cells)
+    first_add[...] = cross[...] * grad
+
+
+def prepare(dx, level_set, velocity, parts):
+    vmem = pl.BlockSpec(memory_space=pltpu.VMEM)
+    whole = pl.BlockSpec(memory_space=pltpu.HBM)
+    return pl.pallas_call(
+        functools.partial(prepare_kernel, len(parts)),
+        out_shape=(jax.ShapeDtypeStruct(level_set.shape, jnp.float32),) * 3,
+        in_specs=[vmem, whole, whole] + [vmem] * len(parts),
+        out_specs=(vmem,) * 3,
+        scratch_shapes=[
+            pltpu.VMEM((2,) + level_set.shape, jnp.float32),
+            pltpu.SemaphoreType.DMA((2,)),
+        ],
+        compiler_params=pltpu.CompilerParams(vmem_limit_bytes=16 * mebibyte),
+        cost_estimate=no_cost,
+        name="prepare",
+    )(dx, level_set, velocity, *parts)
+
+
+def gate_kernel(*refs):
+    pass
+
+
+def gate(pieces, token, after):
+    arrays = [*pieces, token]
+    whole = pl.BlockSpec(memory_space=pl.ANY)
+    outs = pl.pallas_call(
+        gate_kernel,
+        out_shape=tuple(jax.ShapeDtypeStruct(x.shape, x.dtype) for x in arrays),
+        in_specs=[whole] * (len(arrays) + len(after)),
+        out_specs=(whole,) * len(arrays),
+        input_output_aliases={i: i for i in range(len(arrays))},
+        compiler_params=pltpu.CompilerParams(vmem_limit_bytes=mebibyte),
+        cost_estimate=small_cost,
+        name="gate",
+    )(*arrays, *after)
+    return outs[:-1], outs[-1]
+
+
+class Line:
+    def __init__(self):
+        self.arrived = []
+        self.token = jnp.zeros((8, 128), jnp.float32)
+
+    def send(self, piece, axis, step):
+        count = lax.axis_size(axis)
+        if len(self.arrived) >= flight:
+            (piece,), self.token = gate([piece], self.token, [self.arrived[-flight]])
+        got = lax.ppermute(piece, axis, [(i, i ^ step) for i in range(count)])
+        self.arrived.append(got)
+        return got
+
+
+def turns(first, second):
+    both = [x for pair in zip(first, second) for x in pair]
+    shorter = min(len(first), len(second))
+    return both + list(first[shorter:]) + list(second[shorter:])
+
+
+def message_order(count, planes, group_count):
+    far, near = range(count // 2, count), range(1, count // 2)
+    out = [("out", chunk, step) for chunk in range(planes) for step in turns(far, near)]
+    back = [("back", chunk, step) for chunk in range(planes - 1) for step in turns(far, near)]
+    back += [("back", planes - 1, step) for step in turns(near, far)]
+    first_z = count - 1
+    second_z = max(len(out) + 3, first_z + 2 * (group_count - 2) + 1)
+    order = []
+    for place, message in enumerate(out + back + [None] * 2 * (second_z + 2 * group_count)):
+        for start, kind in ((first_z, "z_out"), (second_z, "z_back")):
+            step, odd = divmod(place - start, 2)
+            if not odd and 0 <= step < group_count - 1:
+                order.append((kind, 0, step + 1))
+        if message is not None:
+            order.append(message)
+    return order
 
 
 def by_planes(velocity, level_set):
@@ -182,35 +343,54 @@
     count = lax.axis_size("wide")
     group_count = lax.axis_size("grp")
     planes = slab_z // count
-    table_x = derivative_table(cells_x).T
-    high, low = halves(table_x)
+    high, low = halves(derivative_table(cells_x).T)
     dx = jnp.asarray(np.concatenate([high, high, low], axis=0))
     high, low = halves(derivative_table(slab_y * count))
     dy = jnp.asarray(np.concatenate([high, low, high], axis=1))
-    far = list(range(count // 2, count))
-    near = list(range(1, count // 2))
-    order = [step for pair in zip(far, near + [None]) for step in pair if step is not None]
-
-    arrived = [
-        exchange(pack(velocity, level_set, count, planes, chunk), order) for chunk in range(planes)
-    ]
-    returned = []
-    for chunk in range(planes):
-        returned += exchange(on_plane(arrived[chunk], dx, dy), order)
-
-    viscosity, density = properties(level_set)
-    whole = lax.all_gather(viscosity, "grp", axis=0, tiled=True)
-    dz_rows = lax.dynamic_slice_in_dim(
-        jnp.asarray(derivative_table(slab_z * group_count)),
-        lax.axis_index("grp") * slab_z,
-        slab_z,
-        0,
-    )
-    dz_visc = jnp.einsum("ij,jyx->iyx", dz_rows, whole, precision=lax.Precision.HIGHEST)
-    inverse = 1.0 / density
-    cross = dz_visc * inverse
-    first_add = cross * along_last(velocity[2], jnp.asarray(table_x))
-    return join(returned, inverse, first_add, cross, count, planes)
+    table_z = derivative_table(slab_z * group_count)
+    table_z = table_z.reshape(group_count, slab_z, group_count, slab_z)
+    partners = [place ^ np.arange(group_count) for place in range(group_count)]
+    tables = jnp.asarray(
+        np.stack([table_z[p][:, :, p].reshape((slab_z * group_count,) * 2) for p in partners])
+    )
+
+    order = message_order(count, planes, group_count)
+    first = [(0, step) for kind, chunk, step in order if kind == "out" and chunk == 0]
+    first = [piece for piece in first if piece[1] >= count // 2][:2]
+    rest = [(c, step) for c in range(planes) for step in range(count) if (c, step) not in first]
+    sent = dict(zip(first, pack(velocity, level_set, first, planes)))
+    sent.update(zip(rest, pack(velocity, level_set, rest, planes, [sent[p] for p in first])))
+
+    line = Line()
+    arrived = {(c, 0): sent[c, 0] for c in range(planes)}
+    result, returned = {}, {}
+    panel, z_arrived, z_result, z_returned = None, {}, None, {}
+    for kind, chunk, step in order:
+        if kind == "out":
+            arrived[chunk, step] = line.send(sent[chunk, step], "wide", step)
+        elif kind == "back":
+            if chunk not in result:
+                result[chunk] = on_plane([arrived[chunk, i] for i in range(count)], dx, dy)
+                returned[chunk, 0] = result[chunk][0]
+            returned[chunk, step] = line.send(result[chunk][step], "wide", step)
+        elif kind == "z_out":
+            if panel is None:
+                panel = panels(level_set, line.arrived[0], group_count)
+                z_arrived[0] = panel[0]
+            z_arrived[step] = line.send(panel[step], "grp", step)
+        else:
+            if z_result is None:
+                z_result = z_lines(tables, [z_arrived[i] for i in range(group_count)])
+                z_returned[0] = z_result[0]
+            z_returned[step] = line.send(z_result[step], "grp", step)
+
+    fields = prepare(dx, level_set, velocity, [z_returned[i] for i in range(group_count)])
+    total = None
+    early = [(c, i) for c in range(planes - 1) for i in range(count)] + [(planes - 1, 0)]
+    late = [(c, step) for kind, c, step in order if kind == "back" and c == planes - 1]
+    for steps in [early] + [[piece] for piece in late]:
+        total = join(steps, [returned[piece] for piece in steps], fields, planes, total)
+    return total
 
 
 def by_lines(velocity, level_set):
@@ -271,8 +451,10 @@
 
 
 def shards(velocity, level_set):
-    count = lax.axis_size("wide")
-    if count & (count - 1) == 0 and velocity.shape[1] % count == 0:
+    slab_z, slab_y, cells_x = level_set.shape
+    count, group_count = lax.axis_size("wide"), lax.axis_size("grp")
+    pairs = count > 1 and group_count > 1 and count & (count - 1) == 0 == group_count & (group_count - 1)
+    if pairs and slab_z % count == 0 == cells_x % (128 * group_count) and slab_y % 16 == 0:
         return by_planes(velocity, level_set)
     return by_lines(velocity, level_set)
 

time: 171 us -> 98.8 us (0.58)
  Pallas kernels: 71.4 us -> 15 us
  between operations: 13.6 us -> 0.29 us
  starting transfers between devices: 43.5 us -> 55.5 us
  matrix products: 6.02 us -> 0 us
  waiting for transfers between devices: 31.9 us -> 26.9 us
  other arithmetic: 2.3 us -> 0 us
    pallas_call x5 -> x44, Pallas kernels: 71.4 us -> 15 us  [the longest x8 5.67 us: join(): pl.pallas_call(functools.partial(join_kernel, steps, planes), out_shape=j...]
    ppermute x28 -> x34, starting transfers between devices: 43.5 us -> 55.5 us  [send(): got = lax.ppermute(piece, axis, [(i, i ^ step) for i in range(count)])]
    dot_general x2 -> x0, matrix products: 6.02 us -> none  [the longest x1 3.89 us: by_planes(): jnp.einsum('ij,jyx->iyx', dz_rows, whole, precision=lax.Precision.HIGHEST)]
    ppermute x28 -> x34, waiting for transfers between devices: 31.9 us -> 26.9 us  [send(): got = lax.ppermute(piece, axis, [(i, i ^ step) for i in range(count)])]
    add x1 -> x0, other arithmetic: 1.92 us -> none  [properties(): return (0.2 + 0.8 * heavy, 0.25 + 0.75 * heavy)]
  transfers between devices with their start and end apart: 29 -> 34, of which waited for: 10 -> 11; matrix products, arithmetic and copies ran while one was open for 4% -> 0% of each run, Pallas kernels for 41% -> 13%
where the time goes in v3:
time: 98.8 us; the launch traced here: 98.7 us
  starting transfers between devices  55.5 us (56%)
  waiting for transfers between devices  26.9 us (27%)
  Pallas kernels  15 us (15%)
    ppermute x34, starting transfers between devices, send(): got = lax.ppermute(piece, axis, [(i, i ^ step) for i in range(count)])  55.5 us
    ppermute x34, waiting for transfers between devices, send(): got = lax.ppermute(piece, axis, [(i, i ^ step) for i in range(count)])  26.9 us
    pallas_call x8, Pallas kernels, join(): pl.pallas_call(functools.partial(join_kernel, steps, planes), out_shape=j...  5.67 us
    pallas_call x2, Pallas kernels, on_plane(): pl.pallas_call(functools.partial(plane_kernel, count), out_shape=(jax.Sha...  3.94 us
    pallas_call x2, Pallas kernels, pack(): pl.pallas_call(functools.partial(pack_kernel, steps, planes), out_shape=(...  3.39 us
  transfers between devices with their start and end apart: 34, of which 11 were waited for; matrix products, arithmetic and copies ran while one was open for 0% of the time, Pallas kernels for 13%

profile of v3, /device:TPU:8, one launch (start us, length us, event | category | flops | bytes accessed | tf_op | source)
XLA Modules:
  0.0 98.7 jit_solution(2336573011612879772)
XLA Ops:
  0.0 1.8 %pack.2 = (f32[4,16,512]{2,1,0:T(8,128)}, f32[4,16,512]{2,1,0:T(8,128)}) custom-call(f32[3,16,16,512]{3,2,1,0:T(8,128)} %velocity.5, f32[16,16,512]{2,1,0:T(8,128)} %level_set.7), custom_call_target="tpu_custom_call" | custom-call | tf_op jit(solution)/shard_map/pack/pallas_call | solution.py:63
  1.8 2.7 %collective-permute-start = (f32[4,16,512]{2,1,0:T(8,128)}, f32[4,16,512]{2,1,0:T(8,128)S(1)}, u32[]{:S(2)}, u32[]{:S(2)}) collective-permute-start(f32[4,16,512]{2,1,0:T(8,128)} %get-tuple-element.105.refs_0_), channel_id=1, source_target_pairs={{0,4},{1,5},{2,6},{3,7},{4,0},{5,1},{6,2},{7,3},{8,12},{9,13},{10,... | collective-permute-start | bytes 393224 | tf_op jit(solution)/shard_map/ppermute | solution.py:311
  4.5 0.9 copy-done.5
  5.4 1.6 %pack.3 = (f32[4,16,512]{2,1,0:T(8,128)S(1)}, f32[4,16,512]{2,1,0:T(8,128)S(1)}, f32[4,16,512]{2,1,0:T(8,128)S(1)}, f32[4,16,512]{2,1,0:T(8,128)S(1)}, f32[4,16,...) custom-call(f32[3,16,16,512]{3,2,1,0:T(8,128)S(1)} %copy-done, ...), custom_call_target="tpu_custom_call" | custom-call | tf_op jit(solution)/shard_map/pack/pallas_call | solution.py:63
  7.0 1.6 %collective-permute-start.1 = (f32[4,16,512]{2,1,0:T(8,128)S(1)}, f32[4,16,512]{2,1,0:T(8,128)S(1)}, u32[]{:S(2)}, u32[]{:S(2)}) collective-permute-start(f32[4,16,512]{2,1,0:T(8,128)S(1)} %get-tuple-element.114), channel_id=1, source_target_pairs={{0,1},{1,0},{2,3},{3,2},{4,5},{5,4},{6,7},{7,6},{8,9},{9,8},{10,11... | collective-permute-start | bytes 393224 | tf_op jit(solution)/shard_map/ppermute | solution.py:311
  9.0 3.0 %collective-permute-start.4 = (f32[4,16,512]{2,1,0:T(8,128)S(1)}, f32[4,16,512]{2,1,0:T(8,128)S(1)}, u32[]{:S(2)}, u32[]{:S(2)}) collective-permute-start(f32[4,16,512]{2,1,0:T(8,128)S(1)} %get-tuple-element.119), channel_id=1, source_target_pairs={{0,6},{1,7},{2,4},{3,5},{4,2},{5,3},{6,0},{7,1},{8,14},{9,15},{10,... | collective-permute-start | bytes 393224 | tf_op jit(solution)/shard_map/ppermute | solution.py:311
  12.0 1.3 %collective-permute-done.after.refs_2_.refs_4_ = f32[4,16,512]{2,1,0:T(8,128)S(1)} collective-permute-done((f32[4,16,512]{2,1,0:T(8,128)}, f32[4,16,512]{2,1,0:T(8,128)S(1)}, u32[]{:S(2)}, u32[]{:S(2)}) %collective-permute-start) | collective-permute-done | bytes 131104 | tf_op jit(solution)/shard_map/ppermute | solution.py:311
  13.3 1.1 %collective-permute-start.6 = (f32[4,16,512]{2,1,0:T(8,128)S(1)}, f32[4,16,512]{2,1,0:T(8,128)S(1)}, u32[]{:S(2)}, u32[]{:S(2)}) collective-permute-start(f32[4,16,512]{2,1,0:T(8,128)S(1)} %get-tuple-element.125), channel_id=1, source_target_pairs={{0,3},{1,2},{2,1},{3,0},{4,7},{5,6},{6,5},{7,4},{8,11},{9,10},{10,... | collective-permute-start | bytes 393224 | tf_op jit(solution)/shard_map/ppermute | solution.py:311
  14.4 4.1 %collective-permute-start.7 = (f32[4,16,512]{2,1,0:T(8,128)S(1)}, f32[4,16,512]{2,1,0:T(8,128)S(1)}, u32[]{:S(2)}, u32[]{:S(2)}) collective-permute-start(f32[4,16,512]{2,1,0:T(8,128)S(1)} %get-tuple-element.127), channel_id=1, source_target_pairs={{0,7},{1,6},{2,5},{3,4},{4,3},{5,2},{6,1},{7,0},{8,15},{9,14},{10,... | collective-permute-start | bytes 393224 | tf_op jit(solution)/shard_map/ppermute | solution.py:311
  18.9 8.2 %collective-permute-start.10 = (f32[4,16,512]{2,1,0:T(8,128)S(1)}, f32[4,16,512]{2,1,0:T(8,128)S(1)}, u32[]{:S(2)}, u32[]{:S(2)}) collective-permute-start(f32[4,16,512]{2,1,0:T(8,128)S(1)} %get-tuple-element.135), channel_id=1, source_target_pairs={{0,4},{1,5},{2,6},{3,7},{4,0},{5,1},{6,2},{7,3},{8,12},{9,13},{10,... | collective-permute-start | bytes 393224 | tf_op jit(solution)/shard_map/ppermute | solution.py:311
  27.1 1.5 %collective-permute-start.5 = (f32[4,16,512]{2,1,0:T(8,128)S(1)}, f32[4,16,512]{2,1,0:T(8,128)S(1)}, u32[]{:S(2)}, u32[]{:S(2)}) collective-permute-start(f32[4,16,512]{2,1,0:T(8,128)S(1)} %get-tuple-element.120), channel_id=1, source_target_pairs={{0,1},{1,0},{2,3},{3,2},{4,5},{5,4},{6,7},{7,6},{8,9},{9,8},{10,11... | collective-permute-start | bytes 393224 | tf_op jit(solution)/shard_map/ppermute | solution.py:311
  28.6 1.5 %collective-permute-start.11 = (f32[16,16,128]{2,1,0:T(8,128)S(1)}, f32[16,16,128]{2,1,0:T(8,128)S(1)}, u32[]{:S(2)}, u32[]{:S(2)}) collective-permute-start(f32[16,16,128]{2,1,0:T(8,128)S(1)} %get-tuple-element.138), channel_id=1, source_target_pairs={{0,16},{8,24},{16,0},{24,8},{1,17},{9,25},{17,1},{25,9},{2,18},{10... | collective-permute-start | bytes 393224 | tf_op jit(solution)/shard_map/ppermute | solution.py:311
  30.1 2.2 %collective-permute-done.7.refs_2_.refs_7_ = f32[4,16,512]{2,1,0:T(8,128)S(1)} collective-permute-done((f32[4,16,512]{2,1,0:T(8,128)S(1)}, f32[4,16,512]{2,1,0:T(8,128)S(1)}, u32[]{:S(2)}, u32[]{:S(2)}) %collective-permute-start.7) | collective-permute-done | bytes 131104 | tf_op jit(solution)/shard_map/ppermute | solution.py:311
  32.3 2.5 %collective-permute-start.9 = (f32[4,16,512]{2,1,0:T(8,128)S(1)}, f32[4,16,512]{2,1,0:T(8,128)S(1)}, u32[]{:S(2)}, u32[]{:S(2)}) collective-permute-start(f32[4,16,512]{2,1,0:T(8,128)S(1)} %get-tuple-element.130), channel_id=1, source_target_pairs={{0,2},{1,3},{2,0},{3,1},{4,6},{5,7},{6,4},{7,5},{8,10},{9,11},{10,... | collective-permute-start | bytes 393224 | tf_op jit(solution)/shard_map/ppermute | solution.py:311
  35.3 0.6 collective-permute-start.14
  35.9 2.0 %plane.3 = (f32[4,16,512]{2,1,0:T(8,128)S(1)}, f32[4,16,512]{2,1,0:T(8,128)S(1)}, f32[4,16,512]{2,1,0:T(8,128)S(1)}, f32[4,16,512]{2,1,0:T(8,128)S(1)}, f32[4,16...) custom-call(bf16[1536,512]{1,0:T(8,128)(2,1)S(1)} %copy-done.1, ...), custom_call_target="tpu_custom_call" | custom-call | tf_op jit(solution)/shard_map/plane/pallas_call | solution.py:128
  37.9 3.8 %collective-permute-start.12 = (f32[4,16,512]{2,1,0:T(8,128)S(1)}, f32[4,16,512]{2,1,0:T(8,128)S(1)}, u32[]{:S(2)}, u32[]{:S(2)}) collective-permute-start(f32[4,16,512]{2,1,0:T(8,128)S(1)} %get-tuple-element.139), channel_id=1, source_target_pairs={{0,3},{1,2},{2,1},{3,0},{4,7},{5,6},{6,5},{7,4},{8,11},{9,10},{10,... | collective-permute-start | bytes 393224 | tf_op jit(solution)/shard_map/ppermute | solution.py:311
  41.7 1.4 %collective-permute-done.9.refs_2_ = f32[4,16,512]{2,1,0:T(8,128)S(1)} collective-permute-done((f32[4,16,512]{2,1,0:T(8,128)S(1)}, f32[4,16,512]{2,1,0:T(8,128)S(1)}, u32[]{:S(2)}, u32[]{:S(2)}) %collective-permute-start.9) | collective-permute-done | bytes 131104 | tf_op jit(solution)/shard_map/ppermute | solution.py:311
  43.1 4.6 %collective-permute-start.17 = (f32[4,16,512]{2,1,0:T(8,128)S(1)}, f32[4,16,512]{2,1,0:T(8,128)S(1)}, u32[]{:S(2)}, u32[]{:S(2)}) collective-permute-start(f32[4,16,512]{2,1,0:T(8,128)S(1)} %get-tuple-element.171), channel_id=1, source_target_pairs={{0,4},{1,5},{2,6},{3,7},{4,0},{5,1},{6,2},{7,3},{8,12},{9,13},{10,... | collective-permute-start | bytes 393224 | tf_op jit(solution)/shard_map/ppermute | solution.py:311
  47.7 1.5 %collective-permute-start.19 = (f32[4,16,512]{2,1,0:T(8,128)S(1)}, f32[4,16,512]{2,1,0:T(8,128)S(1)}, u32[]{:S(2)}, u32[]{:S(2)}) collective-permute-start(f32[4,16,512]{2,1,0:T(8,128)S(1)} %get-tuple-element.175), channel_id=1, source_target_pairs={{0,5},{1,4},{2,7},{3,6},{4,1},{5,0},{6,3},{7,2},{8,13},{9,12},{10,... | collective-permute-start | bytes 393224 | tf_op jit(solution)/shard_map/ppermute | solution.py:311
  49.2 0.9 z_lines.1
  50.2 7.2 %collective-permute-done.15.refs_7_.refs_2_ = f32[4,16,512]{2,1,0:T(8,128)S(1)} collective-permute-done((f32[4,16,512]{2,1,0:T(8,128)S(1)}, f32[4,16,512]{2,1,0:T(8,128)S(1)}, u32[]{:S(2)}, u32[]{:S(2)}) %collective-permute-start.15) | collective-permute-done | bytes 131104 | tf_op jit(solution)/shard_map/ppermute | solution.py:311
  57.5 1.0 %collective-permute-done.17.refs_2_.refs_4_ = f32[4,16,512]{2,1,0:T(8,128)S(1)} collective-permute-done((f32[4,16,512]{2,1,0:T(8,128)S(1)}, f32[4,16,512]{2,1,0:T(8,128)S(1)}, u32[]{:S(2)}, u32[]{:S(2)}) %collective-permute-start.17) | collective-permute-done | bytes 131104 | tf_op jit(solution)/shard_map/ppermute | solution.py:311
  58.5 0.9 collective-permute-start.22
  59.4 1.5 %collective-permute-start.23 = (f32[16,16,128]{2,1,0:T(8,128)S(1)}, f32[16,16,128]{2,1,0:T(8,128)S(1)}, u32[]{:S(2)}, u32[]{:S(2)}) collective-permute-start(f32[16,16,128]{2,1,0:T(8,128)S(1)} %get-tuple-element.183), channel_id=1, source_target_pairs={{0,16},{8,24},{16,0},{24,8},{1,17},{9,25},{17,1},{25,9},{2,18},{10... | collective-permute-start | bytes 393224 | tf_op jit(solution)/shard_map/ppermute | solution.py:311
  60.8 0.5 collective-permute-done.19.refs_2_.refs_5_
  61.3 4.2 %collective-permute-start.24 = (f32[4,16,512]{2,1,0:T(8,128)S(1)}, f32[4,16,512]{2,1,0:T(8,128)S(1)}, u32[]{:S(2)}, u32[]{:S(2)}) collective-permute-start(f32[4,16,512]{2,1,0:T(8,128)S(1)} %get-tuple-element.185), channel_id=1, source_target_pairs={{0,3},{1,2},{2,1},{3,0},{4,7},{5,6},{6,5},{7,4},{8,11},{9,10},{10,... | collective-permute-start | bytes 393224 | tf_op jit(solution)/shard_map/ppermute | solution.py:311
  65.5 2.0 %plane.2 = (f32[4,16,512]{2,1,0:T(8,128)S(1)}, f32[4,16,512]{2,1,0:T(8,128)S(1)}, f32[4,16,512]{2,1,0:T(8,128)S(1)}, f32[4,16,512]{2,1,0:T(8,128)S(1)}, f32[4,16...) custom-call(bf16[1536,512]{1,0:T(8,128)(2,1)S(1)} %copy-done.1, ...), custom_call_target="tpu_custom_call" | custom-call | tf_op jit(solution)/shard_map/plane/pallas_call | solution.py:128
  67.5 1.3 %collective-permute-start.25 = (f32[4,16,512]{2,1,0:T(8,128)S(1)}, f32[4,16,512]{2,1,0:T(8,128)S(1)}, u32[]{:S(2)}, u32[]{:S(2)}) collective-permute-start(f32[4,16,512]{2,1,0:T(8,128)S(1)} %get-tuple-element.187), channel_id=1, source_target_pairs={{0,7},{1,6},{2,5},{3,4},{4,3},{5,2},{6,1},{7,0},{8,15},{9,14},{10,... | collective-permute-start | bytes 393224 | tf_op jit(solution)/shard_map/ppermute | solution.py:311
  69.3 0.5 collective-permute-start.27
  69.8 2.6 %collective-permute-start.28 = (f32[4,16,512]{2,1,0:T(8,128)S(1)}, f32[4,16,512]{2,1,0:T(8,128)S(1)}, u32[]{:S(2)}, u32[]{:S(2)}) collective-permute-start(f32[4,16,512]{2,1,0:T(8,128)S(1)} %get-tuple-element.193), channel_id=1, source_target_pairs={{0,4},{1,5},{2,6},{3,7},{4,0},{5,1},{6,2},{7,3},{8,12},{9,13},{10,... | collective-permute-start | bytes 393224 | tf_op jit(solution)/shard_map/ppermute | solution.py:311
  72.6 1.0 %collective-permute-start.33 = (f32[4,16,512]{2,1,0:T(8,128)S(1)}, f32[4,16,512]{2,1,0:T(8,128)S(1)}, u32[]{:S(2)}, u32[]{:S(2)}) collective-permute-start(f32[4,16,512]{2,1,0:T(8,128)S(1)} %get-tuple-element.202), channel_id=1, source_target_pairs={{0,2},{1,3},{2,0},{3,1},{4,6},{5,7},{6,4},{7,5},{8,10},{9,11},{10,... | collective-permute-start | bytes 393224 | tf_op jit(solution)/shard_map/ppermute | solution.py:311
  73.6 5.5 %collective-permute-done.25.refs_2_.refs_7_ = f32[4,16,512]{2,1,0:T(8,128)S(1)} collective-permute-done((f32[4,16,512]{2,1,0:T(8,128)S(1)}, f32[4,16,512]{2,1,0:T(8,128)S(1)}, u32[]{:S(2)}, u32[]{:S(2)}) %collective-permute-start.25) | collective-permute-done | bytes 131104 | tf_op jit(solution)/shard_map/ppermute | solution.py:311
  79.2 3.2 %collective-permute-start.31 = (f32[4,16,512]{2,1,0:T(8,128)S(1)}, f32[4,16,512]{2,1,0:T(8,128)S(1)}, u32[]{:S(2)}, u32[]{:S(2)}) collective-permute-start(f32[4,16,512]{2,1,0:T(8,128)S(1)} %get-tuple-element.200), channel_id=1, source_target_pairs={{0,3},{1,2},{2,1},{3,0},{4,7},{5,6},{6,5},{7,4},{8,11},{9,10},{10,... | collective-permute-start | bytes 393224 | tf_op jit(solution)/shard_map/ppermute | solution.py:311
  82.4 1.2 %collective-permute-start.30 = (f32[4,16,512]{2,1,0:T(8,128)S(1)}, f32[4,16,512]{2,1,0:T(8,128)S(1)}, u32[]{:S(2)}, u32[]{:S(2)}) collective-permute-start(f32[4,16,512]{2,1,0:T(8,128)S(1)} %get-tuple-element.199), channel_id=1, source_target_pairs={{0,6},{1,7},{2,4},{3,5},{4,2},{5,3},{6,0},{7,1},{8,14},{9,15},{10,... | collective-permute-start | bytes 393224 | tf_op jit(solution)/shard_map/ppermute | solution.py:311
  83.5 1.0 collective-permute-start.29
  84.5 0.9 prepare.1
  85.4 1.0 %join.8.refs_4_ = f32[3,16,16,512]{3,2,1,0:T(8,128)} custom-call(f32[4,16,512]{2,1,0:T(8,128)S(1)} %get-tuple-element.203.refs_0_, f32[4,16,512]{2,1,0:T(8,128)S(1)} %collective-permute-done.18.refs_2_.refs_1_, f32[4,16,512]{2,1,0:T(8,128)S(1)} %collective-permute-done.21.refs_2_, f32[4,16,512]{2,1,0:T(8,128)S(1)} %collective-permute-done.24.refs_2_.refs_3_, ...), custom_call_target="tpu_custom_call" | custom-call | flops 10000000 | tf_op jit(solution)/shard_map/join/pallas_call | solution.py:164
  86.4 0.7 join.9.refs_4_
  87.1 0.7 join.10.refs_4_
  87.8 0.7 join.11.refs_4_
  88.5 0.7 join.12.refs_4_
  89.1 2.0 %collective-permute-done.31.refs_0_ = f32[4,16,512]{2,1,0:T(8,128)S(1)} collective-permute-done((f32[4,16,512]{2,1,0:T(8,128)S(1)}, f32[4,16,512]{2,1,0:T(8,128)S(1)}, u32[]{:S(2)}, u32[]{:S(2)}) %collective-permute-start.31) | collective-permute-done | bytes 131104 | tf_op jit(solution)/shard_map/ppermute | solution.py:311
  91.2 0.7 join.13.refs_4_
  91.8 2.7 %collective-permute-done.30.refs_0_ = f32[4,16,512]{2,1,0:T(8,128)S(1)} collective-permute-done((f32[4,16,512]{2,1,0:T(8,128)S(1)}, f32[4,16,512]{2,1,0:T(8,128)S(1)}, u32[]{:S(2)}, u32[]{:S(2)}) %collective-permute-start.30) | collective-permute-done | bytes 131104 | tf_op jit(solution)/shard_map/ppermute | solution.py:311
  94.5 0.7 join.14.refs_4_
  95.2 2.8 %collective-permute-done.29.refs_0_ = f32[4,16,512]{2,1,0:T(8,128)S(1)} collective-permute-done((f32[4,16,512]{2,1,0:T(8,128)S(1)}, f32[4,16,512]{2,1,0:T(8,128)S(1)}, u32[]{:S(2)}, u32[]{:S(2)}) %collective-permute-start.29) | collective-permute-done | bytes 131104 | tf_op jit(solution)/shard_map/ppermute | solution.py:311
  98.0 0.7 join.15
  (77 shorter events, 2.0 us)
Async XLA Ops:
  0.0 4.5 %copy-start.2 = (f32[16,16,512]{2,1,0:T(8,128)S(1)}, f32[16,16,512]{2,1,0:T(8,128)}, u32[]{:S(2)}) copy-start(f32[16,16,512]{2,1,0:T(8,128)} %level_set.7) | copy-start | bytes 1572868
  0.0 4.5 %copy-start = (f32[3,16,16,512]{3,2,1,0:T(8,128)S(1)}, f32[3,16,16,512]{3,2,1,0:T(8,128)}, u32[]{:S(2)}) copy-start(f32[3,16,16,512]{3,2,1,0:T(8,128)} %velocity.5) | copy-start | bytes 4718596
  1.8 11.4 %collective-permute-start = (f32[4,16,512]{2,1,0:T(8,128)}, f32[4,16,512]{2,1,0:T(8,128)S(1)}, u32[]{:S(2)}, u32[]{:S(2)}) collective-permute-start(f32[4,16,512]{2,1,0:T(8,128)} %get-tuple-element.105.refs_0_), channel_id=1, source_target_pairs={{0,4},{1,5},{2,6},{3,7},{4,0},{5,1},{6,2},{7,3},{8,12},{9,13},{10,... | collective-permute-start | bytes 393224 | tf_op jit(solution)/shard_map/ppermute | solution.py:311
  4.5 0.9 copy-start.5
  7.0 7.4 %collective-permute-start.1 = (f32[4,16,512]{2,1,0:T(8,128)S(1)}, f32[4,16,512]{2,1,0:T(8,128)S(1)}, u32[]{:S(2)}, u32[]{:S(2)}) collective-permute-start(f32[4,16,512]{2,1,0:T(8,128)S(1)} %get-tuple-element.114), channel_id=1, source_target_pairs={{0,1},{1,0},{2,3},{3,2},{4,5},{5,4},{6,7},{7,6},{8,9},{9,8},{10,11... | collective-permute-start | bytes 393224 | tf_op jit(solution)/shard_map/ppermute | solution.py:311
  8.6 10.2 %collective-permute-start.2 = (f32[4,16,512]{2,1,0:T(8,128)}, f32[4,16,512]{2,1,0:T(8,128)S(1)}, u32[]{:S(2)}, u32[]{:S(2)}) collective-permute-start(f32[4,16,512]{2,1,0:T(8,128)} %get-tuple-element.106.refs_1_), channel_id=1, source_target_pairs={{0,5},{1,4},{2,7},{3,6},{4,1},{5,0},{6,3},{7,2},{8,13},{9,12},{10,... | collective-permute-start | bytes 393224 | tf_op jit(solution)/shard_map/ppermute | solution.py:311
  8.9 10.0 %collective-permute-start.3 = (f32[4,16,512]{2,1,0:T(8,128)S(1)}, f32[4,16,512]{2,1,0:T(8,128)S(1)}, u32[]{:S(2)}, u32[]{:S(2)}) collective-permute-start(f32[4,16,512]{2,1,0:T(8,128)S(1)} %get-tuple-element.117), channel_id=1, source_target_pairs={{0,2},{1,3},{2,0},{3,1},{4,6},{5,7},{6,4},{7,5},{8,10},{9,11},{10,... | collective-permute-start | bytes 393224 | tf_op jit(solution)/shard_map/ppermute | solution.py:311
  9.0 18.1 %collective-permute-start.4 = (f32[4,16,512]{2,1,0:T(8,128)S(1)}, f32[4,16,512]{2,1,0:T(8,128)S(1)}, u32[]{:S(2)}, u32[]{:S(2)}) collective-permute-start(f32[4,16,512]{2,1,0:T(8,128)S(1)} %get-tuple-element.119), channel_id=1, source_target_pairs={{0,6},{1,7},{2,4},{3,5},{4,2},{5,3},{6,0},{7,1},{8,14},{9,15},{10,... | collective-permute-start | bytes 393224 | tf_op jit(solution)/shard_map/ppermute | solution.py:311
  13.3 22.6 %copy-start.1 = (bf16[1536,512]{1,0:T(8,128)(2,1)S(1)}, bf16[1536,512]{1,0:T(8,128)(2,1)}, u32[]{:S(2)}) copy-start(bf16[1536,512]{1,0:T(8,128)(2,1)} %constant.8.clone.dx) | copy-start | bytes 4718596
  13.3 22.6 %copy-start.3 = (bf16[128,384]{1,0:T(8,128)(2,1)S(1)}, bf16[128,384]{1,0:T(8,128)(2,1)}, u32[]{:S(2)}) copy-start(bf16[128,384]{1,0:T(8,128)(2,1)} %constant.9.clone.dy) | copy-start | bytes 294916
  13.3 15.4 %collective-permute-start.6 = (f32[4,16,512]{2,1,0:T(8,128)S(1)}, f32[4,16,512]{2,1,0:T(8,128)S(1)}, u32[]{:S(2)}, u32[]{:S(2)}) collective-permute-start(f32[4,16,512]{2,1,0:T(8,128)S(1)} %get-tuple-element.125), channel_id=1, source_target_pairs={{0,3},{1,2},{2,1},{3,0},{4,7},{5,6},{6,5},{7,4},{8,11},{9,10},{10,... | collective-permute-start | bytes 393224 | tf_op jit(solution)/shard_map/ppermute | solution.py:311
  14.4 17.9 %collective-permute-start.7 = (f32[4,16,512]{2,1,0:T(8,128)S(1)}, f32[4,16,512]{2,1,0:T(8,128)S(1)}, u32[]{:S(2)}, u32[]{:S(2)}) collective-permute-start(f32[4,16,512]{2,1,0:T(8,128)S(1)} %get-tuple-element.127), channel_id=1, source_target_pairs={{0,7},{1,6},{2,5},{3,4},{4,3},{5,2},{6,1},{7,0},{8,15},{9,14},{10,... | collective-permute-start | bytes 393224 | tf_op jit(solution)/shard_map/ppermute | solution.py:311
  18.8 13.5 %collective-permute-start.8 = (f32[16,16,128]{2,1,0:T(8,128)S(1)}, f32[16,16,128]{2,1,0:T(8,128)S(1)}, u32[]{:S(2)}, u32[]{:S(2)}) collective-permute-start(f32[16,16,128]{2,1,0:T(8,128)S(1)} %get-tuple-element.129), channel_id=1, source_target_pairs={{0,8},{8,0},{16,24},{24,16},{1,9},{9,1},{17,25},{25,17},{2,10},{10... | collective-permute-start | bytes 393224 | tf_op jit(solution)/shard_map/ppermute | solution.py:311
  18.9 15.9 %collective-permute-start.10 = (f32[4,16,512]{2,1,0:T(8,128)S(1)}, f32[4,16,512]{2,1,0:T(8,128)S(1)}, u32[]{:S(2)}, u32[]{:S(2)}) collective-permute-start(f32[4,16,512]{2,1,0:T(8,128)S(1)} %get-tuple-element.135), channel_id=1, source_target_pairs={{0,4},{1,5},{2,6},{3,7},{4,0},{5,1},{6,2},{7,3},{8,12},{9,13},{10,... | collective-permute-start | bytes 393224 | tf_op jit(solution)/shard_map/ppermute | solution.py:311
  27.1 8.1 %collective-permute-start.5 = (f32[4,16,512]{2,1,0:T(8,128)S(1)}, f32[4,16,512]{2,1,0:T(8,128)S(1)}, u32[]{:S(2)}, u32[]{:S(2)}) collective-permute-start(f32[4,16,512]{2,1,0:T(8,128)S(1)} %get-tuple-element.120), channel_id=1, source_target_pairs={{0,1},{1,0},{2,3},{3,2},{4,5},{5,4},{6,7},{7,6},{8,9},{9,8},{10,11... | collective-permute-start | bytes 393224 | tf_op jit(solution)/shard_map/ppermute | solution.py:311
  28.6 9.2 %collective-permute-start.11 = (f32[16,16,128]{2,1,0:T(8,128)S(1)}, f32[16,16,128]{2,1,0:T(8,128)S(1)}, u32[]{:S(2)}, u32[]{:S(2)}) collective-permute-start(f32[16,16,128]{2,1,0:T(8,128)S(1)} %get-tuple-element.138), channel_id=1, source_target_pairs={{0,16},{8,24},{16,0},{24,8},{1,17},{9,25},{17,1},{25,9},{2,18},{10... | collective-permute-start | bytes 393224 | tf_op jit(solution)/shard_map/ppermute | solution.py:311
  32.3 9.4 %collective-permute-start.13 = (f32[4,16,512]{2,1,0:T(8,128)S(1)}, f32[4,16,512]{2,1,0:T(8,128)S(1)}, u32[]{:S(2)}, u32[]{:S(2)}) collective-permute-start(f32[4,16,512]{2,1,0:T(8,128)S(1)} %get-tuple-element.140), channel_id=1, source_target_pairs={{0,5},{1,4},{2,7},{3,6},{4,1},{5,0},{6,3},{7,2},{8,13},{9,12},{10,... | collective-permute-start | bytes 393224 | tf_op jit(solution)/shard_map/ppermute | solution.py:311
  32.3 10.8 %collective-permute-start.9 = (f32[4,16,512]{2,1,0:T(8,128)S(1)}, f32[4,16,512]{2,1,0:T(8,128)S(1)}, u32[]{:S(2)}, u32[]{:S(2)}) collective-permute-start(f32[4,16,512]{2,1,0:T(8,128)S(1)} %get-tuple-element.130), channel_id=1, source_target_pairs={{0,2},{1,3},{2,0},{3,1},{4,6},{5,7},{6,4},{7,5},{8,10},{9,11},{10,... | collective-permute-start | bytes 393224 | tf_op jit(solution)/shard_map/ppermute | solution.py:311
  34.8 12.8 %collective-permute-start.16 = (f32[16,16,128]{2,1,0:T(8,128)S(1)}, f32[16,16,128]{2,1,0:T(8,128)S(1)}, u32[]{:S(2)}, u32[]{:S(2)}) collective-permute-start(f32[16,16,128]{2,1,0:T(8,128)S(1)} %get-tuple-element.153), channel_id=1, source_target_pairs={{0,24},{8,16},{16,8},{24,0},{1,25},{9,17},{17,9},{25,1},{2,26},{10... | collective-permute-start | bytes 393224 | tf_op jit(solution)/shard_map/ppermute | solution.py:311
  35.3 12.4 %collective-permute-start.14 = (f32[4,16,512]{2,1,0:T(8,128)S(1)}, f32[4,16,512]{2,1,0:T(8,128)S(1)}, u32[]{:S(2)}, u32[]{:S(2)}) collective-permute-start(f32[4,16,512]{2,1,0:T(8,128)S(1)} %get-tuple-element.141), channel_id=1, source_target_pairs={{0,6},{1,7},{2,4},{3,5},{4,2},{5,3},{6,0},{7,1},{8,14},{9,15},{10,... | collective-permute-start | bytes 393224 | tf_op jit(solution)/shard_map/ppermute | solution.py:311
  35.9 13.3 %copy-start.4 = (f32[4,64,64]{2,1,0:T(8,128)S(1)}, f32[4,64,64]{2,1,0:T(8,128)}, u32[]{:S(2)}) copy-start(f32[4,64,64]{2,1,0:T(8,128)} %constant.10.clone.tables) | copy-start | bytes 196612
  37.9 12.2 %collective-permute-start.12 = (f32[4,16,512]{2,1,0:T(8,128)S(1)}, f32[4,16,512]{2,1,0:T(8,128)S(1)}, u32[]{:S(2)}, u32[]{:S(2)}) collective-permute-start(f32[4,16,512]{2,1,0:T(8,128)S(1)} %get-tuple-element.139), channel_id=1, source_target_pairs={{0,3},{1,2},{2,1},{3,0},{4,7},{5,6},{6,5},{7,4},{8,11},{9,10},{10,... | collective-permute-start | bytes 393224 | tf_op jit(solution)/shard_map/ppermute | solution.py:311
  41.7 15.8 %collective-permute-start.15 = (f32[4,16,512]{2,1,0:T(8,128)S(1)}, f32[4,16,512]{2,1,0:T(8,128)S(1)}, u32[]{:S(2)}, u32[]{:S(2)}) collective-permute-start(f32[4,16,512]{2,1,0:T(8,128)S(1)} %get-tuple-element.144), channel_id=1, source_target_pairs={{0,7},{1,6},{2,5},{3,4},{4,3},{5,2},{6,1},{7,0},{8,15},{9,14},{10,... | collective-permute-start | bytes 393224 | tf_op jit(solution)/shard_map/ppermute | solution.py:311
  43.1 15.4 %collective-permute-start.17 = (f32[4,16,512]{2,1,0:T(8,128)S(1)}, f32[4,16,512]{2,1,0:T(8,128)S(1)}, u32[]{:S(2)}, u32[]{:S(2)}) collective-permute-start(f32[4,16,512]{2,1,0:T(8,128)S(1)} %get-tuple-element.171), channel_id=1, source_target_pairs={{0,4},{1,5},{2,6},{3,7},{4,0},{5,1},{6,2},{7,3},{8,12},{9,13},{10,... | collective-permute-start | bytes 393224 | tf_op jit(solution)/shard_map/ppermute | solution.py:311
  47.6 11.7 %collective-permute-start.18 = (f32[4,16,512]{2,1,0:T(8,128)S(1)}, f32[4,16,512]{2,1,0:T(8,128)S(1)}, u32[]{:S(2)}, u32[]{:S(2)}) collective-permute-start(f32[4,16,512]{2,1,0:T(8,128)S(1)} %get-tuple-element.173), channel_id=1, source_target_pairs={{0,1},{1,0},{2,3},{3,2},{4,5},{5,4},{6,7},{7,6},{8,9},{9,8},{10,11... | collective-permute-start | bytes 393224 | tf_op jit(solution)/shard_map/ppermute | solution.py:311
  47.7 13.6 %collective-permute-start.19 = (f32[4,16,512]{2,1,0:T(8,128)S(1)}, f32[4,16,512]{2,1,0:T(8,128)S(1)}, u32[]{:S(2)}, u32[]{:S(2)}) collective-permute-start(f32[4,16,512]{2,1,0:T(8,128)S(1)} %get-tuple-element.175), channel_id=1, source_target_pairs={{0,5},{1,4},{2,7},{3,6},{4,1},{5,0},{6,3},{7,2},{8,13},{9,12},{10,... | collective-permute-start | bytes 393224 | tf_op jit(solution)/shard_map/ppermute | solution.py:311
  50.1 17.3 %collective-permute-start.20 = (f32[16,16,128]{2,1,0:T(8,128)S(1)}, f32[16,16,128]{2,1,0:T(8,128)S(1)}, u32[]{:S(2)}, u32[]{:S(2)}) collective-permute-start(f32[16,16,128]{2,1,0:T(8,128)S(1)} %get-tuple-element.177), channel_id=1, source_target_pairs={{0,8},{8,0},{16,24},{24,16},{1,9},{9,1},{17,25},{25,17},{2,10},{10... | collective-permute-start | bytes 393224 | tf_op jit(solution)/shard_map/ppermute | solution.py:311
  57.5 11.3 %collective-permute-start.21 = (f32[4,16,512]{2,1,0:T(8,128)S(1)}, f32[4,16,512]{2,1,0:T(8,128)S(1)}, u32[]{:S(2)}, u32[]{:S(2)}) collective-permute-start(f32[4,16,512]{2,1,0:T(8,128)S(1)} %get-tuple-element.179), channel_id=1, source_target_pairs={{0,2},{1,3},{2,0},{3,1},{4,6},{5,7},{6,4},{7,5},{8,10},{9,11},{10,... | collective-permute-start | bytes 393224 | tf_op jit(solution)/shard_map/ppermute | solution.py:311
  58.5 10.8 %collective-permute-start.22 = (f32[4,16,512]{2,1,0:T(8,128)S(1)}, f32[4,16,512]{2,1,0:T(8,128)S(1)}, u32[]{:S(2)}, u32[]{:S(2)}) collective-permute-start(f32[4,16,512]{2,1,0:T(8,128)S(1)} %get-tuple-element.181), channel_id=1, source_target_pairs={{0,6},{1,7},{2,4},{3,5},{4,2},{5,3},{6,0},{7,1},{8,14},{9,15},{10,... | collective-permute-start | bytes 393224 | tf_op jit(solution)/shard_map/ppermute | solution.py:311
  59.4 10.4 %collective-permute-start.23 = (f32[16,16,128]{2,1,0:T(8,128)S(1)}, f32[16,16,128]{2,1,0:T(8,128)S(1)}, u32[]{:S(2)}, u32[]{:S(2)}) collective-permute-start(f32[16,16,128]{2,1,0:T(8,128)S(1)} %get-tuple-element.183), channel_id=1, source_target_pairs={{0,16},{8,24},{16,0},{24,8},{1,17},{9,25},{17,1},{25,9},{2,18},{10... | collective-permute-start | bytes 393224 | tf_op jit(solution)/shard_map/ppermute | solution.py:311
  61.3 11.3 %collective-permute-start.24 = (f32[4,16,512]{2,1,0:T(8,128)S(1)}, f32[4,16,512]{2,1,0:T(8,128)S(1)}, u32[]{:S(2)}, u32[]{:S(2)}) collective-permute-start(f32[4,16,512]{2,1,0:T(8,128)S(1)} %get-tuple-element.185), channel_id=1, source_target_pairs={{0,3},{1,2},{2,1},{3,0},{4,7},{5,6},{6,5},{7,4},{8,11},{9,10},{10,... | collective-permute-start | bytes 393224 | tf_op jit(solution)/shard_map/ppermute | solution.py:311
  67.5 11.7 %collective-permute-start.25 = (f32[4,16,512]{2,1,0:T(8,128)S(1)}, f32[4,16,512]{2,1,0:T(8,128)S(1)}, u32[]{:S(2)}, u32[]{:S(2)}) collective-permute-start(f32[4,16,512]{2,1,0:T(8,128)S(1)} %get-tuple-element.187), channel_id=1, source_target_pairs={{0,7},{1,6},{2,5},{3,4},{4,3},{5,2},{6,1},{7,0},{8,15},{9,14},{10,... | collective-permute-start | bytes 393224 | tf_op jit(solution)/shard_map/ppermute | solution.py:311
  68.8 10.3 %collective-permute-start.26 = (f32[16,16,128]{2,1,0:T(8,128)S(1)}, f32[16,16,128]{2,1,0:T(8,128)S(1)}, u32[]{:S(2)}, u32[]{:S(2)}) collective-permute-start(f32[16,16,128]{2,1,0:T(8,128)S(1)} %get-tuple-element.189), channel_id=1, source_target_pairs={{0,24},{8,16},{16,8},{24,0},{1,25},{9,17},{17,9},{25,1},{2,26},{10... | collective-permute-start | bytes 393224 | tf_op jit(solution)/shard_map/ppermute | solution.py:311
  69.3 13.1 %collective-permute-start.27 = (f32[4,16,512]{2,1,0:T(8,128)S(1)}, f32[4,16,512]{2,1,0:T(8,128)S(1)}, u32[]{:S(2)}, u32[]{:S(2)}) collective-permute-start(f32[4,16,512]{2,1,0:T(8,128)S(1)} %get-tuple-element.191), channel_id=1, source_target_pairs={{0,1},{1,0},{2,3},{3,2},{4,5},{5,4},{6,7},{7,6},{8,9},{9,8},{10,11... | collective-permute-start | bytes 393224 | tf_op jit(solution)/shard_map/ppermute | solution.py:311
  69.8 13.8 %collective-permute-start.28 = (f32[4,16,512]{2,1,0:T(8,128)S(1)}, f32[4,16,512]{2,1,0:T(8,128)S(1)}, u32[]{:S(2)}, u32[]{:S(2)}) collective-permute-start(f32[4,16,512]{2,1,0:T(8,128)S(1)} %get-tuple-element.193), channel_id=1, source_target_pairs={{0,4},{1,5},{2,6},{3,7},{4,0},{5,1},{6,2},{7,3},{8,12},{9,13},{10,... | collective-permute-start | bytes 393224 | tf_op jit(solution)/shard_map/ppermute | solution.py:311
  72.6 15.2 %collective-permute-start.33 = (f32[4,16,512]{2,1,0:T(8,128)S(1)}, f32[4,16,512]{2,1,0:T(8,128)S(1)}, u32[]{:S(2)}, u32[]{:S(2)}) collective-permute-start(f32[4,16,512]{2,1,0:T(8,128)S(1)} %get-tuple-element.202), channel_id=1, source_target_pairs={{0,2},{1,3},{2,0},{3,1},{4,6},{5,7},{6,4},{7,5},{8,10},{9,11},{10,... | collective-permute-start | bytes 393224 | tf_op jit(solution)/shard_map/ppermute | solution.py:311
  79.1 9.3 %collective-permute-start.32 = (f32[4,16,512]{2,1,0:T(8,128)S(1)}, f32[4,16,512]{2,1,0:T(8,128)S(1)}, u32[]{:S(2)}, u32[]{:S(2)}) collective-permute-start(f32[4,16,512]{2,1,0:T(8,128)S(1)} %get-tuple-element.201), channel_id=1, source_target_pairs={{0,5},{1,4},{2,7},{3,6},{4,1},{5,0},{6,3},{7,2},{8,13},{9,12},{10,... | collective-permute-start | bytes 393224 | tf_op jit(solution)/shard_map/ppermute | solution.py:311
  79.2 12.0 %collective-permute-start.31 = (f32[4,16,512]{2,1,0:T(8,128)S(1)}, f32[4,16,512]{2,1,0:T(8,128)S(1)}, u32[]{:S(2)}, u32[]{:S(2)}) collective-permute-start(f32[4,16,512]{2,1,0:T(8,128)S(1)} %get-tuple-element.200), channel_id=1, source_target_pairs={{0,3},{1,2},{2,1},{3,0},{4,7},{5,6},{6,5},{7,4},{8,11},{9,10},{10,... | collective-permute-start | bytes 393224 | tf_op jit(solution)/shard_map/ppermute | solution.py:311
  82.4 12.2 %collective-permute-start.30 = (f32[4,16,512]{2,1,0:T(8,128)S(1)}, f32[4,16,512]{2,1,0:T(8,128)S(1)}, u32[]{:S(2)}, u32[]{:S(2)}) collective-permute-start(f32[4,16,512]{2,1,0:T(8,128)S(1)} %get-tuple-element.199), channel_id=1, source_target_pairs={{0,6},{1,7},{2,4},{3,5},{4,2},{5,3},{6,0},{7,1},{8,14},{9,15},{10,... | collective-permute-start | bytes 393224 | tf_op jit(solution)/shard_map/ppermute | solution.py:311
  83.5 14.5 %collective-permute-start.29 = (f32[4,16,512]{2,1,0:T(8,128)S(1)}, f32[4,16,512]{2,1,0:T(8,128)S(1)}, u32[]{:S(2)}, u32[]{:S(2)}) collective-permute-start(f32[4,16,512]{2,1,0:T(8,128)S(1)} %get-tuple-element.194), channel_id=1, source_target_pairs={{0,7},{1,6},{2,5},{3,4},{4,3},{5,2},{6,1},{7,0},{8,15},{9,14},{10,... | collective-permute-start | bytes 393224 | tf_op jit(solution)/shard_map/ppermute | solution.py:311

commit v4 on v3

--- a/solution.py
+++ b/solution.py
@@ -38,6 +38,10 @@
 def properties(level_set):
     heavy = 0.5 * (1.0 + jnp.tanh(level_set / interface_width))
     return (0.2 + 0.8 * heavy, 0.25 + 0.75 * heavy)
+
+
+def in_hbm(*arrays):
+    return [pltpu.with_memory_space_constraint(x, pltpu.HBM) for x in arrays]
 
 
 def pack_kernel(steps, planes, velocity, level_set, *refs):
@@ -66,10 +70,10 @@
         in_specs=[hbm] * 2 + [whole] * len(after),
         out_specs=(pl.BlockSpec(memory_space=pltpu.VMEM),) * len(steps),
         scratch_shapes=[pltpu.SemaphoreType.DMA((len(steps), 2))],
-        compiler_params=pltpu.CompilerParams(vmem_limit_bytes=(4 if after else 61) * mebibyte),
+        compiler_params=pltpu.CompilerParams(vmem_limit_bytes=4 * mebibyte),
         cost_estimate=no_cost,
         name="pack",
-    )(velocity, level_set, *after)
+    )(*in_hbm(velocity, level_set), *after)
 
 
 def split(value):
@@ -202,7 +206,7 @@
         compiler_params=pltpu.CompilerParams(vmem_limit_bytes=6 * mebibyte),
         cost_estimate=no_cost,
         name="panels",
-    )(level_set, after)
+    )(*in_hbm(level_set), after)
 
 
 def z_lines_kernel(count, tables, *refs):
@@ -276,7 +280,7 @@
         compiler_params=pltpu.CompilerParams(vmem_limit_bytes=16 * mebibyte),
         cost_estimate=no_cost,
         name="prepare",
-    )(dx, level_set, velocity, *parts)
+    )(dx, *in_hbm(level_set, velocity), *parts)
 
 
 def gate_kernel(*refs):
@@ -304,10 +308,10 @@
         self.arrived = []
         self.token = jnp.zeros((8, 128), jnp.float32)
 
-    def send(self, piece, axis, step):
+    def send(self, piece, axis, step, after=()):
         count = lax.axis_size(axis)
         if len(self.arrived) >= flight:
-            (piece,), self.token = gate([piece], self.token, [self.arrived[-flight]])
+            (piece,), self.token = gate([piece], self.token, [self.arrived[-flight], *after])
         got = lax.ppermute(piece, axis, [(i, i ^ step) for i in range(count)])
         self.arrived.append(got)
         return got
@@ -355,40 +359,54 @@
     )
 
     order = message_order(count, planes, group_count)
-    first = [(0, step) for kind, chunk, step in order if kind == "out" and chunk == 0]
-    first = [piece for piece in first if piece[1] >= count // 2][:2]
-    rest = [(c, step) for c in range(planes) for step in range(count) if (c, step) not in first]
-    sent = dict(zip(first, pack(velocity, level_set, first, planes)))
-    sent.update(zip(rest, pack(velocity, level_set, rest, planes, [sent[p] for p in first])))
+    leaving = [(chunk, step) for kind, chunk, step in order if kind == "out"]
+    own = [(chunk, 0) for chunk in range(planes)]
+    sent, packed = {}, []
+    for steps in (leaving[:1], own + leaving[1:flight], leaving[flight:]):
+        if not steps:
+            continue
+        packed = pack(velocity, level_set, steps, planes, packed)
+        sent.update(zip(steps, packed))
 
     line = Line()
-    arrived = {(c, 0): sent[c, 0] for c in range(planes)}
+    arrived = {place: sent[place] for place in own}
     result, returned = {}, {}
     panel, z_arrived, z_result, z_returned = None, {}, None, {}
-    for kind, chunk, step in order:
+
+    def plane(chunk):
+        if chunk not in result:
+            result[chunk] = on_plane([arrived[chunk, i] for i in range(count)], dx, dy)
+            returned[chunk, 0] = result[chunk][0]
+
+    for place, (kind, chunk, step) in enumerate(order):
+        after = ()
+        if place + flight < len(order):
+            ahead, coming, _ = order[place + flight]
+            known = all((coming, i) in arrived for i in range(count))
+            if ahead == "back" and coming > 0 and coming not in result and known:
+                plane(coming)
+                after = result[coming][:1]
         if kind == "out":
-            arrived[chunk, step] = line.send(sent[chunk, step], "wide", step)
+            arrived[chunk, step] = line.send(sent[chunk, step], "wide", step, after)
         elif kind == "back":
-            if chunk not in result:
-                result[chunk] = on_plane([arrived[chunk, i] for i in range(count)], dx, dy)
-                returned[chunk, 0] = result[chunk][0]
-            returned[chunk, step] = line.send(result[chunk][step], "wide", step)
+            plane(chunk)
+            returned[chunk, step] = line.send(result[chunk][step], "wide", step, after)
         elif kind == "z_out":
             if panel is None:
                 panel = panels(level_set, line.arrived[0], group_count)
                 z_arrived[0] = panel[0]
-            z_arrived[step] = line.send(panel[step], "grp", step)
+            z_arrived[step] = line.send(panel[step], "grp", step, after)
         else:
             if z_result is None:
                 z_result = z_lines(tables, [z_arrived[i] for i in range(group_count)])
                 z_returned[0] = z_result[0]
-            z_returned[step] = line.send(z_result[step], "grp", step)
+            z_returned[step] = line.send(z_result[step], "grp", step, after)
 
     fields = prepare(dx, level_set, velocity, [z_returned[i] for i in range(group_count)])
     total = None
     early = [(c, i) for c in range(planes - 1) for i in range(count)] + [(planes - 1, 0)]
     late = [(c, step) for kind, c, step in order if kind == "back" and c == planes - 1]
-    for steps in [early] + [[piece] for piece in late]:
+    for steps in [early] + [[piece] for piece in late[:-3]] + [late[-3:]]:
         total = join(steps, [returned[piece] for piece in steps], fields, planes, total)
     return total
 

time: 98.8 us -> 96.5 us (0.977)
  waiting for transfers between devices: 26.9 us -> 18.3 us
  starting transfers between devices: 55.5 us -> 61.2 us
  Pallas kernels: 15 us -> 16.2 us
    ppermute x34, waiting for transfers between devices: 26.9 us -> 18.3 us  [send(): got = lax.ppermute(piece, axis, [(i, i ^ step) for i in range(count)])]
    ppermute x34, starting transfers between devices: 55.5 us -> 61.2 us  [send(): got = lax.ppermute(piece, axis, [(i, i ^ step) for i in range(count)])]
    pallas_call x8 -> x6, Pallas kernels: 5.67 us -> 4.43 us  [join(): pl.pallas_call(functools.partial(join_kernel, steps, planes), out_shape=j...]
    pallas_call x1, Pallas kernels: 0.86 us -> 1.98 us  [prepare(): pl.pallas_call(functools.partial(prepare_kernel, len(parts)), out_shape=(...]
    pallas_call x1, Pallas kernels: 0.25 us -> 1.25 us  [panels(): pl.pallas_call(functools.partial(panel_kernel, count), out_shape=(jax.Sha...]
    pallas_call x2 -> x3, Pallas kernels: 3.39 us -> 3.69 us  [pack(): pl.pallas_call(functools.partial(pack_kernel, steps, planes), out_shape=(...]
  transfers between devices with their start and end apart: 34 -> 34, of which waited for: 11 -> 10; matrix products, arithmetic and copies ran while one was open for 0% -> 0% of each run, Pallas kernels for 13% -> 15%
where the time goes in v4:
time: 96.5 us; the launch traced here: 96 us
  starting transfers between devices  61.2 us (63%)
  waiting for transfers between devices  18.3 us (19%)
  Pallas kernels  16.2 us (17%)
    ppermute x34, starting transfers between devices, send(): got = lax.ppermute(piece, axis, [(i, i ^ step) for i in range(count)])  61.2 us
    ppermute x34, waiting for transfers between devices, send(): got = lax.ppermute(piece, axis, [(i, i ^ step) for i in range(count)])  18.3 us
    pallas_call x6, Pallas kernels, join(): pl.pallas_call(functools.partial(join_kernel, steps, planes), out_shape=j...  4.43 us
    pallas_call x2, Pallas kernels, on_plane(): pl.pallas_call(functools.partial(plane_kernel, count), out_shape=(jax.Sha...  3.94 us
    pallas_call x3, Pallas kernels, pack(): pl.pallas_call(functools.partial(pack_kernel, steps, planes), out_shape=(...  3.69 us
    pallas_call x1, Pallas kernels, prepare(): pl.pallas_call(functools.partial(prepare_kernel, len(parts)), out_shape=(...  1.98 us
  transfers between devices with their start and end apart: 34, of which 10 were waited for; matrix products, arithmetic and copies ran while one was open for 0% of the time, Pallas kernels for 15%

profile of v4, /device:TPU:8, one launch (start us, length us, event | category | flops | bytes accessed | tf_op | source)
XLA Modules:
  0.0 96.0 jit_solution(17143954603399313680)
XLA Ops:
  0.0 0.9 pack.3.refs_0_
  0.9 2.7 %collective-permute-start = (f32[4,16,512]{2,1,0:T(8,128)S(1)}, f32[4,16,512]{2,1,0:T(8,128)S(1)}, u32[]{:S(2)}, u32[]{:S(2)}) collective-permute-start(f32[4,16,512]{2,1,0:T(8,128)S(1)} %pack.3.refs_0_), channel_id=1, source_target_pairs={{0,4},{1,5},{2,6},{3,7},{4,0},{5,1},{6,2},{7,3},{8,12},{9,13},{10,... | collective-permute-start | bytes 393224 | tf_op jit(solution)/shard_map/ppermute | solution.py:315
  3.6 1.3 %pack.4 = (f32[4,16,512]{2,1,0:T(8,128)S(1)}, f32[4,16,512]{2,1,0:T(8,128)S(1)}, f32[4,16,512]{2,1,0:T(8,128)S(1)}, f32[4,16,512]{2,1,0:T(8,128)S(1)}, f32[4,16,...) custom-call(f32[3,16,16,512]{3,2,1,0:T(8,128)} %velocity.7, f32[16,16,512]{2,1,0:T(8,128)} %level_set.9, ...), custom_call_target="tpu_custom_call" | custom-call | tf_op jit(solution)/shard_map/pack/pallas_call | solution.py:67
  4.9 1.6 %collective-permute-start.1 = (f32[4,16,512]{2,1,0:T(8,128)S(1)}, f32[4,16,512]{2,1,0:T(8,128)S(1)}, u32[]{:S(2)}, u32[]{:S(2)}) collective-permute-start(f32[4,16,512]{2,1,0:T(8,128)S(1)} %get-tuple-element.106.refs_2_), channel_id=1, source_target_pairs={{0,1},{1,0},{2,3},{3,2},{4,5},{5,4},{6,7},{7,6},{8,9},{9,8},{10,11... | collective-permute-start | bytes 393224 | tf_op jit(solution)/shard_map/ppermute | solution.py:315
  6.5 0.3 collective-permute-start.2
  6.9 3.0 %collective-permute-start.4 = (f32[4,16,512]{2,1,0:T(8,128)S(1)}, f32[4,16,512]{2,1,0:T(8,128)S(1)}, u32[]{:S(2)}, u32[]{:S(2)}) collective-permute-start(f32[4,16,512]{2,1,0:T(8,128)S(1)} %get-tuple-element.109.refs_5_), channel_id=1, source_target_pairs={{0,6},{1,7},{2,4},{3,5},{4,2},{5,3},{6,0},{7,1},{8,14},{9,15},{10,... | collective-permute-start | bytes 393224 | tf_op jit(solution)/shard_map/ppermute | solution.py:315
  9.9 1.5 %pack.5 = (f32[4,16,512]{2,1,0:T(8,128)S(1)}, f32[4,16,512]{2,1,0:T(8,128)S(1)}, f32[4,16,512]{2,1,0:T(8,128)S(1)}, f32[4,16,512]{2,1,0:T(8,128)S(1)}, f32[4,16,...) custom-call(f32[3,16,16,512]{3,2,1,0:T(8,128)} %velocity.7, ...), custom_call_target="tpu_custom_call" | custom-call | tf_op jit(solution)/shard_map/pack/pallas_call | solution.py:67
  11.4 1.6 %collective-permute-done.after.refs_2_.refs_4_ = f32[4,16,512]{2,1,0:T(8,128)S(1)} collective-permute-done((f32[4,16,512]{2,1,0:T(8,128)S(1)}, f32[4,16,512]{2,1,0:T(8,128)S(1)}, u32[]{:S(2)}, u32[]{:S(2)}) %collective-permute-start) | collective-permute-done | bytes 131104 | tf_op jit(solution)/shard_map/ppermute | solution.py:315
  13.0 0.8 collective-permute-start.6
  13.8 6.0 %collective-permute-start.7 = (f32[4,16,512]{2,1,0:T(8,128)S(1)}, f32[4,16,512]{2,1,0:T(8,128)S(1)}, u32[]{:S(2)}, u32[]{:S(2)}) collective-permute-start(f32[4,16,512]{2,1,0:T(8,128)S(1)} %get-tuple-element.126), channel_id=1, source_target_pairs={{0,7},{1,6},{2,5},{3,4},{4,3},{5,2},{6,1},{7,0},{8,15},{9,14},{10,... | collective-permute-start | bytes 393224 | tf_op jit(solution)/shard_map/ppermute | solution.py:315
  19.8 1.3 %panels.1 = (f32[16,16,128]{2,1,0:T(8,128)S(1)}, f32[16,16,128]{2,1,0:T(8,128)S(1)}, f32[16,16,128]{2,1,0:T(8,128)S(1)}, f32[16,16,128]{2,1,0:T(8,128)S(1)}) custom-call(f32[16,16,512]{2,1,0:T(8,128)} %level_set.9, f32[4,16,512]{2,1,0:T(8,128)S(1)} %collective-permute-done.after.refs_2_.refs_4_), custom_call_target="tpu_custom_call" | custom-call | tf_op jit(solution)/shard_map/panels/pallas_call | solution.py:200
  21.1 4.8 %collective-permute-start.10 = (f32[4,16,512]{2,1,0:T(8,128)S(1)}, f32[4,16,512]{2,1,0:T(8,128)S(1)}, u32[]{:S(2)}, u32[]{:S(2)}) collective-permute-start(f32[4,16,512]{2,1,0:T(8,128)S(1)} %get-tuple-element.134), channel_id=1, source_target_pairs={{0,4},{1,5},{2,6},{3,7},{4,0},{5,1},{6,2},{7,3},{8,12},{9,13},{10,... | collective-permute-start | bytes 393224 | tf_op jit(solution)/shard_map/ppermute | solution.py:315
  25.9 1.6 %collective-permute-start.5 = (f32[4,16,512]{2,1,0:T(8,128)S(1)}, f32[4,16,512]{2,1,0:T(8,128)S(1)}, u32[]{:S(2)}, u32[]{:S(2)}) collective-permute-start(f32[4,16,512]{2,1,0:T(8,128)S(1)} %get-tuple-element.119), channel_id=1, source_target_pairs={{0,1},{1,0},{2,3},{3,2},{4,5},{5,4},{6,7},{7,6},{8,9},{9,8},{10,11... | collective-permute-start | bytes 393224 | tf_op jit(solution)/shard_map/ppermute | solution.py:315
  27.5 1.5 %collective-permute-start.11 = (f32[16,16,128]{2,1,0:T(8,128)S(1)}, f32[16,16,128]{2,1,0:T(8,128)S(1)}, u32[]{:S(2)}, u32[]{:S(2)}) collective-permute-start(f32[16,16,128]{2,1,0:T(8,128)S(1)} %get-tuple-element.137), channel_id=1, source_target_pairs={{0,16},{8,24},{16,0},{24,8},{1,17},{9,25},{17,1},{25,9},{2,18},{10... | collective-permute-start | bytes 393224 | tf_op jit(solution)/shard_map/ppermute | solution.py:315
  29.0 1.3 %collective-permute-done.7.refs_2_.refs_7_ = f32[4,16,512]{2,1,0:T(8,128)S(1)} collective-permute-done((f32[4,16,512]{2,1,0:T(8,128)S(1)}, f32[4,16,512]{2,1,0:T(8,128)S(1)}, u32[]{:S(2)}, u32[]{:S(2)}) %collective-permute-start.7) | collective-permute-done | bytes 131104 | tf_op jit(solution)/shard_map/ppermute | solution.py:315
  30.3 3.4 %collective-permute-start.9 = (f32[4,16,512]{2,1,0:T(8,128)S(1)}, f32[4,16,512]{2,1,0:T(8,128)S(1)}, u32[]{:S(2)}, u32[]{:S(2)}) collective-permute-start(f32[4,16,512]{2,1,0:T(8,128)S(1)} %get-tuple-element.129), channel_id=1, source_target_pairs={{0,2},{1,3},{2,0},{3,1},{4,6},{5,7},{6,4},{7,5},{8,10},{9,11},{10,... | collective-permute-start | bytes 393224 | tf_op jit(solution)/shard_map/ppermute | solution.py:315
  33.7 0.4 collective-permute-start.16
  34.1 4.3 %collective-permute-start.12 = (f32[4,16,512]{2,1,0:T(8,128)S(1)}, f32[4,16,512]{2,1,0:T(8,128)S(1)}, u32[]{:S(2)}, u32[]{:S(2)}) collective-permute-start(f32[4,16,512]{2,1,0:T(8,128)S(1)} %get-tuple-element.138), channel_id=1, source_target_pairs={{0,3},{1,2},{2,1},{3,0},{4,7},{5,6},{6,5},{7,4},{8,11},{9,10},{10,... | collective-permute-start | bytes 393224 | tf_op jit(solution)/shard_map/ppermute | solution.py:315
  38.5 1.9 %collective-permute-start.15 = (f32[4,16,512]{2,1,0:T(8,128)S(1)}, f32[4,16,512]{2,1,0:T(8,128)S(1)}, u32[]{:S(2)}, u32[]{:S(2)}) collective-permute-start(f32[4,16,512]{2,1,0:T(8,128)S(1)} %get-tuple-element.143), channel_id=1, source_target_pairs={{0,7},{1,6},{2,5},{3,4},{4,3},{5,2},{6,1},{7,0},{8,15},{9,14},{10,... | collective-permute-start | bytes 393224 | tf_op jit(solution)/shard_map/ppermute | solution.py:315
  40.4 2.0 %plane.3 = (f32[4,16,512]{2,1,0:T(8,128)S(1)}, f32[4,16,512]{2,1,0:T(8,128)S(1)}, f32[4,16,512]{2,1,0:T(8,128)S(1)}, f32[4,16,512]{2,1,0:T(8,128)S(1)}, f32[4,16...) custom-call(bf16[1536,512]{1,0:T(8,128)(2,1)S(1)} %copy-done, ...), custom_call_target="tpu_custom_call" | custom-call | tf_op jit(solution)/shard_map/plane/pallas_call | solution.py:132
  42.4 5.7 %collective-permute-start.17 = (f32[4,16,512]{2,1,0:T(8,128)S(1)}, f32[4,16,512]{2,1,0:T(8,128)S(1)}, u32[]{:S(2)}, u32[]{:S(2)}) collective-permute-start(f32[4,16,512]{2,1,0:T(8,128)S(1)} %get-tuple-element.167), channel_id=1, source_target_pairs={{0,4},{1,5},{2,6},{3,7},{4,0},{5,1},{6,2},{7,3},{8,12},{9,13},{10,... | collective-permute-start | bytes 393224 | tf_op jit(solution)/shard_map/ppermute | solution.py:315
  48.2 1.5 %collective-permute-start.19 = (f32[4,16,512]{2,1,0:T(8,128)S(1)}, f32[4,16,512]{2,1,0:T(8,128)S(1)}, u32[]{:S(2)}, u32[]{:S(2)}) collective-permute-start(f32[4,16,512]{2,1,0:T(8,128)S(1)} %get-tuple-element.172), channel_id=1, source_target_pairs={{0,5},{1,4},{2,7},{3,6},{4,1},{5,0},{6,3},{7,2},{8,13},{9,12},{10,... | collective-permute-start | bytes 393224 | tf_op jit(solution)/shard_map/ppermute | solution.py:315
  49.7 0.9 z_lines.1
  50.7 4.7 %collective-permute-done.15.refs_7_.refs_2_ = f32[4,16,512]{2,1,0:T(8,128)S(1)} collective-permute-done((f32[4,16,512]{2,1,0:T(8,128)S(1)}, f32[4,16,512]{2,1,0:T(8,128)S(1)}, u32[]{:S(2)}, u32[]{:S(2)}) %collective-permute-start.15) | collective-permute-done | bytes 131104 | tf_op jit(solution)/shard_map/ppermute | solution.py:315
  55.4 2.0 %plane.2 = (f32[4,16,512]{2,1,0:T(8,128)S(1)}, f32[4,16,512]{2,1,0:T(8,128)S(1)}, f32[4,16,512]{2,1,0:T(8,128)S(1)}, f32[4,16,512]{2,1,0:T(8,128)S(1)}, f32[4,16...) custom-call(bf16[1536,512]{1,0:T(8,128)(2,1)S(1)} %copy-done, ...), custom_call_target="tpu_custom_call" | custom-call | tf_op jit(solution)/shard_map/plane/pallas_call | solution.py:132
  57.4 2.2 %collective-permute-start.22 = (f32[4,16,512]{2,1,0:T(8,128)S(1)}, f32[4,16,512]{2,1,0:T(8,128)S(1)}, u32[]{:S(2)}, u32[]{:S(2)}) collective-permute-start(f32[4,16,512]{2,1,0:T(8,128)S(1)} %get-tuple-element.178), channel_id=1, source_target_pairs={{0,6},{1,7},{2,4},{3,5},{4,2},{5,3},{6,0},{7,1},{8,14},{9,15},{10,... | collective-permute-start | bytes 393224 | tf_op jit(solution)/shard_map/ppermute | solution.py:315
  59.6 1.5 %collective-permute-start.23 = (f32[16,16,128]{2,1,0:T(8,128)S(1)}, f32[16,16,128]{2,1,0:T(8,128)S(1)}, u32[]{:S(2)}, u32[]{:S(2)}) collective-permute-start(f32[16,16,128]{2,1,0:T(8,128)S(1)} %get-tuple-element.180), channel_id=1, source_target_pairs={{0,16},{8,24},{16,0},{24,8},{1,17},{9,25},{17,1},{25,9},{2,18},{10... | collective-permute-start | bytes 393224 | tf_op jit(solution)/shard_map/ppermute | solution.py:315
  61.1 3.2 %collective-permute-start.24 = (f32[4,16,512]{2,1,0:T(8,128)S(1)}, f32[4,16,512]{2,1,0:T(8,128)S(1)}, u32[]{:S(2)}, u32[]{:S(2)}) collective-permute-start(f32[4,16,512]{2,1,0:T(8,128)S(1)} %get-tuple-element.182), channel_id=1, source_target_pairs={{0,3},{1,2},{2,1},{3,0},{4,7},{5,6},{6,5},{7,4},{8,11},{9,10},{10,... | collective-permute-start | bytes 393224 | tf_op jit(solution)/shard_map/ppermute | solution.py:315
  64.4 1.2 %collective-permute-start.25 = (f32[4,16,512]{2,1,0:T(8,128)S(1)}, f32[4,16,512]{2,1,0:T(8,128)S(1)}, u32[]{:S(2)}, u32[]{:S(2)}) collective-permute-start(f32[4,16,512]{2,1,0:T(8,128)S(1)} %get-tuple-element.184), channel_id=1, source_target_pairs={{0,7},{1,6},{2,5},{3,4},{4,3},{5,2},{6,1},{7,0},{8,15},{9,14},{10,... | collective-permute-start | bytes 393224 | tf_op jit(solution)/shard_map/ppermute | solution.py:315
  65.6 0.2 collective-permute-done.21.refs_2_
  65.8 0.9 collective-permute-start.26
  66.7 0.4 collective-permute-done.22.refs_2_.refs_6_
  67.1 4.2 %collective-permute-start.30 = (f32[4,16,512]{2,1,0:T(8,128)S(1)}, f32[4,16,512]{2,1,0:T(8,128)S(1)}, u32[]{:S(2)}, u32[]{:S(2)}) collective-permute-start(f32[4,16,512]{2,1,0:T(8,128)S(1)} %get-tuple-element.194), channel_id=1, source_target_pairs={{0,4},{1,5},{2,6},{3,7},{4,0},{5,1},{6,2},{7,3},{8,12},{9,13},{10,... | collective-permute-start | bytes 393224 | tf_op jit(solution)/shard_map/ppermute | solution.py:315
  71.3 0.3 collective-permute-done.24.refs_2_.refs_3_
  71.6 2.3 %collective-permute-start.33 = (f32[4,16,512]{2,1,0:T(8,128)S(1)}, f32[4,16,512]{2,1,0:T(8,128)S(1)}, u32[]{:S(2)}, u32[]{:S(2)}) collective-permute-start(f32[4,16,512]{2,1,0:T(8,128)S(1)} %get-tuple-element.201), channel_id=1, source_target_pairs={{0,2},{1,3},{2,0},{3,1},{4,6},{5,7},{6,4},{7,5},{8,10},{9,11},{10,... | collective-permute-start | bytes 393224 | tf_op jit(solution)/shard_map/ppermute | solution.py:315
  74.0 1.9 %collective-permute-done.25.refs_2_.refs_7_ = f32[4,16,512]{2,1,0:T(8,128)S(1)} collective-permute-done((f32[4,16,512]{2,1,0:T(8,128)S(1)}, f32[4,16,512]{2,1,0:T(8,128)S(1)}, u32[]{:S(2)}, u32[]{:S(2)}) %collective-permute-start.25) | collective-permute-done | bytes 131104 | tf_op jit(solution)/shard_map/ppermute | solution.py:315
  75.9 3.0 %collective-permute-done.30.refs_2_.refs_0_ = f32[4,16,512]{2,1,0:T(8,128)S(1)} collective-permute-done((f32[4,16,512]{2,1,0:T(8,128)S(1)}, f32[4,16,512]{2,1,0:T(8,128)S(1)}, u32[]{:S(2)}, u32[]{:S(2)}) %collective-permute-start.30) | collective-permute-done | bytes 131104 | tf_op jit(solution)/shard_map/ppermute | solution.py:315
  78.9 1.4 %collective-permute-start.29 = (f32[4,16,512]{2,1,0:T(8,128)S(1)}, f32[4,16,512]{2,1,0:T(8,128)S(1)}, u32[]{:S(2)}, u32[]{:S(2)}) collective-permute-start(f32[4,16,512]{2,1,0:T(8,128)S(1)} %get-tuple-element.191), channel_id=1, source_target_pairs={{0,6},{1,7},{2,4},{3,5},{4,2},{5,3},{6,0},{7,1},{8,14},{9,15},{10,... | collective-permute-start | bytes 393224 | tf_op jit(solution)/shard_map/ppermute | solution.py:315
  80.3 4.5 %collective-permute-start.27 = (f32[4,16,512]{2,1,0:T(8,128)S(1)}, f32[4,16,512]{2,1,0:T(8,128)S(1)}, u32[]{:S(2)}, u32[]{:S(2)}) collective-permute-start(f32[4,16,512]{2,1,0:T(8,128)S(1)} %get-tuple-element.187), channel_id=1, source_target_pairs={{0,3},{1,2},{2,1},{3,0},{4,7},{5,6},{6,5},{7,4},{8,11},{9,10},{10,... | collective-permute-start | bytes 393224 | tf_op jit(solution)/shard_map/ppermute | solution.py:315
  84.8 2.0 %prepare.1 = (f32[16,16,512]{2,1,0:T(8,128)S(1)}, f32[16,16,512]{2,1,0:T(8,128)S(1)}, f32[16,16,512]{2,1,0:T(8,128)S(1)}) custom-call(bf16[1536,512]{1,0:T(8,128)(2,1)S(1)} %copy-done, f32[16,16,512]{2,1,0:T(8,128)} %level_set.9, f32[3,16,16,512]{3,2,1,0:T(8,128)} %velocity.7, f32[16,16,128]{2,1,0:T(8,128)S(1)} %get-tuple-element.196.refs_0_, ...), custom_call_target="tpu_custom_call" | custom-call | tf_op jit(solution)/shard_map/prepare/pallas_call | solution.py:271
  86.7 1.0 %join.6.refs_4_ = f32[3,16,16,512]{3,2,1,0:T(8,128)} custom-call(f32[4,16,512]{2,1,0:T(8,128)S(1)} %get-tuple-element.202.refs_0_, f32[4,16,512]{2,1,0:T(8,128)S(1)} %collective-permute-done.18.refs_2_.refs_1_, f32[4,16,512]{2,1,0:T(8,128)S(1)} %collective-permute-done.21.refs_2_, f32[4,16,512]{2,1,0:T(8,128)S(1)} %collective-permute-done.24.refs_2_.refs_3_, ...), custom_call_target="tpu_custom_call" | custom-call | flops 10000000 | tf_op jit(solution)/shard_map/join/pallas_call | solution.py:168
  87.7 0.7 join.7.refs_4_
  88.4 0.7 join.8.refs_4_
  89.1 0.7 join.9.refs_4_
  89.8 0.7 join.10.refs_6_
  90.5 3.1 %collective-permute-done.31.refs_2_ = f32[4,16,512]{2,1,0:T(8,128)S(1)} collective-permute-done((f32[4,16,512]{2,1,0:T(8,128)S(1)}, f32[4,16,512]{2,1,0:T(8,128)S(1)}, u32[]{:S(2)}, u32[]{:S(2)}) %collective-permute-start.31) | collective-permute-done | bytes 131104 | tf_op jit(solution)/shard_map/ppermute | solution.py:315
  93.6 1.7 %collective-permute-done.29.refs_1_ = f32[4,16,512]{2,1,0:T(8,128)S(1)} collective-permute-done((f32[4,16,512]{2,1,0:T(8,128)S(1)}, f32[4,16,512]{2,1,0:T(8,128)S(1)}, u32[]{:S(2)}, u32[]{:S(2)}) %collective-permute-start.29) | collective-permute-done | bytes 131104 | tf_op jit(solution)/shard_map/ppermute | solution.py:315
  95.3 0.7 join.11
  (70 shorter events, 0.5 us)
Async XLA Ops:
  0.9 12.1 %collective-permute-start = (f32[4,16,512]{2,1,0:T(8,128)S(1)}, f32[4,16,512]{2,1,0:T(8,128)S(1)}, u32[]{:S(2)}, u32[]{:S(2)}) collective-permute-start(f32[4,16,512]{2,1,0:T(8,128)S(1)} %pack.3.refs_0_), channel_id=1, source_target_pairs={{0,4},{1,5},{2,6},{3,7},{4,0},{5,1},{6,2},{7,3},{8,12},{9,13},{10,... | collective-permute-start | bytes 393224 | tf_op jit(solution)/shard_map/ppermute | solution.py:315
  4.9 8.9 %collective-permute-start.1 = (f32[4,16,512]{2,1,0:T(8,128)S(1)}, f32[4,16,512]{2,1,0:T(8,128)S(1)}, u32[]{:S(2)}, u32[]{:S(2)}) collective-permute-start(f32[4,16,512]{2,1,0:T(8,128)S(1)} %get-tuple-element.106.refs_2_), channel_id=1, source_target_pairs={{0,1},{1,0},{2,3},{3,2},{4,5},{5,4},{6,7},{7,6},{8,9},{9,8},{10,11... | collective-permute-start | bytes 393224 | tf_op jit(solution)/shard_map/ppermute | solution.py:315
  6.5 14.6 %collective-permute-start.2 = (f32[4,16,512]{2,1,0:T(8,128)S(1)}, f32[4,16,512]{2,1,0:T(8,128)S(1)}, u32[]{:S(2)}, u32[]{:S(2)}) collective-permute-start(f32[4,16,512]{2,1,0:T(8,128)S(1)} %get-tuple-element.107.refs_3_), channel_id=1, source_target_pairs={{0,5},{1,4},{2,7},{3,6},{4,1},{5,0},{6,3},{7,2},{8,13},{9,12},{10,... | collective-permute-start | bytes 393224 | tf_op jit(solution)/shard_map/ppermute | solution.py:315
  6.8 14.4 %collective-permute-start.3 = (f32[4,16,512]{2,1,0:T(8,128)S(1)}, f32[4,16,512]{2,1,0:T(8,128)S(1)}, u32[]{:S(2)}, u32[]{:S(2)}) collective-permute-start(f32[4,16,512]{2,1,0:T(8,128)S(1)} %get-tuple-element.108.refs_4_), channel_id=1, source_target_pairs={{0,2},{1,3},{2,0},{3,1},{4,6},{5,7},{6,4},{7,5},{8,10},{9,11},{10,... | collective-permute-start | bytes 393224 | tf_op jit(solution)/shard_map/ppermute | solution.py:315
  6.9 19.0 %collective-permute-start.4 = (f32[4,16,512]{2,1,0:T(8,128)S(1)}, f32[4,16,512]{2,1,0:T(8,128)S(1)}, u32[]{:S(2)}, u32[]{:S(2)}) collective-permute-start(f32[4,16,512]{2,1,0:T(8,128)S(1)} %get-tuple-element.109.refs_5_), channel_id=1, source_target_pairs={{0,6},{1,7},{2,4},{3,5},{4,2},{5,3},{6,0},{7,1},{8,14},{9,15},{10,... | collective-permute-start | bytes 393224 | tf_op jit(solution)/shard_map/ppermute | solution.py:315
  13.0 14.5 %collective-permute-start.6 = (f32[4,16,512]{2,1,0:T(8,128)S(1)}, f32[4,16,512]{2,1,0:T(8,128)S(1)}, u32[]{:S(2)}, u32[]{:S(2)}) collective-permute-start(f32[4,16,512]{2,1,0:T(8,128)S(1)} %get-tuple-element.124), channel_id=1, source_target_pairs={{0,3},{1,2},{2,1},{3,0},{4,7},{5,6},{6,5},{7,4},{8,11},{9,10},{10,... | collective-permute-start | bytes 393224 | tf_op jit(solution)/shard_map/ppermute | solution.py:315
  13.8 26.6 %copy-start = (bf16[1536,512]{1,0:T(8,128)(2,1)S(1)}, bf16[1536,512]{1,0:T(8,128)(2,1)}, u32[]{:S(2)}) copy-start(bf16[1536,512]{1,0:T(8,128)(2,1)} %constant.8.clone.dx) | copy-start | bytes 4718596
  13.8 26.6 %copy-start.1 = (bf16[128,384]{1,0:T(8,128)(2,1)S(1)}, bf16[128,384]{1,0:T(8,128)(2,1)}, u32[]{:S(2)}) copy-start(bf16[128,384]{1,0:T(8,128)(2,1)} %constant.9.clone.dy) | copy-start | bytes 294916
  13.8 16.5 %collective-permute-start.7 = (f32[4,16,512]{2,1,0:T(8,128)S(1)}, f32[4,16,512]{2,1,0:T(8,128)S(1)}, u32[]{:S(2)}, u32[]{:S(2)}) collective-permute-start(f32[4,16,512]{2,1,0:T(8,128)S(1)} %get-tuple-element.126), channel_id=1, source_target_pairs={{0,7},{1,6},{2,5},{3,4},{4,3},{5,2},{6,1},{7,0},{8,15},{9,14},{10,... | collective-permute-start | bytes 393224 | tf_op jit(solution)/shard_map/ppermute | solution.py:315
  21.0 9.2 %collective-permute-start.8 = (f32[16,16,128]{2,1,0:T(8,128)S(1)}, f32[16,16,128]{2,1,0:T(8,128)S(1)}, u32[]{:S(2)}, u32[]{:S(2)}) collective-permute-start(f32[16,16,128]{2,1,0:T(8,128)S(1)} %get-tuple-element.128), channel_id=1, source_target_pairs={{0,8},{8,0},{16,24},{24,16},{1,9},{9,1},{17,25},{25,17},{2,10},{10... | collective-permute-start | bytes 393224 | tf_op jit(solution)/shard_map/ppermute | solution.py:315
  21.1 12.6 %collective-permute-start.10 = (f32[4,16,512]{2,1,0:T(8,128)S(1)}, f32[4,16,512]{2,1,0:T(8,128)S(1)}, u32[]{:S(2)}, u32[]{:S(2)}) collective-permute-start(f32[4,16,512]{2,1,0:T(8,128)S(1)} %get-tuple-element.134), channel_id=1, source_target_pairs={{0,4},{1,5},{2,6},{3,7},{4,0},{5,1},{6,2},{7,3},{8,12},{9,13},{10,... | collective-permute-start | bytes 393224 | tf_op jit(solution)/shard_map/ppermute | solution.py:315
  25.9 8.2 %collective-permute-start.5 = (f32[4,16,512]{2,1,0:T(8,128)S(1)}, f32[4,16,512]{2,1,0:T(8,128)S(1)}, u32[]{:S(2)}, u32[]{:S(2)}) collective-permute-start(f32[4,16,512]{2,1,0:T(8,128)S(1)} %get-tuple-element.119), channel_id=1, source_target_pairs={{0,1},{1,0},{2,3},{3,2},{4,5},{5,4},{6,7},{7,6},{8,9},{9,8},{10,11... | collective-permute-start | bytes 393224 | tf_op jit(solution)/shard_map/ppermute | solution.py:315
  27.5 6.6 %collective-permute-start.11 = (f32[16,16,128]{2,1,0:T(8,128)S(1)}, f32[16,16,128]{2,1,0:T(8,128)S(1)}, u32[]{:S(2)}, u32[]{:S(2)}) collective-permute-start(f32[16,16,128]{2,1,0:T(8,128)S(1)} %get-tuple-element.137), channel_id=1, source_target_pairs={{0,16},{8,24},{16,0},{24,8},{1,17},{9,25},{17,1},{25,9},{2,18},{10... | collective-permute-start | bytes 393224 | tf_op jit(solution)/shard_map/ppermute | solution.py:315
  30.3 8.2 %collective-permute-start.13 = (f32[4,16,512]{2,1,0:T(8,128)S(1)}, f32[4,16,512]{2,1,0:T(8,128)S(1)}, u32[]{:S(2)}, u32[]{:S(2)}) collective-permute-start(f32[4,16,512]{2,1,0:T(8,128)S(1)} %get-tuple-element.139), channel_id=1, source_target_pairs={{0,5},{1,4},{2,7},{3,6},{4,1},{5,0},{6,3},{7,2},{8,13},{9,12},{10,... | collective-permute-start | bytes 393224 | tf_op jit(solution)/shard_map/ppermute | solution.py:315
  30.3 12.2 %collective-permute-start.9 = (f32[4,16,512]{2,1,0:T(8,128)S(1)}, f32[4,16,512]{2,1,0:T(8,128)S(1)}, u32[]{:S(2)}, u32[]{:S(2)}) collective-permute-start(f32[4,16,512]{2,1,0:T(8,128)S(1)} %get-tuple-element.129), channel_id=1, source_target_pairs={{0,2},{1,3},{2,0},{3,1},{4,6},{5,7},{6,4},{7,5},{8,10},{9,11},{10,... | collective-permute-start | bytes 393224 | tf_op jit(solution)/shard_map/ppermute | solution.py:315
  33.7 14.4 %collective-permute-start.16 = (f32[16,16,128]{2,1,0:T(8,128)S(1)}, f32[16,16,128]{2,1,0:T(8,128)S(1)}, u32[]{:S(2)}, u32[]{:S(2)}) collective-permute-start(f32[16,16,128]{2,1,0:T(8,128)S(1)} %get-tuple-element.150), channel_id=1, source_target_pairs={{0,24},{8,16},{16,8},{24,0},{1,25},{9,17},{17,9},{25,1},{2,26},{10... | collective-permute-start | bytes 393224 | tf_op jit(solution)/shard_map/ppermute | solution.py:315
  34.1 14.1 %collective-permute-start.14 = (f32[4,16,512]{2,1,0:T(8,128)S(1)}, f32[4,16,512]{2,1,0:T(8,128)S(1)}, u32[]{:S(2)}, u32[]{:S(2)}) collective-permute-start(f32[4,16,512]{2,1,0:T(8,128)S(1)} %get-tuple-element.140), channel_id=1, source_target_pairs={{0,6},{1,7},{2,4},{3,5},{4,2},{5,3},{6,0},{7,1},{8,14},{9,15},{10,... | collective-permute-start | bytes 393224 | tf_op jit(solution)/shard_map/ppermute | solution.py:315
  34.1 16.5 %collective-permute-start.12 = (f32[4,16,512]{2,1,0:T(8,128)S(1)}, f32[4,16,512]{2,1,0:T(8,128)S(1)}, u32[]{:S(2)}, u32[]{:S(2)}) collective-permute-start(f32[4,16,512]{2,1,0:T(8,128)S(1)} %get-tuple-element.138), channel_id=1, source_target_pairs={{0,3},{1,2},{2,1},{3,0},{4,7},{5,6},{6,5},{7,4},{8,11},{9,10},{10,... | collective-permute-start | bytes 393224 | tf_op jit(solution)/shard_map/ppermute | solution.py:315
  38.5 11.2 %copy-start.2 = (f32[4,64,64]{2,1,0:T(8,128)S(1)}, f32[4,64,64]{2,1,0:T(8,128)}, u32[]{:S(2)}) copy-start(f32[4,64,64]{2,1,0:T(8,128)} %constant.10.clone.tables) | copy-start | bytes 196612
  38.5 17.0 %collective-permute-start.15 = (f32[4,16,512]{2,1,0:T(8,128)S(1)}, f32[4,16,512]{2,1,0:T(8,128)S(1)}, u32[]{:S(2)}, u32[]{:S(2)}) collective-permute-start(f32[4,16,512]{2,1,0:T(8,128)S(1)} %get-tuple-element.143), channel_id=1, source_target_pairs={{0,7},{1,6},{2,5},{3,4},{4,3},{5,2},{6,1},{7,0},{8,15},{9,14},{10,... | collective-permute-start | bytes 393224 | tf_op jit(solution)/shard_map/ppermute | solution.py:315
  42.4 15.0 %collective-permute-start.17 = (f32[4,16,512]{2,1,0:T(8,128)S(1)}, f32[4,16,512]{2,1,0:T(8,128)S(1)}, u32[]{:S(2)}, u32[]{:S(2)}) collective-permute-start(f32[4,16,512]{2,1,0:T(8,128)S(1)} %get-tuple-element.167), channel_id=1, source_target_pairs={{0,4},{1,5},{2,6},{3,7},{4,0},{5,1},{6,2},{7,3},{8,12},{9,13},{10,... | collective-permute-start | bytes 393224 | tf_op jit(solution)/shard_map/ppermute | solution.py:315
  48.1 11.5 %collective-permute-start.18 = (f32[4,16,512]{2,1,0:T(8,128)S(1)}, f32[4,16,512]{2,1,0:T(8,128)S(1)}, u32[]{:S(2)}, u32[]{:S(2)}) collective-permute-start(f32[4,16,512]{2,1,0:T(8,128)S(1)} %get-tuple-element.170), channel_id=1, source_target_pairs={{0,1},{1,0},{2,3},{3,2},{4,5},{5,4},{6,7},{7,6},{8,9},{9,8},{10,11... | collective-permute-start | bytes 393224 | tf_op jit(solution)/shard_map/ppermute | solution.py:315
  48.2 13.0 %collective-permute-start.19 = (f32[4,16,512]{2,1,0:T(8,128)S(1)}, f32[4,16,512]{2,1,0:T(8,128)S(1)}, u32[]{:S(2)}, u32[]{:S(2)}) collective-permute-start(f32[4,16,512]{2,1,0:T(8,128)S(1)} %get-tuple-element.172), channel_id=1, source_target_pairs={{0,5},{1,4},{2,7},{3,6},{4,1},{5,0},{6,3},{7,2},{8,13},{9,12},{10,... | collective-permute-start | bytes 393224 | tf_op jit(solution)/shard_map/ppermute | solution.py:315
  50.6 13.7 %collective-permute-start.20 = (f32[16,16,128]{2,1,0:T(8,128)S(1)}, f32[16,16,128]{2,1,0:T(8,128)S(1)}, u32[]{:S(2)}, u32[]{:S(2)}) collective-permute-start(f32[16,16,128]{2,1,0:T(8,128)S(1)} %get-tuple-element.174), channel_id=1, source_target_pairs={{0,8},{8,0},{16,24},{24,16},{1,9},{9,1},{17,25},{25,17},{2,10},{10... | collective-permute-start | bytes 393224 | tf_op jit(solution)/shard_map/ppermute | solution.py:315
  55.4 10.4 %collective-permute-start.21 = (f32[4,16,512]{2,1,0:T(8,128)S(1)}, f32[4,16,512]{2,1,0:T(8,128)S(1)}, u32[]{:S(2)}, u32[]{:S(2)}) collective-permute-start(f32[4,16,512]{2,1,0:T(8,128)S(1)} %get-tuple-element.176), channel_id=1, source_target_pairs={{0,2},{1,3},{2,0},{3,1},{4,6},{5,7},{6,4},{7,5},{8,10},{9,11},{10,... | collective-permute-start | bytes 393224 | tf_op jit(solution)/shard_map/ppermute | solution.py:315
  57.4 9.7 %collective-permute-start.22 = (f32[4,16,512]{2,1,0:T(8,128)S(1)}, f32[4,16,512]{2,1,0:T(8,128)S(1)}, u32[]{:S(2)}, u32[]{:S(2)}) collective-permute-start(f32[4,16,512]{2,1,0:T(8,128)S(1)} %get-tuple-element.178), channel_id=1, source_target_pairs={{0,6},{1,7},{2,4},{3,5},{4,2},{5,3},{6,0},{7,1},{8,14},{9,15},{10,... | collective-permute-start | bytes 393224 | tf_op jit(solution)/shard_map/ppermute | solution.py:315
  59.6 7.5 %collective-permute-start.23 = (f32[16,16,128]{2,1,0:T(8,128)S(1)}, f32[16,16,128]{2,1,0:T(8,128)S(1)}, u32[]{:S(2)}, u32[]{:S(2)}) collective-permute-start(f32[16,16,128]{2,1,0:T(8,128)S(1)} %get-tuple-element.180), channel_id=1, source_target_pairs={{0,16},{8,24},{16,0},{24,8},{1,17},{9,25},{17,1},{25,9},{2,18},{10... | collective-permute-start | bytes 393224 | tf_op jit(solution)/shard_map/ppermute | solution.py:315
  61.1 10.5 %collective-permute-start.24 = (f32[4,16,512]{2,1,0:T(8,128)S(1)}, f32[4,16,512]{2,1,0:T(8,128)S(1)}, u32[]{:S(2)}, u32[]{:S(2)}) collective-permute-start(f32[4,16,512]{2,1,0:T(8,128)S(1)} %get-tuple-element.182), channel_id=1, source_target_pairs={{0,3},{1,2},{2,1},{3,0},{4,7},{5,6},{6,5},{7,4},{8,11},{9,10},{10,... | collective-permute-start | bytes 393224 | tf_op jit(solution)/shard_map/ppermute | solution.py:315
  64.4 11.5 %collective-permute-start.25 = (f32[4,16,512]{2,1,0:T(8,128)S(1)}, f32[4,16,512]{2,1,0:T(8,128)S(1)}, u32[]{:S(2)}, u32[]{:S(2)}) collective-permute-start(f32[4,16,512]{2,1,0:T(8,128)S(1)} %get-tuple-element.184), channel_id=1, source_target_pairs={{0,7},{1,6},{2,5},{3,4},{4,3},{5,2},{6,1},{7,0},{8,15},{9,14},{10,... | collective-permute-start | bytes 393224 | tf_op jit(solution)/shard_map/ppermute | solution.py:315
  65.8 10.0 %collective-permute-start.26 = (f32[16,16,128]{2,1,0:T(8,128)S(1)}, f32[16,16,128]{2,1,0:T(8,128)S(1)}, u32[]{:S(2)}, u32[]{:S(2)}) collective-permute-start(f32[16,16,128]{2,1,0:T(8,128)S(1)} %get-tuple-element.186), channel_id=1, source_target_pairs={{0,24},{8,16},{16,8},{24,0},{1,25},{9,17},{17,9},{25,1},{2,26},{10... | collective-permute-start | bytes 393224 | tf_op jit(solution)/shard_map/ppermute | solution.py:315
  67.1 8.8 %collective-permute-start.28 = (f32[4,16,512]{2,1,0:T(8,128)S(1)}, f32[4,16,512]{2,1,0:T(8,128)S(1)}, u32[]{:S(2)}, u32[]{:S(2)}) collective-permute-start(f32[4,16,512]{2,1,0:T(8,128)S(1)} %get-tuple-element.190), channel_id=1, source_target_pairs={{0,1},{1,0},{2,3},{3,2},{4,5},{5,4},{6,7},{7,6},{8,9},{9,8},{10,11... | collective-permute-start | bytes 393224 | tf_op jit(solution)/shard_map/ppermute | solution.py:315
  67.1 11.8 %collective-permute-start.30 = (f32[4,16,512]{2,1,0:T(8,128)S(1)}, f32[4,16,512]{2,1,0:T(8,128)S(1)}, u32[]{:S(2)}, u32[]{:S(2)}) collective-permute-start(f32[4,16,512]{2,1,0:T(8,128)S(1)} %get-tuple-element.194), channel_id=1, source_target_pairs={{0,4},{1,5},{2,6},{3,7},{4,0},{5,1},{6,2},{7,3},{8,12},{9,13},{10,... | collective-permute-start | bytes 393224 | tf_op jit(solution)/shard_map/ppermute | solution.py:315
  71.6 17.5 %collective-permute-start.33 = (f32[4,16,512]{2,1,0:T(8,128)S(1)}, f32[4,16,512]{2,1,0:T(8,128)S(1)}, u32[]{:S(2)}, u32[]{:S(2)}) collective-permute-start(f32[4,16,512]{2,1,0:T(8,128)S(1)} %get-tuple-element.201), channel_id=1, source_target_pairs={{0,2},{1,3},{2,0},{3,1},{4,6},{5,7},{6,4},{7,5},{8,10},{9,11},{10,... | collective-permute-start | bytes 393224 | tf_op jit(solution)/shard_map/ppermute | solution.py:315
  75.8 14.0 %collective-permute-start.32 = (f32[4,16,512]{2,1,0:T(8,128)S(1)}, f32[4,16,512]{2,1,0:T(8,128)S(1)}, u32[]{:S(2)}, u32[]{:S(2)}) collective-permute-start(f32[4,16,512]{2,1,0:T(8,128)S(1)} %get-tuple-element.200), channel_id=1, source_target_pairs={{0,5},{1,4},{2,7},{3,6},{4,1},{5,0},{6,3},{7,2},{8,13},{9,12},{10,... | collective-permute-start | bytes 393224 | tf_op jit(solution)/shard_map/ppermute | solution.py:315
  78.9 14.7 %collective-permute-start.31 = (f32[4,16,512]{2,1,0:T(8,128)S(1)}, f32[4,16,512]{2,1,0:T(8,128)S(1)}, u32[]{:S(2)}, u32[]{:S(2)}) collective-permute-start(f32[4,16,512]{2,1,0:T(8,128)S(1)} %get-tuple-element.195), channel_id=1, source_target_pairs={{0,7},{1,6},{2,5},{3,4},{4,3},{5,2},{6,1},{7,0},{8,15},{9,14},{10,... | collective-permute-start | bytes 393224 | tf_op jit(solution)/shard_map/ppermute | solution.py:315
  78.9 16.4 %collective-permute-start.29 = (f32[4,16,512]{2,1,0:T(8,128)S(1)}, f32[4,16,512]{2,1,0:T(8,128)S(1)}, u32[]{:S(2)}, u32[]{:S(2)}) collective-permute-start(f32[4,16,512]{2,1,0:T(8,128)S(1)} %get-tuple-element.191), channel_id=1, source_target_pairs={{0,6},{1,7},{2,4},{3,5},{4,2},{5,3},{6,0},{7,1},{8,14},{9,15},{10,... | collective-permute-start | bytes 393224 | tf_op jit(solution)/shard_map/ppermute | solution.py:315
  80.3 15.0 %collective-permute-start.27 = (f32[4,16,512]{2,1,0:T(8,128)S(1)}, f32[4,16,512]{2,1,0:T(8,128)S(1)}, u32[]{:S(2)}, u32[]{:S(2)}) collective-permute-start(f32[4,16,512]{2,1,0:T(8,128)S(1)} %get-tuple-element.187), channel_id=1, source_target_pairs={{0,3},{1,2},{2,1},{3,0},{4,7},{5,6},{6,5},{7,4},{8,11},{9,10},{10,... | collective-permute-start | bytes 393224 | tf_op jit(solution)/shard_map/ppermute | solution.py:315

commit v5 on v4

--- a/solution.py
+++ b/solution.py
@@ -323,11 +323,22 @@
     return both + list(first[shorter:]) + list(second[shorter:])
 
 
+measured_steps = {
+    (8, 2): (
+        (6, 1, 4, 3, 5, 2, 7),
+        (4, 1, 5, 2, 6, 3, 7),
+        (6, 3, 5, 2, 4, 1, 7),
+        (1, 4, 3, 5, 2, 6, 7),
+    )
+}
+
+
 def message_order(count, planes, group_count):
     far, near = range(count // 2, count), range(1, count // 2)
-    out = [("out", chunk, step) for chunk in range(planes) for step in turns(far, near)]
-    back = [("back", chunk, step) for chunk in range(planes - 1) for step in turns(far, near)]
-    back += [("back", planes - 1, step) for step in turns(near, far)]
+    phases = [turns(far, near)] * (2 * planes - 1) + [turns(near, far)]
+    phases = measured_steps.get((count, planes), phases)
+    out = [("out", chunk, step) for chunk in range(planes) for step in phases[chunk]]
+    back = [("back", chunk, step) for chunk in range(planes) for step in phases[planes + chunk]]
     first_z = count - 1
     second_z = max(len(out) + 3, first_z + 2 * (group_count - 2) + 1)
     order = []

time: 96.5 us -> 95 us (0.984)
  starting transfers between devices: 61.2 us -> 51.2 us
  waiting for transfers between devices: 18.3 us -> 27 us
    ppermute x34, starting transfers between devices: 61.2 us -> 51.2 us  [send(): got = lax.ppermute(piece, axis, [(i, i ^ step) for i in range(count)])]
    ppermute x34, waiting for transfers between devices: 18.3 us -> 27 us  [send(): got = lax.ppermute(piece, axis, [(i, i ^ step) for i in range(count)])]
  transfers between devices with their start and end apart: 34 -> 34, of which waited for: 10 -> 12; matrix products, arithmetic and copies ran while one was open for 0% -> 0% of each run, Pallas kernels for 15% -> 15%
where the time goes in v5:
time: 95 us; the launch traced here: 94.7 us
  starting transfers between devices  51.2 us (54%)
  waiting for transfers between devices  27 us (28%)
  Pallas kernels  16.2 us (17%)
    ppermute x34, starting transfers between devices, send(): got = lax.ppermute(piece, axis, [(i, i ^ step) for i in range(count)])  51.2 us
    ppermute x34, waiting for transfers between devices, send(): got = lax.ppermute(piece, axis, [(i, i ^ step) for i in range(count)])  27 us
    pallas_call x6, Pallas kernels, join(): pl.pallas_call(functools.partial(join_kernel, steps, planes), out_shape=j...  4.43 us
    pallas_call x2, Pallas kernels, on_plane(): pl.pallas_call(functools.partial(plane_kernel, count), out_shape=(jax.Sha...  3.94 us
    pallas_call x3, Pallas kernels, pack(): pl.pallas_call(functools.partial(pack_kernel, steps, planes), out_shape=(...  3.69 us
    pallas_call x1, Pallas kernels, prepare(): pl.pallas_call(functools.partial(prepare_kernel, len(parts)), out_shape=(...  1.98 us
  transfers between devices with their start and end apart: 34, of which 12 were waited for; matrix products, arithmetic and copies ran while one was open for 0% of the time, Pallas kernels for 15%

profile of v5, /device:TPU:8, one launch (start us, length us, event | category | flops | bytes accessed | tf_op | source)
XLA Modules:
  0.0 94.7 jit_solution(2373524112867676243)
XLA Ops:
  0.0 0.9 pack.3.refs_0_
  0.9 1.6 %collective-permute-start = (f32[4,16,512]{2,1,0:T(8,128)S(1)}, f32[4,16,512]{2,1,0:T(8,128)S(1)}, u32[]{:S(2)}, u32[]{:S(2)}) collective-permute-start(f32[4,16,512]{2,1,0:T(8,128)S(1)} %pack.3.refs_0_), channel_id=1, source_target_pairs={{0,6},{1,7},{2,4},{3,5},{4,2},{5,3},{6,0},{7,1},{8,14},{9,15},{10,... | collective-permute-start | bytes 393224 | tf_op jit(solution)/shard_map/ppermute | solution.py:315
  2.6 1.3 %pack.4 = (f32[4,16,512]{2,1,0:T(8,128)S(1)}, f32[4,16,512]{2,1,0:T(8,128)S(1)}, f32[4,16,512]{2,1,0:T(8,128)S(1)}, f32[4,16,512]{2,1,0:T(8,128)S(1)}, f32[4,16,...) custom-call(f32[3,16,16,512]{3,2,1,0:T(8,128)} %velocity.7, f32[16,16,512]{2,1,0:T(8,128)} %level_set.9, ...), custom_call_target="tpu_custom_call" | custom-call | tf_op jit(solution)/shard_map/pack/pallas_call | solution.py:67
  3.9 1.6 %collective-permute-start.1 = (f32[4,16,512]{2,1,0:T(8,128)S(1)}, f32[4,16,512]{2,1,0:T(8,128)S(1)}, u32[]{:S(2)}, u32[]{:S(2)}) collective-permute-start(f32[4,16,512]{2,1,0:T(8,128)S(1)} %get-tuple-element.106.refs_2_), channel_id=1, source_target_pairs={{0,1},{1,0},{2,3},{3,2},{4,5},{5,4},{6,7},{7,6},{8,9},{9,8},{10,11... | collective-permute-start | bytes 393224 | tf_op jit(solution)/shard_map/ppermute | solution.py:315
  5.5 1.2 %collective-permute-start.2 = (f32[4,16,512]{2,1,0:T(8,128)S(1)}, f32[4,16,512]{2,1,0:T(8,128)S(1)}, u32[]{:S(2)}, u32[]{:S(2)}) collective-permute-start(f32[4,16,512]{2,1,0:T(8,128)S(1)} %get-tuple-element.107.refs_3_), channel_id=1, source_target_pairs={{0,4},{1,5},{2,6},{3,7},{4,0},{5,1},{6,2},{7,3},{8,12},{9,13},{10,... | collective-permute-start | bytes 393224 | tf_op jit(solution)/shard_map/ppermute | solution.py:315
  6.7 1.2 %collective-permute-start.3 = (f32[4,16,512]{2,1,0:T(8,128)S(1)}, f32[4,16,512]{2,1,0:T(8,128)S(1)}, u32[]{:S(2)}, u32[]{:S(2)}) collective-permute-start(f32[4,16,512]{2,1,0:T(8,128)S(1)} %get-tuple-element.108.refs_4_), channel_id=1, source_target_pairs={{0,3},{1,2},{2,1},{3,0},{4,7},{5,6},{6,5},{7,4},{8,11},{9,10},{10,... | collective-permute-start | bytes 393224 | tf_op jit(solution)/shard_map/ppermute | solution.py:315
  7.9 3.9 %collective-permute-start.4 = (f32[4,16,512]{2,1,0:T(8,128)S(1)}, f32[4,16,512]{2,1,0:T(8,128)S(1)}, u32[]{:S(2)}, u32[]{:S(2)}) collective-permute-start(f32[4,16,512]{2,1,0:T(8,128)S(1)} %get-tuple-element.109.refs_5_), channel_id=1, source_target_pairs={{0,5},{1,4},{2,7},{3,6},{4,1},{5,0},{6,3},{7,2},{8,13},{9,12},{10,... | collective-permute-start | bytes 393224 | tf_op jit(solution)/shard_map/ppermute | solution.py:315
  11.8 1.5 %pack.5 = (f32[4,16,512]{2,1,0:T(8,128)S(1)}, f32[4,16,512]{2,1,0:T(8,128)S(1)}, f32[4,16,512]{2,1,0:T(8,128)S(1)}, f32[4,16,512]{2,1,0:T(8,128)S(1)}, f32[4,16,...) custom-call(f32[3,16,16,512]{3,2,1,0:T(8,128)} %velocity.7, ...), custom_call_target="tpu_custom_call" | custom-call | tf_op jit(solution)/shard_map/pack/pallas_call | solution.py:67
  13.4 1.8 %collective-permute-start.7 = (f32[4,16,512]{2,1,0:T(8,128)S(1)}, f32[4,16,512]{2,1,0:T(8,128)S(1)}, u32[]{:S(2)}, u32[]{:S(2)}) collective-permute-start(f32[4,16,512]{2,1,0:T(8,128)S(1)} %get-tuple-element.126), channel_id=1, source_target_pairs={{0,7},{1,6},{2,5},{3,4},{4,3},{5,2},{6,1},{7,0},{8,15},{9,14},{10,... | collective-permute-start | bytes 393224 | tf_op jit(solution)/shard_map/ppermute | solution.py:315
  15.2 1.3 %panels.1 = (f32[16,16,128]{2,1,0:T(8,128)S(1)}, f32[16,16,128]{2,1,0:T(8,128)S(1)}, f32[16,16,128]{2,1,0:T(8,128)S(1)}, f32[16,16,128]{2,1,0:T(8,128)S(1)}) custom-call(f32[16,16,512]{2,1,0:T(8,128)} %level_set.9, f32[4,16,512]{2,1,0:T(8,128)S(1)} %collective-permute-done.after.refs_2_.refs_6_), custom_call_target="tpu_custom_call" | custom-call | tf_op jit(solution)/shard_map/panels/pallas_call | solution.py:200
  16.5 0.7 collective-permute-done.2.refs_2_.refs_4_
  17.1 3.9 %collective-permute-start.10 = (f32[4,16,512]{2,1,0:T(8,128)S(1)}, f32[4,16,512]{2,1,0:T(8,128)S(1)}, u32[]{:S(2)}, u32[]{:S(2)}) collective-permute-start(f32[4,16,512]{2,1,0:T(8,128)S(1)} %get-tuple-element.134), channel_id=1, source_target_pairs={{0,4},{1,5},{2,6},{3,7},{4,0},{5,1},{6,2},{7,3},{8,12},{9,13},{10,... | collective-permute-start | bytes 393224 | tf_op jit(solution)/shard_map/ppermute | solution.py:315
  21.1 4.6 %collective-permute-done.4.refs_2_.refs_5_ = f32[4,16,512]{2,1,0:T(8,128)S(1)} collective-permute-done((f32[4,16,512]{2,1,0:T(8,128)S(1)}, f32[4,16,512]{2,1,0:T(8,128)S(1)}, u32[]{:S(2)}, u32[]{:S(2)}) %collective-permute-start.4) | collective-permute-done | bytes 131104 | tf_op jit(solution)/shard_map/ppermute | solution.py:315
  25.7 1.5 %collective-permute-start.5 = (f32[4,16,512]{2,1,0:T(8,128)S(1)}, f32[4,16,512]{2,1,0:T(8,128)S(1)}, u32[]{:S(2)}, u32[]{:S(2)}) collective-permute-start(f32[4,16,512]{2,1,0:T(8,128)S(1)} %get-tuple-element.119), channel_id=1, source_target_pairs={{0,1},{1,0},{2,3},{3,2},{4,5},{5,4},{6,7},{7,6},{8,9},{9,8},{10,11... | collective-permute-start | bytes 393224 | tf_op jit(solution)/shard_map/ppermute | solution.py:315
  27.2 1.5 %collective-permute-start.11 = (f32[16,16,128]{2,1,0:T(8,128)S(1)}, f32[16,16,128]{2,1,0:T(8,128)S(1)}, u32[]{:S(2)}, u32[]{:S(2)}) collective-permute-start(f32[16,16,128]{2,1,0:T(8,128)S(1)} %get-tuple-element.137), channel_id=1, source_target_pairs={{0,16},{8,24},{16,0},{24,8},{1,17},{9,25},{17,1},{25,9},{2,18},{10... | collective-permute-start | bytes 393224 | tf_op jit(solution)/shard_map/ppermute | solution.py:315
  28.7 1.9 %collective-permute-done.7.refs_2_.refs_7_ = f32[4,16,512]{2,1,0:T(8,128)S(1)} collective-permute-done((f32[4,16,512]{2,1,0:T(8,128)S(1)}, f32[4,16,512]{2,1,0:T(8,128)S(1)}, u32[]{:S(2)}, u32[]{:S(2)}) %collective-permute-start.7) | collective-permute-done | bytes 131104 | tf_op jit(solution)/shard_map/ppermute | solution.py:315
  30.6 2.4 %collective-permute-start.13 = (f32[4,16,512]{2,1,0:T(8,128)S(1)}, f32[4,16,512]{2,1,0:T(8,128)S(1)}, u32[]{:S(2)}, u32[]{:S(2)}) collective-permute-start(f32[4,16,512]{2,1,0:T(8,128)S(1)} %get-tuple-element.139), channel_id=1, source_target_pairs={{0,5},{1,4},{2,7},{3,6},{4,1},{5,0},{6,3},{7,2},{8,13},{9,12},{10,... | collective-permute-start | bytes 393224 | tf_op jit(solution)/shard_map/ppermute | solution.py:315
  33.9 3.0 %collective-permute-start.12 = (f32[4,16,512]{2,1,0:T(8,128)S(1)}, f32[4,16,512]{2,1,0:T(8,128)S(1)}, u32[]{:S(2)}, u32[]{:S(2)}) collective-permute-start(f32[4,16,512]{2,1,0:T(8,128)S(1)} %get-tuple-element.138), channel_id=1, source_target_pairs={{0,3},{1,2},{2,1},{3,0},{4,7},{5,6},{6,5},{7,4},{8,11},{9,10},{10,... | collective-permute-start | bytes 393224 | tf_op jit(solution)/shard_map/ppermute | solution.py:315
  36.9 0.6 collective-permute-done.13.refs_2_.refs_5_
  37.6 1.7 %collective-permute-start.15 = (f32[4,16,512]{2,1,0:T(8,128)S(1)}, f32[4,16,512]{2,1,0:T(8,128)S(1)}, u32[]{:S(2)}, u32[]{:S(2)}) collective-permute-start(f32[4,16,512]{2,1,0:T(8,128)S(1)} %get-tuple-element.143), channel_id=1, source_target_pairs={{0,7},{1,6},{2,5},{3,4},{4,3},{5,2},{6,1},{7,0},{8,15},{9,14},{10,... | collective-permute-start | bytes 393224 | tf_op jit(solution)/shard_map/ppermute | solution.py:315
  39.3 2.0 %plane.3 = (f32[4,16,512]{2,1,0:T(8,128)S(1)}, f32[4,16,512]{2,1,0:T(8,128)S(1)}, f32[4,16,512]{2,1,0:T(8,128)S(1)}, f32[4,16,512]{2,1,0:T(8,128)S(1)}, f32[4,16...) custom-call(bf16[1536,512]{1,0:T(8,128)(2,1)S(1)} %copy-done, ...), custom_call_target="tpu_custom_call" | custom-call | tf_op jit(solution)/shard_map/plane/pallas_call | solution.py:132
  41.9 6.5 %collective-permute-start.18 = (f32[4,16,512]{2,1,0:T(8,128)S(1)}, f32[4,16,512]{2,1,0:T(8,128)S(1)}, u32[]{:S(2)}, u32[]{:S(2)}) collective-permute-start(f32[4,16,512]{2,1,0:T(8,128)S(1)} %get-tuple-element.170), channel_id=1, source_target_pairs={{0,3},{1,2},{2,1},{3,0},{4,7},{5,6},{6,5},{7,4},{8,11},{9,10},{10,... | collective-permute-start | bytes 393224 | tf_op jit(solution)/shard_map/ppermute | solution.py:315
  48.4 0.9 z_lines.1
  49.4 3.8 %collective-permute-done.15.refs_7_.refs_2_ = f32[4,16,512]{2,1,0:T(8,128)S(1)} collective-permute-done((f32[4,16,512]{2,1,0:T(8,128)S(1)}, f32[4,16,512]{2,1,0:T(8,128)S(1)}, u32[]{:S(2)}, u32[]{:S(2)}) %collective-permute-start.15) | collective-permute-done | bytes 131104 | tf_op jit(solution)/shard_map/ppermute | solution.py:315
  53.2 1.6 %collective-permute-start.21 = (f32[4,16,512]{2,1,0:T(8,128)S(1)}, f32[4,16,512]{2,1,0:T(8,128)S(1)}, u32[]{:S(2)}, u32[]{:S(2)}) collective-permute-start(f32[4,16,512]{2,1,0:T(8,128)S(1)} %get-tuple-element.176), channel_id=1, source_target_pairs={{0,2},{1,3},{2,0},{3,1},{4,6},{5,7},{6,4},{7,5},{8,10},{9,11},{10,... | collective-permute-start | bytes 393224 | tf_op jit(solution)/shard_map/ppermute | solution.py:315
  54.8 2.0 %plane.2 = (f32[4,16,512]{2,1,0:T(8,128)S(1)}, f32[4,16,512]{2,1,0:T(8,128)S(1)}, f32[4,16,512]{2,1,0:T(8,128)S(1)}, f32[4,16,512]{2,1,0:T(8,128)S(1)}, f32[4,16...) custom-call(bf16[1536,512]{1,0:T(8,128)(2,1)S(1)} %copy-done, ...), custom_call_target="tpu_custom_call" | custom-call | tf_op jit(solution)/shard_map/plane/pallas_call | solution.py:132
  56.7 0.7 collective-permute-done.17.refs_2_.refs_6_
  57.4 1.4 %collective-permute-start.22 = (f32[4,16,512]{2,1,0:T(8,128)S(1)}, f32[4,16,512]{2,1,0:T(8,128)S(1)}, u32[]{:S(2)}, u32[]{:S(2)}) collective-permute-start(f32[4,16,512]{2,1,0:T(8,128)S(1)} %get-tuple-element.178), channel_id=1, source_target_pairs={{0,4},{1,5},{2,6},{3,7},{4,0},{5,1},{6,2},{7,3},{8,12},{9,13},{10,... | collective-permute-start | bytes 393224 | tf_op jit(solution)/shard_map/ppermute | solution.py:315
  58.8 1.2 %collective-permute-start.23 = (f32[16,16,128]{2,1,0:T(8,128)S(1)}, f32[16,16,128]{2,1,0:T(8,128)S(1)}, u32[]{:S(2)}, u32[]{:S(2)}) collective-permute-start(f32[16,16,128]{2,1,0:T(8,128)S(1)} %get-tuple-element.180), channel_id=1, source_target_pairs={{0,16},{8,24},{16,0},{24,8},{1,17},{9,25},{17,1},{25,9},{2,18},{10... | collective-permute-start | bytes 393224 | tf_op jit(solution)/shard_map/ppermute | solution.py:315
  60.0 1.6 %collective-permute-done.19.refs_2_.refs_5_ = f32[4,16,512]{2,1,0:T(8,128)S(1)} collective-permute-done((f32[4,16,512]{2,1,0:T(8,128)S(1)}, f32[4,16,512]{2,1,0:T(8,128)S(1)}, u32[]{:S(2)}, u32[]{:S(2)}) %collective-permute-start.19) | collective-permute-done | bytes 131104 | tf_op jit(solution)/shard_map/ppermute | solution.py:315
  61.6 1.7 %collective-permute-start.25 = (f32[4,16,512]{2,1,0:T(8,128)S(1)}, f32[4,16,512]{2,1,0:T(8,128)S(1)}, u32[]{:S(2)}, u32[]{:S(2)}) collective-permute-start(f32[4,16,512]{2,1,0:T(8,128)S(1)} %get-tuple-element.184), channel_id=1, source_target_pairs={{0,7},{1,6},{2,5},{3,4},{4,3},{5,2},{6,1},{7,0},{8,15},{9,14},{10,... | collective-permute-start | bytes 393224 | tf_op jit(solution)/shard_map/ppermute | solution.py:315
  63.3 3.8 %collective-permute-done.22.refs_2_.refs_4_ = f32[4,16,512]{2,1,0:T(8,128)S(1)} collective-permute-done((f32[4,16,512]{2,1,0:T(8,128)S(1)}, f32[4,16,512]{2,1,0:T(8,128)S(1)}, u32[]{:S(2)}, u32[]{:S(2)}) %collective-permute-start.22) | collective-permute-done | bytes 131104 | tf_op jit(solution)/shard_map/ppermute | solution.py:315
  67.1 0.7 collective-permute-start.28
  67.8 3.5 %collective-permute-start.30 = (f32[4,16,512]{2,1,0:T(8,128)S(1)}, f32[4,16,512]{2,1,0:T(8,128)S(1)}, u32[]{:S(2)}, u32[]{:S(2)}) collective-permute-start(f32[4,16,512]{2,1,0:T(8,128)S(1)} %get-tuple-element.194), channel_id=1, source_target_pairs={{0,4},{1,5},{2,6},{3,7},{4,0},{5,1},{6,2},{7,3},{8,12},{9,13},{10,... | collective-permute-start | bytes 393224 | tf_op jit(solution)/shard_map/ppermute | solution.py:315
  71.3 2.9 %collective-permute-done.25.refs_2_.refs_7_ = f32[4,16,512]{2,1,0:T(8,128)S(1)} collective-permute-done((f32[4,16,512]{2,1,0:T(8,128)S(1)}, f32[4,16,512]{2,1,0:T(8,128)S(1)}, u32[]{:S(2)}, u32[]{:S(2)}) %collective-permute-start.25) | collective-permute-done | bytes 131104 | tf_op jit(solution)/shard_map/ppermute | solution.py:315
  74.3 2.7 %collective-permute-done.30.refs_2_.refs_0_ = f32[4,16,512]{2,1,0:T(8,128)S(1)} collective-permute-done((f32[4,16,512]{2,1,0:T(8,128)S(1)}, f32[4,16,512]{2,1,0:T(8,128)S(1)}, u32[]{:S(2)}, u32[]{:S(2)}) %collective-permute-start.30) | collective-permute-done | bytes 131104 | tf_op jit(solution)/shard_map/ppermute | solution.py:315
  77.0 1.0 %collective-permute-start.31 = (f32[4,16,512]{2,1,0:T(8,128)S(1)}, f32[4,16,512]{2,1,0:T(8,128)S(1)}, u32[]{:S(2)}, u32[]{:S(2)}) collective-permute-start(f32[4,16,512]{2,1,0:T(8,128)S(1)} %get-tuple-element.195), channel_id=1, source_target_pairs={{0,7},{1,6},{2,5},{3,4},{4,3},{5,2},{6,1},{7,0},{8,15},{9,14},{10,... | collective-permute-start | bytes 393224 | tf_op jit(solution)/shard_map/ppermute | solution.py:315
  78.0 2.1 %collective-permute-start.29 = (f32[4,16,512]{2,1,0:T(8,128)S(1)}, f32[4,16,512]{2,1,0:T(8,128)S(1)}, u32[]{:S(2)}, u32[]{:S(2)}) collective-permute-start(f32[4,16,512]{2,1,0:T(8,128)S(1)} %get-tuple-element.191), channel_id=1, source_target_pairs={{0,6},{1,7},{2,4},{3,5},{4,2},{5,3},{6,0},{7,1},{8,14},{9,15},{10,... | collective-permute-start | bytes 393224 | tf_op jit(solution)/shard_map/ppermute | solution.py:315
  80.1 4.4 %collective-permute-start.27 = (f32[4,16,512]{2,1,0:T(8,128)S(1)}, f32[4,16,512]{2,1,0:T(8,128)S(1)}, u32[]{:S(2)}, u32[]{:S(2)}) collective-permute-start(f32[4,16,512]{2,1,0:T(8,128)S(1)} %get-tuple-element.187), channel_id=1, source_target_pairs={{0,2},{1,3},{2,0},{3,1},{4,6},{5,7},{6,4},{7,5},{8,10},{9,11},{10,... | collective-permute-start | bytes 393224 | tf_op jit(solution)/shard_map/ppermute | solution.py:315
  84.5 2.0 %prepare.1 = (f32[16,16,512]{2,1,0:T(8,128)S(1)}, f32[16,16,512]{2,1,0:T(8,128)S(1)}, f32[16,16,512]{2,1,0:T(8,128)S(1)}) custom-call(bf16[1536,512]{1,0:T(8,128)(2,1)S(1)} %copy-done, f32[16,16,512]{2,1,0:T(8,128)} %level_set.9, f32[3,16,16,512]{3,2,1,0:T(8,128)} %velocity.7, f32[16,16,128]{2,1,0:T(8,128)S(1)} %get-tuple-element.196.refs_0_, ...), custom_call_target="tpu_custom_call" | custom-call | tf_op jit(solution)/shard_map/prepare/pallas_call | solution.py:271
  86.5 1.0 %join.6.refs_4_ = f32[3,16,16,512]{3,2,1,0:T(8,128)} custom-call(f32[4,16,512]{2,1,0:T(8,128)S(1)} %get-tuple-element.202.refs_0_, f32[4,16,512]{2,1,0:T(8,128)S(1)} %collective-permute-done.24.refs_2_.refs_1_, f32[4,16,512]{2,1,0:T(8,128)S(1)} %collective-permute-done.21.refs_2_, f32[4,16,512]{2,1,0:T(8,128)S(1)} %collective-permute-done.18.refs_2_.refs_3_, ...), custom_call_target="tpu_custom_call" | custom-call | flops 10000000 | tf_op jit(solution)/shard_map/join/pallas_call | solution.py:168
  87.5 0.7 join.7.refs_4_
  88.2 0.7 join.8.refs_4_
  88.9 0.7 join.9.refs_4_
  89.6 0.7 join.10.refs_6_
  90.2 1.9 %collective-permute-done.31.refs_2_ = f32[4,16,512]{2,1,0:T(8,128)S(1)} collective-permute-done((f32[4,16,512]{2,1,0:T(8,128)S(1)}, f32[4,16,512]{2,1,0:T(8,128)S(1)}, u32[]{:S(2)}, u32[]{:S(2)}) %collective-permute-start.31) | collective-permute-done | bytes 131104 | tf_op jit(solution)/shard_map/ppermute | solution.py:315
  92.2 1.8 %collective-permute-done.29.refs_1_ = f32[4,16,512]{2,1,0:T(8,128)S(1)} collective-permute-done((f32[4,16,512]{2,1,0:T(8,128)S(1)}, f32[4,16,512]{2,1,0:T(8,128)S(1)}, u32[]{:S(2)}, u32[]{:S(2)}) %collective-permute-start.29) | collective-permute-done | bytes 131104 | tf_op jit(solution)/shard_map/ppermute | solution.py:315
  94.0 0.7 join.11
  (70 shorter events, 1.7 us)
Async XLA Ops:
  0.9 12.3 %collective-permute-start = (f32[4,16,512]{2,1,0:T(8,128)S(1)}, f32[4,16,512]{2,1,0:T(8,128)S(1)}, u32[]{:S(2)}, u32[]{:S(2)}) collective-permute-start(f32[4,16,512]{2,1,0:T(8,128)S(1)} %pack.3.refs_0_), channel_id=1, source_target_pairs={{0,6},{1,7},{2,4},{3,5},{4,2},{5,3},{6,0},{7,1},{8,14},{9,15},{10,... | collective-permute-start | bytes 393224 | tf_op jit(solution)/shard_map/ppermute | solution.py:315
  3.9 9.5 %collective-permute-start.1 = (f32[4,16,512]{2,1,0:T(8,128)S(1)}, f32[4,16,512]{2,1,0:T(8,128)S(1)}, u32[]{:S(2)}, u32[]{:S(2)}) collective-permute-start(f32[4,16,512]{2,1,0:T(8,128)S(1)} %get-tuple-element.106.refs_2_), channel_id=1, source_target_pairs={{0,1},{1,0},{2,3},{3,2},{4,5},{5,4},{6,7},{7,6},{8,9},{9,8},{10,11... | collective-permute-start | bytes 393224 | tf_op jit(solution)/shard_map/ppermute | solution.py:315
  5.5 11.7 %collective-permute-start.2 = (f32[4,16,512]{2,1,0:T(8,128)S(1)}, f32[4,16,512]{2,1,0:T(8,128)S(1)}, u32[]{:S(2)}, u32[]{:S(2)}) collective-permute-start(f32[4,16,512]{2,1,0:T(8,128)S(1)} %get-tuple-element.107.refs_3_), channel_id=1, source_target_pairs={{0,4},{1,5},{2,6},{3,7},{4,0},{5,1},{6,2},{7,3},{8,12},{9,13},{10,... | collective-permute-start | bytes 393224 | tf_op jit(solution)/shard_map/ppermute | solution.py:315
  6.7 10.4 %collective-permute-start.3 = (f32[4,16,512]{2,1,0:T(8,128)S(1)}, f32[4,16,512]{2,1,0:T(8,128)S(1)}, u32[]{:S(2)}, u32[]{:S(2)}) collective-permute-start(f32[4,16,512]{2,1,0:T(8,128)S(1)} %get-tuple-element.108.refs_4_), channel_id=1, source_target_pairs={{0,3},{1,2},{2,1},{3,0},{4,7},{5,6},{6,5},{7,4},{8,11},{9,10},{10,... | collective-permute-start | bytes 393224 | tf_op jit(solution)/shard_map/ppermute | solution.py:315
  7.9 17.8 %collective-permute-start.4 = (f32[4,16,512]{2,1,0:T(8,128)S(1)}, f32[4,16,512]{2,1,0:T(8,128)S(1)}, u32[]{:S(2)}, u32[]{:S(2)}) collective-permute-start(f32[4,16,512]{2,1,0:T(8,128)S(1)} %get-tuple-element.109.refs_5_), channel_id=1, source_target_pairs={{0,5},{1,4},{2,7},{3,6},{4,1},{5,0},{6,3},{7,2},{8,13},{9,12},{10,... | collective-permute-start | bytes 393224 | tf_op jit(solution)/shard_map/ppermute | solution.py:315
  13.3 14.0 %collective-permute-start.6 = (f32[4,16,512]{2,1,0:T(8,128)S(1)}, f32[4,16,512]{2,1,0:T(8,128)S(1)}, u32[]{:S(2)}, u32[]{:S(2)}) collective-permute-start(f32[4,16,512]{2,1,0:T(8,128)S(1)} %get-tuple-element.124), channel_id=1, source_target_pairs={{0,2},{1,3},{2,0},{3,1},{4,6},{5,7},{6,4},{7,5},{8,10},{9,11},{10,... | collective-permute-start | bytes 393224 | tf_op jit(solution)/shard_map/ppermute | solution.py:315
  13.4 25.9 %copy-start = (bf16[1536,512]{1,0:T(8,128)(2,1)S(1)}, bf16[1536,512]{1,0:T(8,128)(2,1)}, u32[]{:S(2)}) copy-start(bf16[1536,512]{1,0:T(8,128)(2,1)} %constant.8.clone.dx) | copy-start | bytes 4718596
  13.4 25.9 %copy-start.1 = (bf16[128,384]{1,0:T(8,128)(2,1)S(1)}, bf16[128,384]{1,0:T(8,128)(2,1)}, u32[]{:S(2)}) copy-start(bf16[128,384]{1,0:T(8,128)(2,1)} %constant.9.clone.dy) | copy-start | bytes 294916
  13.4 17.2 %collective-permute-start.7 = (f32[4,16,512]{2,1,0:T(8,128)S(1)}, f32[4,16,512]{2,1,0:T(8,128)S(1)}, u32[]{:S(2)}, u32[]{:S(2)}) collective-permute-start(f32[4,16,512]{2,1,0:T(8,128)S(1)} %get-tuple-element.126), channel_id=1, source_target_pairs={{0,7},{1,6},{2,5},{3,4},{4,3},{5,2},{6,1},{7,0},{8,15},{9,14},{10,... | collective-permute-start | bytes 393224 | tf_op jit(solution)/shard_map/ppermute | solution.py:315
  17.1 15.9 %collective-permute-start.8 = (f32[16,16,128]{2,1,0:T(8,128)S(1)}, f32[16,16,128]{2,1,0:T(8,128)S(1)}, u32[]{:S(2)}, u32[]{:S(2)}) collective-permute-start(f32[16,16,128]{2,1,0:T(8,128)S(1)} %get-tuple-element.128), channel_id=1, source_target_pairs={{0,8},{8,0},{16,24},{24,16},{1,9},{9,1},{17,25},{25,17},{2,10},{10... | collective-permute-start | bytes 393224 | tf_op jit(solution)/shard_map/ppermute | solution.py:315
  17.1 16.2 %collective-permute-start.10 = (f32[4,16,512]{2,1,0:T(8,128)S(1)}, f32[4,16,512]{2,1,0:T(8,128)S(1)}, u32[]{:S(2)}, u32[]{:S(2)}) collective-permute-start(f32[4,16,512]{2,1,0:T(8,128)S(1)} %get-tuple-element.134), channel_id=1, source_target_pairs={{0,4},{1,5},{2,6},{3,7},{4,0},{5,1},{6,2},{7,3},{8,12},{9,13},{10,... | collective-permute-start | bytes 393224 | tf_op jit(solution)/shard_map/ppermute | solution.py:315
  25.7 7.7 %collective-permute-start.5 = (f32[4,16,512]{2,1,0:T(8,128)S(1)}, f32[4,16,512]{2,1,0:T(8,128)S(1)}, u32[]{:S(2)}, u32[]{:S(2)}) collective-permute-start(f32[4,16,512]{2,1,0:T(8,128)S(1)} %get-tuple-element.119), channel_id=1, source_target_pairs={{0,1},{1,0},{2,3},{3,2},{4,5},{5,4},{6,7},{7,6},{8,9},{9,8},{10,11... | collective-permute-start | bytes 393224 | tf_op jit(solution)/shard_map/ppermute | solution.py:315
  27.2 6.7 %collective-permute-start.11 = (f32[16,16,128]{2,1,0:T(8,128)S(1)}, f32[16,16,128]{2,1,0:T(8,128)S(1)}, u32[]{:S(2)}, u32[]{:S(2)}) collective-permute-start(f32[16,16,128]{2,1,0:T(8,128)S(1)} %get-tuple-element.137), channel_id=1, source_target_pairs={{0,16},{8,24},{16,0},{24,8},{1,17},{9,25},{17,1},{25,9},{2,18},{10... | collective-permute-start | bytes 393224 | tf_op jit(solution)/shard_map/ppermute | solution.py:315
  30.6 6.9 %collective-permute-start.13 = (f32[4,16,512]{2,1,0:T(8,128)S(1)}, f32[4,16,512]{2,1,0:T(8,128)S(1)}, u32[]{:S(2)}, u32[]{:S(2)}) collective-permute-start(f32[4,16,512]{2,1,0:T(8,128)S(1)} %get-tuple-element.139), channel_id=1, source_target_pairs={{0,5},{1,4},{2,7},{3,6},{4,1},{5,0},{6,3},{7,2},{8,13},{9,12},{10,... | collective-permute-start | bytes 393224 | tf_op jit(solution)/shard_map/ppermute | solution.py:315
  33.0 8.3 %collective-permute-start.9 = (f32[4,16,512]{2,1,0:T(8,128)S(1)}, f32[4,16,512]{2,1,0:T(8,128)S(1)}, u32[]{:S(2)}, u32[]{:S(2)}) collective-permute-start(f32[4,16,512]{2,1,0:T(8,128)S(1)} %get-tuple-element.129), channel_id=1, source_target_pairs={{0,2},{1,3},{2,0},{3,1},{4,6},{5,7},{6,4},{7,5},{8,10},{9,11},{10,... | collective-permute-start | bytes 393224 | tf_op jit(solution)/shard_map/ppermute | solution.py:315
  33.4 8.6 %collective-permute-start.16 = (f32[16,16,128]{2,1,0:T(8,128)S(1)}, f32[16,16,128]{2,1,0:T(8,128)S(1)}, u32[]{:S(2)}, u32[]{:S(2)}) collective-permute-start(f32[16,16,128]{2,1,0:T(8,128)S(1)} %get-tuple-element.150), channel_id=1, source_target_pairs={{0,24},{8,16},{16,8},{24,0},{1,25},{9,17},{17,9},{25,1},{2,26},{10... | collective-permute-start | bytes 393224 | tf_op jit(solution)/shard_map/ppermute | solution.py:315
  33.4 15.0 %collective-permute-start.14 = (f32[4,16,512]{2,1,0:T(8,128)S(1)}, f32[4,16,512]{2,1,0:T(8,128)S(1)}, u32[]{:S(2)}, u32[]{:S(2)}) collective-permute-start(f32[4,16,512]{2,1,0:T(8,128)S(1)} %get-tuple-element.140), channel_id=1, source_target_pairs={{0,6},{1,7},{2,4},{3,5},{4,2},{5,3},{6,0},{7,1},{8,14},{9,15},{10,... | collective-permute-start | bytes 393224 | tf_op jit(solution)/shard_map/ppermute | solution.py:315
  33.9 15.4 %collective-permute-start.12 = (f32[4,16,512]{2,1,0:T(8,128)S(1)}, f32[4,16,512]{2,1,0:T(8,128)S(1)}, u32[]{:S(2)}, u32[]{:S(2)}) collective-permute-start(f32[4,16,512]{2,1,0:T(8,128)S(1)} %get-tuple-element.138), channel_id=1, source_target_pairs={{0,3},{1,2},{2,1},{3,0},{4,7},{5,6},{6,5},{7,4},{8,11},{9,10},{10,... | collective-permute-start | bytes 393224 | tf_op jit(solution)/shard_map/ppermute | solution.py:315
  37.6 10.8 %copy-start.2 = (f32[4,64,64]{2,1,0:T(8,128)S(1)}, f32[4,64,64]{2,1,0:T(8,128)}, u32[]{:S(2)}) copy-start(f32[4,64,64]{2,1,0:T(8,128)} %constant.10.clone.tables) | copy-start | bytes 196612
  37.6 15.6 %collective-permute-start.15 = (f32[4,16,512]{2,1,0:T(8,128)S(1)}, f32[4,16,512]{2,1,0:T(8,128)S(1)}, u32[]{:S(2)}, u32[]{:S(2)}) collective-permute-start(f32[4,16,512]{2,1,0:T(8,128)S(1)} %get-tuple-element.143), channel_id=1, source_target_pairs={{0,7},{1,6},{2,5},{3,4},{4,3},{5,2},{6,1},{7,0},{8,15},{9,14},{10,... | collective-permute-start | bytes 393224 | tf_op jit(solution)/shard_map/ppermute | solution.py:315
  41.3 16.1 %collective-permute-start.17 = (f32[4,16,512]{2,1,0:T(8,128)S(1)}, f32[4,16,512]{2,1,0:T(8,128)S(1)}, u32[]{:S(2)}, u32[]{:S(2)}) collective-permute-start(f32[4,16,512]{2,1,0:T(8,128)S(1)} %get-tuple-element.167), channel_id=1, source_target_pairs={{0,6},{1,7},{2,4},{3,5},{4,2},{5,3},{6,0},{7,1},{8,14},{9,15},{10,... | collective-permute-start | bytes 393224 | tf_op jit(solution)/shard_map/ppermute | solution.py:315
  41.9 16.9 %collective-permute-start.18 = (f32[4,16,512]{2,1,0:T(8,128)S(1)}, f32[4,16,512]{2,1,0:T(8,128)S(1)}, u32[]{:S(2)}, u32[]{:S(2)}) collective-permute-start(f32[4,16,512]{2,1,0:T(8,128)S(1)} %get-tuple-element.170), channel_id=1, source_target_pairs={{0,3},{1,2},{2,1},{3,0},{4,7},{5,6},{6,5},{7,4},{8,11},{9,10},{10,... | collective-permute-start | bytes 393224 | tf_op jit(solution)/shard_map/ppermute | solution.py:315
  48.4 13.2 %collective-permute-start.19 = (f32[4,16,512]{2,1,0:T(8,128)S(1)}, f32[4,16,512]{2,1,0:T(8,128)S(1)}, u32[]{:S(2)}, u32[]{:S(2)}) collective-permute-start(f32[4,16,512]{2,1,0:T(8,128)S(1)} %get-tuple-element.172), channel_id=1, source_target_pairs={{0,5},{1,4},{2,7},{3,6},{4,1},{5,0},{6,3},{7,2},{8,13},{9,12},{10,... | collective-permute-start | bytes 393224 | tf_op jit(solution)/shard_map/ppermute | solution.py:315
  49.3 12.3 %collective-permute-start.20 = (f32[16,16,128]{2,1,0:T(8,128)S(1)}, f32[16,16,128]{2,1,0:T(8,128)S(1)}, u32[]{:S(2)}, u32[]{:S(2)}) collective-permute-start(f32[16,16,128]{2,1,0:T(8,128)S(1)} %get-tuple-element.174), channel_id=1, source_target_pairs={{0,8},{8,0},{16,24},{24,16},{1,9},{9,1},{17,25},{25,17},{2,10},{10... | collective-permute-start | bytes 393224 | tf_op jit(solution)/shard_map/ppermute | solution.py:315
  53.2 10.1 %collective-permute-start.21 = (f32[4,16,512]{2,1,0:T(8,128)S(1)}, f32[4,16,512]{2,1,0:T(8,128)S(1)}, u32[]{:S(2)}, u32[]{:S(2)}) collective-permute-start(f32[4,16,512]{2,1,0:T(8,128)S(1)} %get-tuple-element.176), channel_id=1, source_target_pairs={{0,2},{1,3},{2,0},{3,1},{4,6},{5,7},{6,4},{7,5},{8,10},{9,11},{10,... | collective-permute-start | bytes 393224 | tf_op jit(solution)/shard_map/ppermute | solution.py:315
  57.4 9.7 %collective-permute-start.22 = (f32[4,16,512]{2,1,0:T(8,128)S(1)}, f32[4,16,512]{2,1,0:T(8,128)S(1)}, u32[]{:S(2)}, u32[]{:S(2)}) collective-permute-start(f32[4,16,512]{2,1,0:T(8,128)S(1)} %get-tuple-element.178), channel_id=1, source_target_pairs={{0,4},{1,5},{2,6},{3,7},{4,0},{5,1},{6,2},{7,3},{8,12},{9,13},{10,... | collective-permute-start | bytes 393224 | tf_op jit(solution)/shard_map/ppermute | solution.py:315
  58.8 9.0 %collective-permute-start.23 = (f32[16,16,128]{2,1,0:T(8,128)S(1)}, f32[16,16,128]{2,1,0:T(8,128)S(1)}, u32[]{:S(2)}, u32[]{:S(2)}) collective-permute-start(f32[16,16,128]{2,1,0:T(8,128)S(1)} %get-tuple-element.180), channel_id=1, source_target_pairs={{0,16},{8,24},{16,0},{24,8},{1,17},{9,25},{17,1},{25,9},{2,18},{10... | collective-permute-start | bytes 393224 | tf_op jit(solution)/shard_map/ppermute | solution.py:315
  61.6 9.7 %collective-permute-start.24 = (f32[4,16,512]{2,1,0:T(8,128)S(1)}, f32[4,16,512]{2,1,0:T(8,128)S(1)}, u32[]{:S(2)}, u32[]{:S(2)}) collective-permute-start(f32[4,16,512]{2,1,0:T(8,128)S(1)} %get-tuple-element.182), channel_id=1, source_target_pairs={{0,1},{1,0},{2,3},{3,2},{4,5},{5,4},{6,7},{7,6},{8,9},{9,8},{10,11... | collective-permute-start | bytes 393224 | tf_op jit(solution)/shard_map/ppermute | solution.py:315
  61.6 12.6 %collective-permute-start.25 = (f32[4,16,512]{2,1,0:T(8,128)S(1)}, f32[4,16,512]{2,1,0:T(8,128)S(1)}, u32[]{:S(2)}, u32[]{:S(2)}) collective-permute-start(f32[4,16,512]{2,1,0:T(8,128)S(1)} %get-tuple-element.184), channel_id=1, source_target_pairs={{0,7},{1,6},{2,5},{3,4},{4,3},{5,2},{6,1},{7,0},{8,15},{9,14},{10,... | collective-permute-start | bytes 393224 | tf_op jit(solution)/shard_map/ppermute | solution.py:315
  63.3 10.9 %collective-permute-start.26 = (f32[16,16,128]{2,1,0:T(8,128)S(1)}, f32[16,16,128]{2,1,0:T(8,128)S(1)}, u32[]{:S(2)}, u32[]{:S(2)}) collective-permute-start(f32[16,16,128]{2,1,0:T(8,128)S(1)} %get-tuple-element.186), channel_id=1, source_target_pairs={{0,24},{8,16},{16,8},{24,0},{1,25},{9,17},{17,9},{25,1},{2,26},{10... | collective-permute-start | bytes 393224 | tf_op jit(solution)/shard_map/ppermute | solution.py:315
  67.1 7.2 %collective-permute-start.28 = (f32[4,16,512]{2,1,0:T(8,128)S(1)}, f32[4,16,512]{2,1,0:T(8,128)S(1)}, u32[]{:S(2)}, u32[]{:S(2)}) collective-permute-start(f32[4,16,512]{2,1,0:T(8,128)S(1)} %get-tuple-element.190), channel_id=1, source_target_pairs={{0,1},{1,0},{2,3},{3,2},{4,5},{5,4},{6,7},{7,6},{8,9},{9,8},{10,11... | collective-permute-start | bytes 393224 | tf_op jit(solution)/shard_map/ppermute | solution.py:315
  67.8 9.2 %collective-permute-start.30 = (f32[4,16,512]{2,1,0:T(8,128)S(1)}, f32[4,16,512]{2,1,0:T(8,128)S(1)}, u32[]{:S(2)}, u32[]{:S(2)}) collective-permute-start(f32[4,16,512]{2,1,0:T(8,128)S(1)} %get-tuple-element.194), channel_id=1, source_target_pairs={{0,4},{1,5},{2,6},{3,7},{4,0},{5,1},{6,2},{7,3},{8,12},{9,13},{10,... | collective-permute-start | bytes 393224 | tf_op jit(solution)/shard_map/ppermute | solution.py:315
  71.3 17.5 %collective-permute-start.33 = (f32[4,16,512]{2,1,0:T(8,128)S(1)}, f32[4,16,512]{2,1,0:T(8,128)S(1)}, u32[]{:S(2)}, u32[]{:S(2)}) collective-permute-start(f32[4,16,512]{2,1,0:T(8,128)S(1)} %get-tuple-element.201), channel_id=1, source_target_pairs={{0,3},{1,2},{2,1},{3,0},{4,7},{5,6},{6,5},{7,4},{8,11},{9,10},{10,... | collective-permute-start | bytes 393224 | tf_op jit(solution)/shard_map/ppermute | solution.py:315
  74.2 15.3 %collective-permute-start.32 = (f32[4,16,512]{2,1,0:T(8,128)S(1)}, f32[4,16,512]{2,1,0:T(8,128)S(1)}, u32[]{:S(2)}, u32[]{:S(2)}) collective-permute-start(f32[4,16,512]{2,1,0:T(8,128)S(1)} %get-tuple-element.200), channel_id=1, source_target_pairs={{0,5},{1,4},{2,7},{3,6},{4,1},{5,0},{6,3},{7,2},{8,13},{9,12},{10,... | collective-permute-start | bytes 393224 | tf_op jit(solution)/shard_map/ppermute | solution.py:315
  77.0 15.1 %collective-permute-start.31 = (f32[4,16,512]{2,1,0:T(8,128)S(1)}, f32[4,16,512]{2,1,0:T(8,128)S(1)}, u32[]{:S(2)}, u32[]{:S(2)}) collective-permute-start(f32[4,16,512]{2,1,0:T(8,128)S(1)} %get-tuple-element.195), channel_id=1, source_target_pairs={{0,7},{1,6},{2,5},{3,4},{4,3},{5,2},{6,1},{7,0},{8,15},{9,14},{10,... | collective-permute-start | bytes 393224 | tf_op jit(solution)/shard_map/ppermute | solution.py:315
  78.0 15.9 %collective-permute-start.29 = (f32[4,16,512]{2,1,0:T(8,128)S(1)}, f32[4,16,512]{2,1,0:T(8,128)S(1)}, u32[]{:S(2)}, u32[]{:S(2)}) collective-permute-start(f32[4,16,512]{2,1,0:T(8,128)S(1)} %get-tuple-element.191), channel_id=1, source_target_pairs={{0,6},{1,7},{2,4},{3,5},{4,2},{5,3},{6,0},{7,1},{8,14},{9,15},{10,... | collective-permute-start | bytes 393224 | tf_op jit(solution)/shard_map/ppermute | solution.py:315
  80.1 13.8 %collective-permute-start.27 = (f32[4,16,512]{2,1,0:T(8,128)S(1)}, f32[4,16,512]{2,1,0:T(8,128)S(1)}, u32[]{:S(2)}, u32[]{:S(2)}) collective-permute-start(f32[4,16,512]{2,1,0:T(8,128)S(1)} %get-tuple-element.187), channel_id=1, source_target_pairs={{0,2},{1,3},{2,0},{3,1},{4,6},{5,7},{6,4},{7,5},{8,10},{9,11},{10,... | collective-permute-start | bytes 393224 | tf_op jit(solution)/shard_map/ppermute | solution.py:315
